TPU v7x, 32 devices: a whole 2x2x4 slice. The times are simulated.
32 devices in a mesh: chan: 8 (over y, x, core), freq: 4 (over z).
Axes of the slice: x: 2, y: 2, z: 4, core: 2. Of those that a mesh axis runs over, the one named last changes fastest.
Arguments:
- spectra: bfloat16 [2, 30, 1024, 1024], P(None, None, 'freq', 'chan'), may hold values from -6 to 6
- src_ids: int32 [2, 32], replicated, may hold values from 0 to 1023
- pair_bin: int32 [2, 32, 1024], P(None, None, 'chan'), may hold values from 0 to 255, as said below
- slot_of_bin: int32 [256], replicated, may hold values from 0 to 255, each once
Outputs:
- offset_gather: float32 [256, 256], P('chan')
Inputs may be any that keep to these rules, and one draw needn't show every extreme that they name: slot_of_bin names every row of offset_gather once. `pair_bin`: some offset bins are named by no pair.
All inputs are finite; a program needn't handle non-finite values.
Results may differ from a plain program's by a relative error of at most 0.0003.
Values may be sent and summed in bfloat16 or wider, within the bound.
No kernel may reach another device: no remote copies, remote signals or barrier semaphores. Data moves between devices by JAX's collectives and lax.ppermute only.
A program may use at most 64 MiB of HBM per device.

v0:
```python
import functools
import math

import jax
import jax.numpy as jnp
from jax import lax
from jax.experimental import pallas as pl
from jax.experimental.pallas import tpu as pltpu
from jax.sharding import PartitionSpec as P

F = 1024
NLAG = 256
BF = jnp.bfloat16
F32 = jnp.float32
I32 = jnp.int32
FB = 16
WROWS = 16
LANES = 128
LIMIT = 60 * 1024 * 1024
PITCH = LANES + 9
PARAMS = pltpu.CompilerParams(vmem_limit_bytes=LIMIT)
ANY = pl.BlockSpec(memory_space=pl.ANY)
VMEM = pl.BlockSpec(memory_space=pltpu.VMEM)


def lag_basis(anchor, amount, totals, lag_count, windows):
    frequency = anchor + lax.iota(I32, amount)
    shifts = lax.iota(I32, lag_count) - lag_count // 2
    phases = frequency[:, None] * shifts[None, :] % (2 * totals)
    angles = phases.astype(F32) * (math.pi / totals)
    factor = 1.0 / math.sqrt(windows * totals)
    return jnp.cos(angles) * factor, -jnp.sin(angles) * factor


def iota(shape, dim):
    return lax.broadcasted_iota(I32, shape, dim)


def shift(values, size):
    return lax.shift_right_logical(values, jnp.int32(size.bit_length() - 1))


def as_column(row):
    size = row.shape[1]
    eye = iota((size, size), 0) == iota((size, size), 1)
    return jnp.sum(jnp.where(eye, row, 0), axis=1, keepdims=True)


def source_row(src_ref):
    return jnp.concatenate([src_ref[t : t + 1, :] for t in range(src_ref.shape[0])], axis=1)


def chip_ranks(row, per_chip):
    size = row.shape[1]
    own_row = shift(row, per_chip)
    col = as_column(row)
    own_col = shift(col, per_chip)
    same = own_col == own_row
    q0, q1 = iota((size, size), 0), iota((size, size), 1)
    rank_col = jnp.sum(jnp.where(same & (q1 < q0), 1, 0), axis=1, keepdims=True)
    rank_row = jnp.sum(jnp.where(same & (q0 < q1), 1, 0), axis=0, keepdims=True)
    return col, own_col, rank_col, own_row, rank_row


def frequency_first(rows):
    shape = (FB * WROWS, rows * FB)
    r, c = iota(shape, 0), iota(shape, 1)
    hit = (shift(r, WROWS) == (c & (FB - 1))) & ((r & (WROWS - 1)) == shift(c, FB))
    return jnp.where(hit, 1.0, 0.0).astype(BF)


def pick_kernel(cap, pieces, src_ref, spec_ref, keep_ref, send_ref, spec_send_ref, buf, keep_buf, send_buf, in_sem, out_sem):
    _, windows, freqs, chans = spec_ref.shape
    wp = windows // 2
    half = freqs // 2
    part = half // pieces
    me = lax.axis_index("chan")
    core = me & 1
    chunks = 5 if wp % 5 == 0 else 1
    wc = wp // chunks
    ins = []
    for j in range(chunks):
        for k in range(2):
            for w2 in range(2):
                at = pl.ds(w2 * wp + j * wc, wc)
                ins.append(pltpu.make_async_copy(spec_ref.at[k, at], buf.at[k, at], in_sem.at[j, 2 * k + w2]))
    for copy in ins:
        copy.start()

    row = source_row(src_ref)
    col, own_col, rank_col, _, _ = chip_ranks(row, 2 * chans)
    slots = row.shape[1]
    lane_r = iota((slots, LANES), 1) & (cap - 1)
    match = (own_col == shift(me, 2)) & (rank_col == lane_r)
    local = col - me * chans
    found = jnp.sum(jnp.where(match, local + 1, 0), axis=0, keepdims=True) - 1
    groups = LANES // cap
    shape = (groups * chans, LANES)
    r, c = iota(shape, 0), iota(shape, 1)
    hit = (shift(r, chans) == shift(c, cap)) & ((r & (chans - 1)) == found)
    picker = jnp.where(hit, 1.0, 0.0).astype(BF)

    mine = pl.multiple_of(core * half, half)
    other = pl.multiple_of((1 - core) * half, half)
    outs = []
    for j in range(chunks):
        for copy in ins[4 * j : 4 * j + 4]:
            copy.wait()
        for k in range(2):
            for w2 in range(2):
                at = pl.ds(w2 * wp + j * wc, wc)
                outs.append(
                    pltpu.make_async_copy(buf.at[k, at, pl.ds(other, half)], spec_send_ref.at[k, at], out_sem.at[j, 2 * k + w2])
                )
                outs[-1].start()
        for i in range(wc):
            w = j * wc + i
            for start, dest in ((other, send_buf), (mine, keep_buf)):
                at = pl.ds(start, half)
                if groups == 4:
                    turns = [[(w, 0), (w, 1), (wp + w, 0), (wp + w, 1)]]
                    places = [w]
                else:
                    turns = [[(w, 0), (w, 1)], [(wp + w, 0), (wp + w, 1)]]
                    places = [w, wp + w]
                for turn, place in zip(turns, places):
                    left = jnp.concatenate([buf[k, ww, at, :] for ww, k in turn], axis=1)
                    got = jnp.dot(left, picker, preferred_element_type=F32).astype(BF)
                    for p in range(pieces):
                        dest[p, place] = got[p * part : (p + 1) * part]
    last = [
        pltpu.make_async_copy(send_buf, send_ref, out_sem.at[chunks, 0]),
        pltpu.make_async_copy(keep_buf, keep_ref, out_sem.at[chunks, 1]),
    ]
    for copy in last:
        copy.start()
    for copy in outs + last:
        copy.wait()


def pick(spectra, src_ids, cap, pieces):
    _, windows, freqs, chans = spectra.shape
    half = freqs // 2
    rows = windows * cap * 2 // LANES
    chunks = 5 if (windows // 2) % 5 == 0 else 1
    shape = (pieces, rows, half // pieces, LANES)
    out = jax.ShapeDtypeStruct(shape, BF)
    return pl.pallas_call(
        functools.partial(pick_kernel, cap, pieces),
        in_specs=[VMEM, ANY],
        out_specs=[ANY, ANY, ANY],
        out_shape=[out, out, jax.ShapeDtypeStruct((2, windows, half, chans), BF)],
        scratch_shapes=[
            pltpu.VMEM(spectra.shape, BF),
            pltpu.VMEM(shape, BF),
            pltpu.VMEM(shape, BF),
            pltpu.SemaphoreType.DMA((chunks, 4)),
            pltpu.SemaphoreType.DMA((chunks + 1, 4)),
        ],
        compiler_params=PARAMS,
        name="pick_sources",
    )(src_ids, spectra)


def prep_kernel(own_ref, got_ref, out_ref, own, got, res, in_sem, out_sem):
    _, windows, half, chans = got.shape
    wp = windows // 2
    core = lax.axis_index("chan") & 1
    mine = pl.ds(pl.multiple_of(core * half, half), half)
    ins = []
    for k in range(2):
        ins.append(pltpu.make_async_copy(own_ref.at[k, :, mine], own.at[k], in_sem.at[k, 0]))
        ins.append(pltpu.make_async_copy(got_ref.at[k], got.at[k], in_sem.at[k, 1]))
    for copy in ins:
        copy.start()
    turn = frequency_first(wp)
    for copy in ins:
        copy.wait()
    outs = []
    for b in range(half // FB):
        at = pl.ds(b * FB, FB)
        for k in range(2):
            for w2 in range(2):
                ws = pl.ds(w2 * wp, wp)
                both = jnp.concatenate([own[k, ws, at, :], got[k, ws, at, :]], axis=2).reshape(wp * FB, 2 * chans)
                moved = jnp.dot(turn, both, preferred_element_type=F32).astype(BF)
                res[at, pl.ds((2 * k + w2) * WROWS, WROWS), :] = moved.reshape(FB, WROWS, 2 * chans)
        outs.append(pltpu.make_async_copy(res.at[at], out_ref.at[at], out_sem.at[b]))
        outs[-1].start()
    for copy in outs:
        copy.wait()


def prep(spectra, got):
    _, windows, freqs, chans = spectra.shape
    half = freqs // 2
    shape = (half, 4 * WROWS, 2 * chans)
    return pl.pallas_call(
        prep_kernel,
        in_specs=[ANY, ANY],
        out_specs=ANY,
        out_shape=jax.ShapeDtypeStruct(shape, BF),
        scratch_shapes=[
            pltpu.VMEM(got.shape, BF),
            pltpu.VMEM(got.shape, BF),
            pltpu.VMEM(shape, BF),
            pltpu.SemaphoreType.DMA((2, 2)),
            pltpu.SemaphoreType.DMA((half // FB,)),
        ],
        compiler_params=PARAMS,
        name="frequency_major",
    )(spectra, got)


def onehot_kernel(nchan, own_ref, got_ref, slot_ref, out_ref, count_ref, pairs, row_bin):
    chans = own_ref.shape[1]
    bins = slot_ref.shape[1]
    per = bins // nchan
    group = out_ref.shape[0]
    step = pl.program_id(0)

    @pl.when(step == 0)
    def _():
        pairs[:, pl.ds(0, chans)] = own_ref[...]
        pairs[:, pl.ds(chans, chans)] = got_ref[...]
        slot_col = as_column(slot_ref[...])
        r = iota((1, bins), 1)
        block, rest = shift(r, per), r & (per - 1)
        core, chip = shift(block, nchan // 2), block & (nchan // 2 - 1)
        order = (chip * 2 + core) * per + rest
        row_bin[...] = jnp.sum(jnp.where(slot_col == order, iota((bins, 1), 0), 0), axis=0, keepdims=True)
        count_ref[...] = jnp.zeros_like(count_ref)

    named = row_bin[...]
    total = jnp.zeros(count_ref.shape, F32)
    block = jnp.transpose(pairs[pl.ds(pl.multiple_of(step * group, group), group), :])
    for s in range(group):
        hit = jnp.where(block[:, s : s + 1] == named, 1.0, 0.0)
        out_ref[s] = hit.astype(BF)
        total = total + jnp.sum(hit[:chans], axis=0, keepdims=True)
    count_ref[...] += total


def onehot(own, got, slot_of_bin, nchan):
    slots, chans = own.shape
    bins = slot_of_bin.shape[0]
    group = 8
    return pl.pallas_call(
        functools.partial(onehot_kernel, nchan),
        grid=(slots // group,),
        in_specs=[
            pl.BlockSpec((slots, chans), lambda i: (0, 0)),
            pl.BlockSpec((slots, chans), lambda i: (0, 0)),
            pl.BlockSpec((1, bins), lambda i: (0, 0)),
        ],
        out_specs=[
            pl.BlockSpec((group, 2 * chans, bins), lambda i: (i, 0, 0)),
            pl.BlockSpec((1, bins), lambda i: (0, 0)),
        ],
        out_shape=[
            jax.ShapeDtypeStruct((slots, 2 * chans, bins), BF),
            jax.ShapeDtypeStruct((1, bins), F32),
        ],
        scratch_shapes=[pltpu.VMEM((slots, 2 * chans), I32), pltpu.VMEM((1, bins), I32)],
        compiler_params=PARAMS,
        name="bin_onehot",
    )(own, got, slot_of_bin[None, :])


def cross_kernel(cap, chips, routes, first_f, final, *refs):
    pieces = len(routes)
    src_ref, recv_ref, hot_ref, cos_ref, sin_ref, count_ref, prior_ref = refs[:7]
    xrefs = refs[7 : 7 + pieces * chips]
    refs = refs[7 + pieces * chips :]
    outs, refs = (refs[:2], refs[2:]) if final else (refs[:1], refs[1:])
    xbuf, recv, hot, xs, cross, whole, in_sem, hot_sem, recv_sem = refs
    _, _, rows, part, _ = xbuf.shape
    count, chans2 = recv.shape[0], recv.shape[2]
    slots, _, bins = hot.shape
    wp = rows * LANES // (2 * cap) // 2
    groups = LANES // cap

    xin = []
    for p in range(pieces):
        for d in range(chips):
            xin.append(pltpu.make_async_copy(xrefs[p * chips + d], xbuf.at[p, d], in_sem.at[p, d]))
    rin = pltpu.make_async_copy(recv_ref.at[pl.ds(first_f, count)], recv, recv_sem)
    hgroup = slots // hot_sem.shape[0]
    hin = [
        pltpu.make_async_copy(hot_ref.at[pl.ds(g * hgroup, hgroup)], hot.at[pl.ds(g * hgroup, hgroup)], hot_sem.at[g])
        for g in range(hot_sem.shape[0])
    ]
    for copy in xin + [rin] + hin:
        copy.start()

    me = lax.axis_index("chan")
    row = source_row(src_ref)
    _, _, _, own_row, rank_row = chip_ranks(row, chans2)
    own_row = jnp.concatenate([own_row] * groups, axis=1)
    rank_row = jnp.concatenate([rank_row] * groups, axis=1)
    shape = (LANES, groups * slots)
    r, c = iota(shape, 0), iota(shape, 1)
    aligned = (shift(r, cap) == shift(c, slots)) & ((r & (cap - 1)) == rank_row)
    turn = frequency_first(wp)
    for copy in xin:
        copy.wait()
    for p in range(pieces):
        place = jnp.concatenate(
            [jnp.where(aligned & (own_row == (shift(me, 2) ^ (routes[p][d] >> 1))), 1.0, 0.0).astype(BF) for d in range(chips)],
            axis=0,
        )
        for b in range(part // FB):
            at = pl.ds(b * FB, FB)
            sides = []
            for h in range(rows // wp):
                ws = pl.ds(h * wp, wp)
                got = jnp.concatenate([xbuf[p, d, ws, at, :] for d in range(chips)], axis=2)
                got = got.reshape(wp * FB, chips * LANES)
                sides.append(jnp.dot(got, place, preferred_element_type=F32).astype(BF))
            moved = jnp.concatenate(sides, axis=1) if len(sides) > 1 else sides[0]
            xs[pl.ds((p * part + b * FB) * WROWS, FB * WROWS), :] = jnp.dot(turn, moved, preferred_element_type=F32)

    rin.wait()
    imag = iota((2 * WROWS, LANES), 1) >= slots

    def one_group(g, carry):
        for j in range(8):
            f = g * 8 + j
            x = xs[pl.ds(pl.multiple_of(f * WROWS, WROWS), WROWS), :]
            x = jnp.concatenate([x[:, :LANES], x[:, LANES:]], axis=0)
            upper = jnp.where(imag, -x, x)
            if j:
                upper = pltpu.roll(upper, j, 1)
            left = jnp.concatenate([upper, pltpu.roll(x, slots + j, 1)], axis=0).astype(BF)
            got = lax.dot_general(left, recv[f], (((0,), (0,)), ((), ())), preferred_element_type=F32)
            base = pl.multiple_of(g * (8 * PITCH) + j * (PITCH - 1), 8)
            for h in range(2):
                side = got[:, h * LANES : (h + 1) * LANES]
                cross[h, pl.ds(base, LANES), :] = side
                if j:
                    cross[h, pl.ds(pl.multiple_of(base + LANES, 8), 8), :] = side[:8]
        return carry

    lax.fori_loop(0, count // 8, one_group, 0)

    total = jnp.zeros((2 * count, bins), F32)
    for copy in hin:
        copy.wait()

    def one_slot(s2, total):
        for s in (2 * s2, 2 * s2 + 1):
            parts = []
            for turn in range(2):
                at = pl.ds(s + turn * slots, count, stride=PITCH)
                parts.append(jnp.concatenate([cross[0, at, :], cross[1, at, :]], axis=1))
            x = jnp.concatenate(parts, axis=0)
            high = x.astype(BF)
            low = (x - high.astype(F32)).astype(BF)
            weights = hot[s]
            total = total + jnp.dot(high, weights, preferred_element_type=F32)
            total = total + jnp.dot(low, weights, preferred_element_type=F32)
        return total

    total = lax.fori_loop(0, slots // 2, one_slot, total)
    at = pl.ds(first_f, count)
    table = jnp.concatenate([cos_ref[at, :], sin_ref[at, :]], axis=0)
    lagged = lax.dot_general(total, table, (((0,), (0,)), ((), ())), precision=lax.Precision.HIGHEST, preferred_element_type=F32)
    if not final:
        outs[0][...] = lagged
        return
    if first_f:
        lagged = lagged + prior_ref[...]
    whole[...] = lagged
    core = me & 1
    blocks, padded, lags = outs[0].shape
    per = bins // (2 * blocks)
    crows = count_ref.shape[0]
    for which, dest in ((core, outs[0]), (1 - core, outs[1])):
        for d in range(blocks):
            start = pl.multiple_of((which * blocks + d) * per, per)
            dest[d, pl.ds(0, per), :] = whole[pl.ds(start, per), :]
            dest[d, pl.ds(per, crows), :] = count_ref[...]


def cross_and_bin(arrays, routes, src_ids, recv, hot, counts, cos, sin, prior, first_f, cap, nchan, final):
    pieces, chips = len(arrays), len(arrays[0])
    rows, part, _ = arrays[0][0].shape
    slots, chans2, bins = hot.shape
    lags = cos.shape[1]
    count = pieces * part
    per = bins // nchan
    if final:
        out = jax.ShapeDtypeStruct((nchan // 2, per + 8, lags), F32)
        out_shape, out_specs = [out, out], [VMEM, VMEM]
    else:
        out_shape, out_specs = [jax.ShapeDtypeStruct((bins, lags), F32)], [VMEM]
    return pl.pallas_call(
        functools.partial(cross_kernel, cap, chips, routes, first_f, final),
        in_specs=[VMEM, ANY, ANY, VMEM, VMEM, VMEM, VMEM] + [ANY] * (pieces * chips),
        out_specs=out_specs,
        out_shape=out_shape,
        scratch_shapes=[
            pltpu.VMEM((pieces, chips, rows, part, LANES), BF),
            pltpu.VMEM((count,) + recv.shape[1:], BF),
            pltpu.VMEM(hot.shape, BF),
            pltpu.VMEM((count * WROWS, 2 * LANES), F32),
            pltpu.VMEM((2, count * PITCH + 8, chans2 // 2), F32),
            pltpu.VMEM((bins, lags), F32),
            pltpu.SemaphoreType.DMA((pieces, chips)),
            pltpu.SemaphoreType.DMA((8,)),
            pltpu.SemaphoreType.DMA,
        ],
        compiler_params=PARAMS,
        name="cross_and_bin",
    )(src_ids, recv, hot, cos, sin, counts, prior, *[x for held in arrays for x in held])


def swap(x, size, bit):
    return lax.ppermute(x, "chan", [(i, i ^ bit) for i in range(size)])


def sums(nchan, nfreq, cap, spectra, src_ids, pair_bin, slot_of_bin):
    _, windows, freqs, chans = spectra.shape
    half = freqs // 2
    bins = slot_of_bin.shape[0]
    slots = src_ids.shape[0] * src_ids.shape[1]
    me = lax.axis_index("chan")
    core = me & 1
    rest = [1 << k for k in range(1, nchan.bit_length() - 1)]
    pieces = min(4, half // FB)

    keep, send, spec_send = pick(spectra, src_ids, cap, pieces)
    got = swap(send, nchan, 1)
    chip = [keep[p] + got[p] for p in range(pieces)]
    arrays, routes = [], []
    for p in range(pieces):
        held, names = [chip[p]], [0]
        for bit in rest if p % 2 == 0 else rest[::-1]:
            held = held + [swap(x, nchan, bit) for x in held]
            names = names + [name ^ bit for name in names]
        arrays.append(held)
        routes.append(names)

    pairs_own = pair_bin.reshape(slots, chans)
    got_pairs = swap(pairs_own, nchan, 1)
    got_spec = swap(spec_send, nchan, 1)
    hot, counts = onehot(pairs_own, got_pairs, slot_of_bin, nchan)
    recv = prep(spectra, got_spec)
    cos, sin = lag_basis(lax.axis_index("freq") * freqs + core * half, half, F, NLAG, windows)
    counts = counts.reshape(bins // NLAG, NLAG)
    chunk = 2
    prior = jnp.zeros((bins, NLAG), F32)
    for p in range(0, pieces, chunk):
        final = p + chunk >= pieces
        out = cross_and_bin(
            arrays[p : p + chunk], routes[p : p + chunk], src_ids, recv, hot, counts, cos, sin, prior, p * (half // pieces), cap, nchan, final
        )
        if not final:
            prior = out[0]
    mine, other = out

    per = bins // nchan
    mine = mine + swap(other, nchan, 1)
    at = me // 2
    if nchan // 2 <= 4:
        total = lax.dynamic_index_in_dim(mine, at, 0, keepdims=False)
        for move in range(1, nchan // 2):
            total = total + swap(lax.dynamic_index_in_dim(mine, at ^ move, 0, keepdims=False), nchan, 2 * move)
    else:
        for bit in rest[::-1]:
            size = mine.shape[0] // 2
            up = (me & bit) != 0
            low, high = mine[:size], mine[size:]
            mine = jnp.where(up, high, low) + swap(jnp.where(up, low, high), nchan, bit)
        total = mine[0]
    owned = total[:per]
    parts = [owned]
    if nfreq <= 4:
        parts += [lax.ppermute(owned, "freq", [(i, i ^ k) for i in range(nfreq)]) for k in range(1, nfreq)]
    else:
        for k in range(nfreq.bit_length() - 1):
            owned = parts[0]
            parts = [owned + lax.ppermute(owned, "freq", [(i, i ^ (1 << k)) for i in range(nfreq)])]
    counted = total[per : per + bins // NLAG].reshape(bins)
    count = lax.dynamic_slice(counted, ((core * (nchan // 2) + at) * per,), (per,))
    return parts, count


def scaled(parts, count):
    total = parts[0]
    for part in parts[1:]:
        total = total + part
    return total / jnp.sqrt(jnp.maximum(count, 1.0))[:, None]


def body(nchan, nfreq, spectra, src_ids, pair_bin, slot_of_bin):
    args = (spectra, src_ids, pair_bin, slot_of_bin)
    slots = src_ids.shape[0] * src_ids.shape[1]
    cap = slots // 2
    owner = src_ids.reshape(-1) // (2 * spectra.shape[3])
    loads = jnp.sum((owner[None, :] == lax.iota(I32, nchan // 2)[:, None]).astype(I32), axis=1)
    fits = jnp.max(loads) <= cap
    parts, count = sums(nchan, nfreq, cap, *args)
    return lax.cond(
        fits,
        lambda parts, count, *args: scaled(parts, count),
        lambda parts, count, *args: scaled(*sums(nchan, nfreq, slots, *args)),
        parts,
        count,
        *args,
    )


def solution(mesh):
    return jax.shard_map(
        functools.partial(body, mesh.shape["chan"], mesh.shape["freq"]),
        mesh=mesh,
        in_specs=(P(None, None, "freq", "chan"), P(), P(None, None, "chan"), P()),
        out_specs=P("chan", None),
        check_vma=False,
    )
```

profile of v0, /device:TPU:0, one launch (start us, length us, event | category | flops | bytes accessed | tf_op | source)
XLA Modules:
  0.0 102.4 jit_solution(9109179978752199006)
XLA Ops:
  0.0 5.1 %pick_sources.3 = (bf16[4,15,32,128]{3,2,1,0:T(8,128)(2,1)}, bf16[4,15,32,128]{3,2,1,0:T(8,128)(2,1)}, bf16[2,30,128,128]{3,2,1,0:T(8,128)(2,1)}) custom-call(s32[2,32]{1,0:T(2,128)} %refs_0_.3, bf16[2,30,256,128]{3,2,1,0:T(8,128)(2,1)} %own_ref.1), custom_call_target="tpu_custom_call" | custom-call | tf_op jit(solution)/shard_map/pick_sources/pallas_call | solution.py:148
  5.1 0.5 collective-permute-start.22
  5.6 0.1 collective-permute-start.24
  5.7 4.4 %collective-permute-done.24 = bf16[4,15,32,128]{3,2,1,0:T(8,128)(2,1)S(1)} collective-permute-done((bf16[4,15,32,128]{3,2,1,0:T(8,128)(2,1)}, bf16[4,15,32,128]{3,2,1,0:T(8,128)(2,1)S(1)}, u32[]{:S(2)}, u32[]{:S(2)}) %collective-permute-start.24) | collective-permute-done | bytes 491552 | tf_op jit(solution)/shard_map/ppermute | solution.py:419
  10.1 1.1 %fusion.15 = (bf16[15,32,128]{2,1,0:T(8,128)(2,1)S(1)}, bf16[15,32,128]{2,1,0:T(8,128)(2,1)S(1)}, bf16[15,32,128]{2,1,0:T(8,128)(2,1)S(1)}, bf16[15,32,128]{2,1,0:T(8,128)(2,1)S(1)}) fusion(bf16[4,15,32,128]{3,2,1,0:T(8,128)(2,1)S(1)} %collective-permute-done.24, bf16[4,15,32,128]{3,2,1,0:T(8,128)(2,1)} %get-tuple-element.74), kind=kLoop, calls=%fused_computation.44 | loop fusion | flops 245760 | bytes 1474560 | tf_op jit(solution)/shard_map/add | solution.py:434
  11.3 2.9 %collective-permute-start.25 = (bf16[15,32,128]{2,1,0:T(8,128)(2,1)S(1)}, bf16[15,32,128]{2,1,0:T(8,128)(2,1)S(1)}, u32[]{:S(2)}, u32[]{:S(2)}) collective-permute-start(bf16[15,32,128]{2,1,0:T(8,128)(2,1)S(1)} %get-tuple-element.91.refs_7_), channel_id=1, source_target_pairs={{0,8},{4,12},{8,0},{12,4},{16,24},{20,28},{24,16},{28,20},{1,9},{5... | collective-permute-start | bytes 368648 | tf_op jit(solution)/shard_map/ppermute | solution.py:419
  14.2 1.5 %collective-permute-start.28 = (bf16[15,32,128]{2,1,0:T(8,128)(2,1)S(1)}, bf16[15,32,128]{2,1,0:T(8,128)(2,1)S(1)}, u32[]{:S(2)}, u32[]{:S(2)}) collective-permute-start(bf16[15,32,128]{2,1,0:T(8,128)(2,1)S(1)} %get-tuple-element.90.refs_11_), channel_id=1, source_target_pairs={{0,16},{4,20},{8,24},{12,28},{16,0},{20,4},{24,8},{28,12},{1,17},{... | collective-permute-start | bytes 368648 | tf_op jit(solution)/shard_map/ppermute | solution.py:419
  15.7 0.5 collective-permute-start.26
  16.3 0.0 collective-permute-start.23
  16.3 1.2 %collective-permute-done.23.got_ref = s32[64,128]{1,0:T(8,128)S(1)} collective-permute-done((s32[64,128]{1,0:T(8,128)S(1)}, s32[64,128]{1,0:T(8,128)S(1)}, u32[]{:S(2)}, u32[]{:S(2)}) %collective-permute-start.23) | collective-permute-done | bytes 32800 | tf_op jit(solution)/shard_map/ppermute | solution.py:419
  17.5 0.1 collective-permute-start.29
  17.5 0.3 collective-permute-done.25.refs_8_
  17.9 1.7 %collective-permute-start.31 = (bf16[15,32,128]{2,1,0:T(8,128)(2,1)S(1)}, bf16[15,32,128]{2,1,0:T(8,128)(2,1)S(1)}, u32[]{:S(2)}, u32[]{:S(2)}) collective-permute-start(bf16[15,32,128]{2,1,0:T(8,128)(2,1)S(1)} %get-tuple-element.89.refs_7_), channel_id=1, source_target_pairs={{0,8},{4,12},{8,0},{12,4},{16,24},{20,28},{24,16},{28,20},{1,9},{5... | collective-permute-start | bytes 368648 | tf_op jit(solution)/shard_map/ppermute | solution.py:419
  19.6 0.8 collective-permute-done.28.refs_12_
  20.4 1.5 %collective-permute-start.34 = (bf16[15,32,128]{2,1,0:T(8,128)(2,1)S(1)}, bf16[15,32,128]{2,1,0:T(8,128)(2,1)S(1)}, u32[]{:S(2)}, u32[]{:S(2)}) collective-permute-start(bf16[15,32,128]{2,1,0:T(8,128)(2,1)S(1)} %get-tuple-element.88.refs_11_), channel_id=1, source_target_pairs={{0,16},{4,20},{8,24},{12,28},{16,0},{20,4},{24,8},{28,12},{1,17},{... | collective-permute-start | bytes 368648 | tf_op jit(solution)/shard_map/ppermute | solution.py:419
  22.0 0.2 collective-permute-done.26.refs_9_
  22.1 1.5 %collective-permute-start.27 = (bf16[15,32,128]{2,1,0:T(8,128)(2,1)S(1)}, bf16[15,32,128]{2,1,0:T(8,128)(2,1)S(1)}, u32[]{:S(2)}, u32[]{:S(2)}) collective-permute-start(bf16[15,32,128]{2,1,0:T(8,128)(2,1)S(1)} %collective-permute-done.25.refs_8_), channel_id=1, source_target_pairs={{0,16},{4,20},{8,24},{12,28},{16,0},{20,4},{24,8},{28,12},{1,17},{... | collective-permute-start | bytes 368648 | tf_op jit(solution)/shard_map/ppermute | solution.py:419
  23.6 0.0 collective-permute-done.29.refs_13_
  23.7 1.5 %collective-permute-start.32 = (bf16[15,32,128]{2,1,0:T(8,128)(2,1)S(1)}, bf16[15,32,128]{2,1,0:T(8,128)(2,1)S(1)}, u32[]{:S(2)}, u32[]{:S(2)}) collective-permute-start(bf16[15,32,128]{2,1,0:T(8,128)(2,1)S(1)} %get-tuple-element.89.refs_7_), channel_id=1, source_target_pairs={{0,16},{4,20},{8,24},{12,28},{16,0},{20,4},{24,8},{28,12},{1,17},{... | collective-permute-start | bytes 368648 | tf_op jit(solution)/shard_map/ppermute | solution.py:419
  25.2 0.3 collective-permute-done.31.refs_8_
  25.5 0.3 collective-permute-start.35
  25.8 0.8 collective-permute-done.34.refs_12_
  26.6 1.0 collective-permute-start.30
  27.5 1.3 %collective-permute-done.27.refs_10_ = bf16[15,32,128]{2,1,0:T(8,128)(2,1)S(1)} collective-permute-done((bf16[15,32,128]{2,1,0:T(8,128)(2,1)S(1)}, bf16[15,32,128]{2,1,0:T(8,128)(2,1)S(1)}, u32[]{:S(2)}, u32[]{:S(2)}) %collective-permute-start.27) | collective-permute-done | bytes 122912 | tf_op jit(solution)/shard_map/ppermute | solution.py:419
  28.8 1.5 %collective-permute-start.33 = (bf16[15,32,128]{2,1,0:T(8,128)(2,1)S(1)}, bf16[15,32,128]{2,1,0:T(8,128)(2,1)S(1)}, u32[]{:S(2)}, u32[]{:S(2)}) collective-permute-start(bf16[15,32,128]{2,1,0:T(8,128)(2,1)S(1)} %collective-permute-done.31.refs_8_), channel_id=1, source_target_pairs={{0,16},{4,20},{8,24},{12,28},{16,0},{20,4},{24,8},{28,12},{1,17},{... | collective-permute-start | bytes 368648 | tf_op jit(solution)/shard_map/ppermute | solution.py:419
  30.3 0.0 collective-permute-done.22.got_ref
  30.3 0.5 collective-permute-start.36
  30.9 1.3 %negate_multiply_fusion.1 = (f32[128,256]{1,0:T(8,128)}, f32[128,256]{1,0:T(8,128)}) fusion(s32[256]{0:T(256)S(1)} %iota_add_fusion.2, s32[128]{0:T(128)S(1)} %iota_add_fusion.3), kind=kLoop, calls=%fused_computation.41 | loop fusion | flops 557056 | bytes 263680 | tf_op jit(solution)/shard_map/mul | solution.py:32
  32.2 7.5 %bin_onehot.3 = (bf16[64,256,256]{2,1,0:T(8,128)(2,1)}, f32[1,256]{1,0:T(1,128)}) custom-call(s32[64,128]{1,0:T(8,128)S(1)} %bitcast.49, s32[64,128]{1,0:T(8,128)} %copy-done.31, s32[1,256]{1,0:T(1,128)S(1)} %bitcast.52), custom_call_target="tpu_custom_call" | custom-call | tf_op jit(solution)/shard_map/bin_onehot/pallas_call | solution.py:248
  39.7 4.6 %frequency_major.3.refs_1_ = bf16[128,64,256]{2,1,0:T(8,128)(2,1)} custom-call(bf16[2,30,256,128]{3,2,1,0:T(8,128)(2,1)} %own_ref.1, bf16[2,30,128,128]{3,2,1,0:T(8,128)(2,1)} %copy-done), custom_call_target="tpu_custom_call" | custom-call | tf_op jit(solution)/shard_map/frequency_major/pallas_call | solution.py:198
  44.3 0.0 collective-permute-done.30.refs_14_
  44.4 0.7 broadcast_18_refs_6_.2.refs_6_
  45.1 18.6 %cross_and_bin.6.refs_6_ = f32[256,256]{1,0:T(8,128)} custom-call(s32[2,32]{1,0:T(2,128)S(1)} %copy-done.29, bf16[128,64,256]{2,1,0:T(8,128)(2,1)} %frequency_major.3.refs_1_, bf16[64,256,256]{2,1,0:T(8,128)(2,1)} %get-tuple-element.72.refs_2_, f32[128,256]{1,0:T(8,128)} %get-tuple-element.96.refs_3_, f32[128,256]{1,0:T(8,128)} %get-tuple-element.95.refs_4_, ...), custom_call_target="tpu_custom_call" | custom-call | tf_op jit(solution)/shard_map/cross_and_bin/pallas_call | solution.py:397
  63.8 0.0 collective-permute-done.32.refs_9_
  63.8 0.0 collective-permute-done.35.refs_13_
  63.8 0.0 collective-permute-done.33.refs_10_
  63.8 0.0 collective-permute-done.36.refs_14_
  63.8 0.6 copy-done.23
  64.4 0.1 copy-done.24
  64.5 0.0 copy-done.26
  64.5 0.6 copy-done.27
  65.2 16.9 %cross_and_bin.7 = (f32[4,40,256]{2,1,0:T(8,128)}, f32[4,40,256]{2,1,0:T(8,128)}) custom-call(s32[2,32]{1,0:T(2,128)S(1)} %copy-done.29, bf16[128,64,256]{2,1,0:T(8,128)(2,1)} %frequency_major.3.refs_1_, bf16[64,256,256]{2,1,0:T(8,128)(2,1)} %get-tuple-element.72.refs_2_, f32[128,256]{1,0:T(8,128)} %get-tuple-element.96.refs_3_, ...), custom_call_target="tpu_custom_call" | custom-call | tf_op jit(solution)/shard_map/cross_and_bin/pallas_call | solution.py:397
  82.1 0.1 collective-permute-start.37
  82.2 0.1 reshape.79
  82.3 1.5 %collective-permute-done.37 = f32[4,40,256]{2,1,0:T(8,128)S(1)} collective-permute-done((f32[4,40,256]{2,1,0:T(8,128)}, f32[4,40,256]{2,1,0:T(8,128)S(1)}, u32[]{:S(2)}, u32[]{:S(2)}) %collective-permute-start.37) | collective-permute-done | bytes 163872 | tf_op jit(solution)/shard_map/ppermute | solution.py:419
  83.8 0.9 add.186
  84.7 1.5 %collective-permute-start.38 = (f32[40,256]{1,0:T(8,128)S(1)}, f32[40,256]{1,0:T(8,128)S(1)}, u32[]{:S(2)}, u32[]{:S(2)}) collective-permute-start(f32[40,256]{1,0:T(8,128)S(1)} %get-tuple-element.92), channel_id=1, source_target_pairs={{0,8},{4,12},{8,0},{12,4},{16,24},{20,28},{24,16},{28,20},{1,9},{5... | collective-permute-start | bytes 122888 | tf_op jit(solution)/shard_map/ppermute | solution.py:419
  86.3 0.5 collective-permute-start.39
  86.8 1.5 %collective-permute-start.40 = (f32[40,256]{1,0:T(8,128)S(1)}, f32[40,256]{1,0:T(8,128)S(1)}, u32[]{:S(2)}, u32[]{:S(2)}) collective-permute-start(f32[40,256]{1,0:T(8,128)S(1)} %get-tuple-element.93), channel_id=1, source_target_pairs={{0,24},{4,28},{8,16},{12,20},{16,8},{20,12},{24,0},{28,4},{1,25},{... | collective-permute-start | bytes 122888 | tf_op jit(solution)/shard_map/ppermute | solution.py:419
  88.3 0.5 collective-permute-done.38
  88.8 1.9 %collective-permute-done.39 = f32[40,256]{1,0:T(8,128)S(1)} collective-permute-done((f32[40,256]{1,0:T(8,128)S(1)}, f32[40,256]{1,0:T(8,128)S(1)}, u32[]{:S(2)}, u32[]{:S(2)}) %collective-permute-start.39) | collective-permute-done | bytes 40992 | tf_op jit(solution)/shard_map/ppermute | solution.py:419
  90.7 1.0 collective-permute-done.40
  91.7 1.6 %collective-permute-start.41 = (f32[32,256]{1,0:T(8,128)S(1)}, f32[32,256]{1,0:T(8,128)S(1)}, u32[]{:S(2)}, u32[]{:S(2)}) collective-permute-start(f32[32,256]{1,0:T(8,128)S(1)} %slice.80), channel_id=1, source_target_pairs={{0,1},{1,0},{2,3},{3,2},{4,5},{5,4},{6,7},{7,6},{8,9},{9,8},{10,11... | collective-permute-start | bytes 98312 | tf_op jit(solution)/shard_map/ppermute | solution.py:479
  93.4 2.6 %collective-permute-start.42 = (f32[32,256]{1,0:T(8,128)S(1)}, f32[32,256]{1,0:T(8,128)S(1)}, u32[]{:S(2)}, u32[]{:S(2)}) collective-permute-start(f32[32,256]{1,0:T(8,128)S(1)} %slice.80), channel_id=1, source_target_pairs={{0,2},{1,3},{2,0},{3,1},{4,6},{5,7},{6,4},{7,5},{8,10},{9,11},{10,... | collective-permute-start | bytes 98312 | tf_op jit(solution)/shard_map/ppermute | solution.py:479
  95.9 0.2 collective-permute-start.43
  96.2 0.1 convert_reduce_fusion
  96.3 0.6 reduce_max.9
  97.6 0.0 collective-permute-done.41
  97.6 1.2 %collective-permute-done.42 = f32[32,256]{1,0:T(8,128)S(1)} collective-permute-done((f32[32,256]{1,0:T(8,128)S(1)}, f32[32,256]{1,0:T(8,128)S(1)}, u32[]{:S(2)}, u32[]{:S(2)}) %collective-permute-start.42) | collective-permute-done | bytes 32800 | tf_op jit(solution)/shard_map/ppermute | solution.py:479
  98.8 2.9 %collective-permute-done.43 = f32[32,256]{1,0:T(8,128)S(1)} collective-permute-done((f32[32,256]{1,0:T(8,128)S(1)}, f32[32,256]{1,0:T(8,128)S(1)}, u32[]{:S(2)}, u32[]{:S(2)}) %collective-permute-start.43) | collective-permute-done | bytes 32800 | tf_op jit(solution)/shard_map/ppermute | solution.py:479
  101.7 0.2 conditional.1
  101.7 0.1 sqrt_bitcast_fusion
  101.7 0.1 add_divide_fusion.1
  101.8 0.6 copy-done.30
  (46 shorter events, 0.1 us)
Async XLA Ops:
  0.0 16.3 %copy-start.16 = (s32[2,32,128]{2,1,0:T(8,128)S(1)}, s32[2,32,128]{2,1,0:T(8,128)}, u32[]{:S(2)}) copy-start(s32[2,32,128]{2,1,0:T(8,128)} %param.8) | copy-start | bytes 98308
  0.0 32.2 %copy-start.33 = (s32[256]{0:T(256)S(1)}, s32[256]{0:T(256)}, u32[]{:S(2)}) copy-start(s32[256]{0:T(256)} %param.9) | copy-start | bytes 3076
  5.1 25.2 %collective-permute-start.22 = (bf16[2,30,128,128]{3,2,1,0:T(8,128)(2,1)}, bf16[2,30,128,128]{3,2,1,0:T(8,128)(2,1)S(1)}, u32[]{:S(2)}, u32[]{:S(2)}) collective-permute-start(bf16[2,30,128,128]{3,2,1,0:T(8,128)(2,1)} %get-tuple-element.71), channel_id=1, source_target_pairs={{0,4},{4,0},{8,12},{12,8},{16,20},{20,16},{24,28},{28,24},{1,5},{5... | collective-permute-start | bytes 5898248 | tf_op jit(solution)/shard_map/ppermute | solution.py:419
  5.6 4.5 %collective-permute-start.24 = (bf16[4,15,32,128]{3,2,1,0:T(8,128)(2,1)}, bf16[4,15,32,128]{3,2,1,0:T(8,128)(2,1)S(1)}, u32[]{:S(2)}, u32[]{:S(2)}) collective-permute-start(bf16[4,15,32,128]{3,2,1,0:T(8,128)(2,1)} %get-tuple-element.75), channel_id=1, source_target_pairs={{0,4},{4,0},{8,12},{12,8},{16,20},{20,16},{24,28},{28,24},{1,5},{5... | collective-permute-start | bytes 1474568 | tf_op jit(solution)/shard_map/ppermute | solution.py:419
  11.3 33.1 %copy-start.6 = (bf16[15,32,128]{2,1,0:T(8,128)(2,1)}, bf16[15,32,128]{2,1,0:T(8,128)(2,1)S(1)}, u32[]{:S(2)}) copy-start(bf16[15,32,128]{2,1,0:T(8,128)(2,1)S(1)} %get-tuple-element.88.refs_11_) | copy-start | bytes 368644
  11.3 33.1 %copy-start.7 = (bf16[15,32,128]{2,1,0:T(8,128)(2,1)}, bf16[15,32,128]{2,1,0:T(8,128)(2,1)S(1)}, u32[]{:S(2)}) copy-start(bf16[15,32,128]{2,1,0:T(8,128)(2,1)S(1)} %get-tuple-element.89.refs_7_) | copy-start | bytes 368644
  11.3 33.8 %copy-start.8 = (bf16[15,32,128]{2,1,0:T(8,128)(2,1)}, bf16[15,32,128]{2,1,0:T(8,128)(2,1)S(1)}, u32[]{:S(2)}) copy-start(bf16[15,32,128]{2,1,0:T(8,128)(2,1)S(1)} %get-tuple-element.90.refs_11_) | copy-start | bytes 368644
  11.3 33.8 %copy-start.9 = (bf16[15,32,128]{2,1,0:T(8,128)(2,1)}, bf16[15,32,128]{2,1,0:T(8,128)(2,1)S(1)}, u32[]{:S(2)}) copy-start(bf16[15,32,128]{2,1,0:T(8,128)(2,1)S(1)} %get-tuple-element.91.refs_7_) | copy-start | bytes 368644
  11.3 6.5 %collective-permute-start.25 = (bf16[15,32,128]{2,1,0:T(8,128)(2,1)S(1)}, bf16[15,32,128]{2,1,0:T(8,128)(2,1)S(1)}, u32[]{:S(2)}, u32[]{:S(2)}) collective-permute-start(bf16[15,32,128]{2,1,0:T(8,128)(2,1)S(1)} %get-tuple-element.91.refs_7_), channel_id=1, source_target_pairs={{0,8},{4,12},{8,0},{12,4},{16,24},{20,28},{24,16},{28,20},{1,9},{5... | collective-permute-start | bytes 368648 | tf_op jit(solution)/shard_map/ppermute | solution.py:419
  14.2 6.2 %collective-permute-start.28 = (bf16[15,32,128]{2,1,0:T(8,128)(2,1)S(1)}, bf16[15,32,128]{2,1,0:T(8,128)(2,1)S(1)}, u32[]{:S(2)}, u32[]{:S(2)}) collective-permute-start(bf16[15,32,128]{2,1,0:T(8,128)(2,1)S(1)} %get-tuple-element.90.refs_11_), channel_id=1, source_target_pairs={{0,16},{4,20},{8,24},{12,28},{16,0},{20,4},{24,8},{28,12},{1,17},{... | collective-permute-start | bytes 368648 | tf_op jit(solution)/shard_map/ppermute | solution.py:419
  15.7 6.4 %collective-permute-start.26 = (bf16[15,32,128]{2,1,0:T(8,128)(2,1)S(1)}, bf16[15,32,128]{2,1,0:T(8,128)(2,1)S(1)}, u32[]{:S(2)}, u32[]{:S(2)}) collective-permute-start(bf16[15,32,128]{2,1,0:T(8,128)(2,1)S(1)} %get-tuple-element.91.refs_7_), channel_id=1, source_target_pairs={{0,16},{4,20},{8,24},{12,28},{16,0},{20,4},{24,8},{28,12},{1,17},{... | collective-permute-start | bytes 368648 | tf_op jit(solution)/shard_map/ppermute | solution.py:419
  16.3 1.2 %collective-permute-start.23 = (s32[64,128]{1,0:T(8,128)S(1)}, s32[64,128]{1,0:T(8,128)S(1)}, u32[]{:S(2)}, u32[]{:S(2)}) collective-permute-start(s32[64,128]{1,0:T(8,128)S(1)} %bitcast.48), channel_id=1, source_target_pairs={{0,4},{4,0},{8,12},{12,8},{16,20},{20,16},{24,28},{28,24},{1,5},{5... | collective-permute-start | bytes 98312 | tf_op jit(solution)/shard_map/ppermute | solution.py:419
  17.5 14.7 %copy-start.31 = (s32[64,128]{1,0:T(8,128)}, s32[64,128]{1,0:T(8,128)S(1)}, u32[]{:S(2)}) copy-start(s32[64,128]{1,0:T(8,128)S(1)} %collective-permute-done.23.got_ref) | copy-start | bytes 98308
  17.5 6.2 %collective-permute-start.29 = (bf16[15,32,128]{2,1,0:T(8,128)(2,1)S(1)}, bf16[15,32,128]{2,1,0:T(8,128)(2,1)S(1)}, u32[]{:S(2)}, u32[]{:S(2)}) collective-permute-start(bf16[15,32,128]{2,1,0:T(8,128)(2,1)S(1)} %get-tuple-element.90.refs_11_), channel_id=1, source_target_pairs={{0,8},{4,12},{8,0},{12,4},{16,24},{20,28},{24,16},{28,20},{1,9},{5... | collective-permute-start | bytes 368648 | tf_op jit(solution)/shard_map/ppermute | solution.py:419
  17.9 27.2 %copy-start.17 = (bf16[15,32,128]{2,1,0:T(8,128)(2,1)}, bf16[15,32,128]{2,1,0:T(8,128)(2,1)S(1)}, u32[]{:S(2)}) copy-start(bf16[15,32,128]{2,1,0:T(8,128)(2,1)S(1)} %collective-permute-done.25.refs_8_) | copy-start | bytes 368644
  17.9 7.6 %collective-permute-start.31 = (bf16[15,32,128]{2,1,0:T(8,128)(2,1)S(1)}, bf16[15,32,128]{2,1,0:T(8,128)(2,1)S(1)}, u32[]{:S(2)}, u32[]{:S(2)}) collective-permute-start(bf16[15,32,128]{2,1,0:T(8,128)(2,1)S(1)} %get-tuple-element.89.refs_7_), channel_id=1, source_target_pairs={{0,8},{4,12},{8,0},{12,4},{16,24},{20,28},{24,16},{28,20},{1,9},{5... | collective-permute-start | bytes 368648 | tf_op jit(solution)/shard_map/ppermute | solution.py:419
  20.4 24.6 %copy-start.18 = (bf16[15,32,128]{2,1,0:T(8,128)(2,1)}, bf16[15,32,128]{2,1,0:T(8,128)(2,1)S(1)}, u32[]{:S(2)}) copy-start(bf16[15,32,128]{2,1,0:T(8,128)(2,1)S(1)} %collective-permute-done.28.refs_12_) | copy-start | bytes 368644
  20.4 6.1 %collective-permute-start.34 = (bf16[15,32,128]{2,1,0:T(8,128)(2,1)S(1)}, bf16[15,32,128]{2,1,0:T(8,128)(2,1)S(1)}, u32[]{:S(2)}, u32[]{:S(2)}) collective-permute-start(bf16[15,32,128]{2,1,0:T(8,128)(2,1)S(1)} %get-tuple-element.88.refs_11_), channel_id=1, source_target_pairs={{0,16},{4,20},{8,24},{12,28},{16,0},{20,4},{24,8},{28,12},{1,17},{... | collective-permute-start | bytes 368648 | tf_op jit(solution)/shard_map/ppermute | solution.py:419
  22.1 23.0 %copy-start.19 = (bf16[15,32,128]{2,1,0:T(8,128)(2,1)}, bf16[15,32,128]{2,1,0:T(8,128)(2,1)S(1)}, u32[]{:S(2)}) copy-start(bf16[15,32,128]{2,1,0:T(8,128)(2,1)S(1)} %collective-permute-done.26.refs_9_) | copy-start | bytes 368644
  22.1 6.7 %collective-permute-start.27 = (bf16[15,32,128]{2,1,0:T(8,128)(2,1)S(1)}, bf16[15,32,128]{2,1,0:T(8,128)(2,1)S(1)}, u32[]{:S(2)}, u32[]{:S(2)}) collective-permute-start(bf16[15,32,128]{2,1,0:T(8,128)(2,1)S(1)} %collective-permute-done.25.refs_8_), channel_id=1, source_target_pairs={{0,16},{4,20},{8,24},{12,28},{16,0},{20,4},{24,8},{28,12},{1,17},{... | collective-permute-start | bytes 368648 | tf_op jit(solution)/shard_map/ppermute | solution.py:419
  23.6 21.4 %copy-start.22 = (bf16[15,32,128]{2,1,0:T(8,128)(2,1)}, bf16[15,32,128]{2,1,0:T(8,128)(2,1)S(1)}, u32[]{:S(2)}) copy-start(bf16[15,32,128]{2,1,0:T(8,128)(2,1)S(1)} %collective-permute-done.29.refs_13_) | copy-start | bytes 368644
  23.7 40.1 %collective-permute-start.32 = (bf16[15,32,128]{2,1,0:T(8,128)(2,1)S(1)}, bf16[15,32,128]{2,1,0:T(8,128)(2,1)S(1)}, u32[]{:S(2)}, u32[]{:S(2)}) collective-permute-start(bf16[15,32,128]{2,1,0:T(8,128)(2,1)S(1)} %get-tuple-element.89.refs_7_), channel_id=1, source_target_pairs={{0,16},{4,20},{8,24},{12,28},{16,0},{20,4},{24,8},{28,12},{1,17},{... | collective-permute-start | bytes 368648 | tf_op jit(solution)/shard_map/ppermute | solution.py:419
  25.5 38.3 %copy-start.20 = (bf16[15,32,128]{2,1,0:T(8,128)(2,1)}, bf16[15,32,128]{2,1,0:T(8,128)(2,1)S(1)}, u32[]{:S(2)}) copy-start(bf16[15,32,128]{2,1,0:T(8,128)(2,1)S(1)} %collective-permute-done.31.refs_8_) | copy-start | bytes 368644
  25.5 38.3 %collective-permute-start.35 = (bf16[15,32,128]{2,1,0:T(8,128)(2,1)S(1)}, bf16[15,32,128]{2,1,0:T(8,128)(2,1)S(1)}, u32[]{:S(2)}, u32[]{:S(2)}) collective-permute-start(bf16[15,32,128]{2,1,0:T(8,128)(2,1)S(1)} %get-tuple-element.88.refs_11_), channel_id=1, source_target_pairs={{0,8},{4,12},{8,0},{12,4},{16,24},{20,28},{24,16},{28,20},{1,9},{5... | collective-permute-start | bytes 368648 | tf_op jit(solution)/shard_map/ppermute | solution.py:419
  26.6 37.2 %copy-start.21 = (bf16[15,32,128]{2,1,0:T(8,128)(2,1)}, bf16[15,32,128]{2,1,0:T(8,128)(2,1)S(1)}, u32[]{:S(2)}) copy-start(bf16[15,32,128]{2,1,0:T(8,128)(2,1)S(1)} %collective-permute-done.34.refs_12_) | copy-start | bytes 368644
  26.6 17.8 %collective-permute-start.30 = (bf16[15,32,128]{2,1,0:T(8,128)(2,1)S(1)}, bf16[15,32,128]{2,1,0:T(8,128)(2,1)S(1)}, u32[]{:S(2)}, u32[]{:S(2)}) collective-permute-start(bf16[15,32,128]{2,1,0:T(8,128)(2,1)S(1)} %collective-permute-done.28.refs_12_), channel_id=1, source_target_pairs={{0,8},{4,12},{8,0},{12,4},{16,24},{20,28},{24,16},{28,20},{1,9},{5... | collective-permute-start | bytes 368648 | tf_op jit(solution)/shard_map/ppermute | solution.py:419
  28.8 16.3 %copy-start.25 = (bf16[15,32,128]{2,1,0:T(8,128)(2,1)}, bf16[15,32,128]{2,1,0:T(8,128)(2,1)S(1)}, u32[]{:S(2)}) copy-start(bf16[15,32,128]{2,1,0:T(8,128)(2,1)S(1)} %collective-permute-done.27.refs_10_) | copy-start | bytes 368644
  28.8 35.0 %collective-permute-start.33 = (bf16[15,32,128]{2,1,0:T(8,128)(2,1)S(1)}, bf16[15,32,128]{2,1,0:T(8,128)(2,1)S(1)}, u32[]{:S(2)}, u32[]{:S(2)}) collective-permute-start(bf16[15,32,128]{2,1,0:T(8,128)(2,1)S(1)} %collective-permute-done.31.refs_8_), channel_id=1, source_target_pairs={{0,16},{4,20},{8,24},{12,28},{16,0},{20,4},{24,8},{28,12},{1,17},{... | collective-permute-start | bytes 368648 | tf_op jit(solution)/shard_map/ppermute | solution.py:419
  30.3 9.4 %copy-start = (bf16[2,30,128,128]{3,2,1,0:T(8,128)(2,1)}, bf16[2,30,128,128]{3,2,1,0:T(8,128)(2,1)S(1)}, u32[]{:S(2)}) copy-start(bf16[2,30,128,128]{3,2,1,0:T(8,128)(2,1)S(1)} %collective-permute-done.22.got_ref) | copy-start | bytes 5898244
  30.3 33.5 %collective-permute-start.36 = (bf16[15,32,128]{2,1,0:T(8,128)(2,1)S(1)}, bf16[15,32,128]{2,1,0:T(8,128)(2,1)S(1)}, u32[]{:S(2)}, u32[]{:S(2)}) collective-permute-start(bf16[15,32,128]{2,1,0:T(8,128)(2,1)S(1)} %collective-permute-done.34.refs_12_), channel_id=1, source_target_pairs={{0,8},{4,12},{8,0},{12,4},{16,24},{20,28},{24,16},{28,20},{1,9},{5... | collective-permute-start | bytes 368648 | tf_op jit(solution)/shard_map/ppermute | solution.py:419
  39.7 5.4 %copy-start.29 = (s32[2,32]{1,0:T(2,128)S(1)}, s32[2,32]{1,0:T(2,128)}, u32[]{:S(2)}) copy-start(s32[2,32]{1,0:T(2,128)} %refs_0_.3) | copy-start | bytes 772
  44.4 0.8 copy-start.28
  63.8 0.6 copy-start.23
  63.8 0.7 copy-start.24
  63.8 0.7 copy-start.26
  64.5 0.7 copy-start.27
  82.1 1.7 %collective-permute-start.37 = (f32[4,40,256]{2,1,0:T(8,128)}, f32[4,40,256]{2,1,0:T(8,128)S(1)}, u32[]{:S(2)}, u32[]{:S(2)}) collective-permute-start(f32[4,40,256]{2,1,0:T(8,128)} %get-tuple-element.77), channel_id=1, source_target_pairs={{0,4},{4,0},{8,12},{12,8},{16,20},{20,16},{24,28},{28,24},{1,5},{5... | collective-permute-start | bytes 491528 | tf_op jit(solution)/shard_map/ppermute | solution.py:419
  84.7 4.1 %collective-permute-start.38 = (f32[40,256]{1,0:T(8,128)S(1)}, f32[40,256]{1,0:T(8,128)S(1)}, u32[]{:S(2)}, u32[]{:S(2)}) collective-permute-start(f32[40,256]{1,0:T(8,128)S(1)} %get-tuple-element.92), channel_id=1, source_target_pairs={{0,8},{4,12},{8,0},{12,4},{16,24},{20,28},{24,16},{28,20},{1,9},{5... | collective-permute-start | bytes 122888 | tf_op jit(solution)/shard_map/ppermute | solution.py:419
  86.3 4.4 %collective-permute-start.39 = (f32[40,256]{1,0:T(8,128)S(1)}, f32[40,256]{1,0:T(8,128)S(1)}, u32[]{:S(2)}, u32[]{:S(2)}) collective-permute-start(f32[40,256]{1,0:T(8,128)S(1)} %get-tuple-element.94), channel_id=1, source_target_pairs={{0,16},{4,20},{8,24},{12,28},{16,0},{20,4},{24,8},{28,12},{1,17},{... | collective-permute-start | bytes 122888 | tf_op jit(solution)/shard_map/ppermute | solution.py:419
  86.8 4.9 %collective-permute-start.40 = (f32[40,256]{1,0:T(8,128)S(1)}, f32[40,256]{1,0:T(8,128)S(1)}, u32[]{:S(2)}, u32[]{:S(2)}) collective-permute-start(f32[40,256]{1,0:T(8,128)S(1)} %get-tuple-element.93), channel_id=1, source_target_pairs={{0,24},{4,28},{8,16},{12,20},{16,8},{20,12},{24,0},{28,4},{1,25},{... | collective-permute-start | bytes 122888 | tf_op jit(solution)/shard_map/ppermute | solution.py:419
  91.7 5.9 %collective-permute-start.41 = (f32[32,256]{1,0:T(8,128)S(1)}, f32[32,256]{1,0:T(8,128)S(1)}, u32[]{:S(2)}, u32[]{:S(2)}) collective-permute-start(f32[32,256]{1,0:T(8,128)S(1)} %slice.80), channel_id=1, source_target_pairs={{0,1},{1,0},{2,3},{3,2},{4,5},{5,4},{6,7},{7,6},{8,9},{9,8},{10,11... | collective-permute-start | bytes 98312 | tf_op jit(solution)/shard_map/ppermute | solution.py:479
  93.4 5.4 %collective-permute-start.42 = (f32[32,256]{1,0:T(8,128)S(1)}, f32[32,256]{1,0:T(8,128)S(1)}, u32[]{:S(2)}, u32[]{:S(2)}) collective-permute-start(f32[32,256]{1,0:T(8,128)S(1)} %slice.80), channel_id=1, source_target_pairs={{0,2},{1,3},{2,0},{3,1},{4,6},{5,7},{6,4},{7,5},{8,10},{9,11},{10,... | collective-permute-start | bytes 98312 | tf_op jit(solution)/shard_map/ppermute | solution.py:479
  95.9 5.7 %collective-permute-start.43 = (f32[32,256]{1,0:T(8,128)S(1)}, f32[32,256]{1,0:T(8,128)S(1)}, u32[]{:S(2)}, u32[]{:S(2)}) collective-permute-start(f32[32,256]{1,0:T(8,128)S(1)} %slice.80), channel_id=1, source_target_pairs={{0,3},{1,2},{2,1},{3,0},{4,7},{5,6},{6,5},{7,4},{8,11},{9,10},{10,... | collective-permute-start | bytes 98312 | tf_op jit(solution)/shard_map/ppermute | solution.py:479
  101.8 0.6 copy-start.30
where the time goes:
time: 103 us; the launch traced here: 102 us
  Pallas kernels  52.7 us (51%)
  starting transfers between devices  23.3 us (23%)
  waiting for transfers between devices  18.3 us (18%)
  other arithmetic  4.32 us (4%)
  local copies, waits for them, and re-layouts  2.85 us (3%)
    pallas_call x2, Pallas kernels, cross_and_bin(): pl.pallas_call(functools.partial(cross_kernel, cap, chips, routes, first_...  35.5 us
    ppermute x19, starting transfers between devices, swap(): return lax.ppermute(x, 'chan', [(i, i ^ bit) for i in range(size)])  18.8 us
    ppermute x19, waiting for transfers between devices, swap(): return lax.ppermute(x, 'chan', [(i, i ^ bit) for i in range(size)])  14.2 us
    pallas_call x1, Pallas kernels, onehot(): pl.pallas_call(functools.partial(onehot_kernel, nchan), grid=(slots // gr...  7.52 us
    pallas_call x1, Pallas kernels, pick(): pl.pallas_call(functools.partial(pick_kernel, cap, pieces), in_specs=[VME...  5.09 us
    pallas_call x1, Pallas kernels, prep(): pl.pallas_call(prep_kernel, in_specs=[ANY, ANY], out_specs=ANY, out_shape...  4.6 us
    ppermute x3, starting transfers between devices, sums(): lax.ppermute(owned, 'freq', [(i, i ^ k) for i in range(nfreq)])  4.45 us
    ppermute x3, waiting for transfers between devices, sums(): lax.ppermute(owned, 'freq', [(i, i ^ k) for i in range(nfreq)])  4.08 us
  transfers between devices with their start and end apart: 22, of which 14 were waited for; matrix products, arithmetic and copies ran while one was open for 4% of the time, Pallas kernels for 30%

commit v1 on v0

v1 whole, which is shorter than its diff:
```python
import functools
import math

import jax
import jax.numpy as jnp
from jax import lax
from jax.experimental import pallas as pl
from jax.experimental.pallas import tpu as pltpu
from jax.sharding import PartitionSpec as P

F = 1024
NLAG = 256
BF = jnp.bfloat16
F32 = jnp.float32
I32 = jnp.int32
FB = 16
WROWS = 16
LANES = 128
SLACK = 6 * 1024 * 1024
PITCH = LANES + 9
TURN = 8
GROUPS = 4
ANY = pl.BlockSpec(memory_space=pl.ANY)
VMEM = pl.BlockSpec(memory_space=pltpu.VMEM)


def lag_basis(anchor, amount, totals, lag_count, windows):
    frequency = anchor + lax.iota(I32, amount)
    shifts = lax.iota(I32, lag_count) - lag_count // 2
    phases = frequency[:, None] * shifts[None, :] % (2 * totals)
    angles = phases.astype(F32) * (math.pi / totals)
    factor = 1.0 / math.sqrt(windows * totals)
    return jnp.cos(angles) * factor, -jnp.sin(angles) * factor


def params(*buffers):
    used = sum(math.prod(shape) * jnp.dtype(kind).itemsize for shape, kind in buffers)
    return pltpu.CompilerParams(vmem_limit_bytes=used + SLACK)


def iota(shape, dim):
    return lax.broadcasted_iota(I32, shape, dim)


def shift(values, size):
    return lax.shift_right_logical(values, jnp.int32(size.bit_length() - 1))


def as_column(row):
    size = row.shape[1]
    eye = iota((size, size), 0) == iota((size, size), 1)
    return jnp.sum(jnp.where(eye, row, 0), axis=1, keepdims=True)


def source_row(src_ref):
    return jnp.concatenate([src_ref[t : t + 1, :] for t in range(src_ref.shape[0])], axis=1)


def chip_ranks(row, per_chip):
    size = row.shape[1]
    own_row = shift(row, per_chip)
    col = as_column(row)
    own_col = shift(col, per_chip)
    same = own_col == own_row
    q0, q1 = iota((size, size), 0), iota((size, size), 1)
    rank_col = jnp.sum(jnp.where(same & (q1 < q0), 1, 0), axis=1, keepdims=True)
    rank_row = jnp.sum(jnp.where(same & (q0 < q1), 1, 0), axis=0, keepdims=True)
    return col, own_col, rank_col, own_row, rank_row


def frequency_first(rows):
    shape = (FB * WROWS, rows * FB)
    r, c = iota(shape, 0), iota(shape, 1)
    hit = (shift(r, WROWS) == (c & (FB - 1))) & ((r & (WROWS - 1)) == shift(c, FB))
    return jnp.where(hit, 1.0, 0.0).astype(BF)


def pick_kernel(cap, pieces, src_ref, spec_ref, keep_ref, send_ref, buf, keep_buf, send_buf, in_sem, out_sem):
    _, windows, freqs, chans = spec_ref.shape
    wp = windows // 2
    half = freqs // 2
    part = half // pieces
    groups = LANES // cap
    me = lax.axis_index("chan")
    core = me & 1
    chunks = in_sem.shape[0]
    wc = wp // chunks
    ins = []
    for j in range(chunks):
        for k in range(2):
            for w2 in range(2):
                at = pl.ds(w2 * wp + j * wc, wc)
                ins.append(pltpu.make_async_copy(spec_ref.at[k, at], buf.at[k, at], in_sem.at[j, 2 * k + w2]))
    for copy in ins:
        copy.start()

    row = source_row(src_ref)
    col, own_col, rank_col, _, _ = chip_ranks(row, 2 * chans)
    slots = row.shape[1]
    lane_r = iota((slots, LANES), 1) & (cap - 1)
    match = (own_col == shift(me, 2)) & (rank_col == lane_r)
    local = col - me * chans
    found = jnp.sum(jnp.where(match, local + 1, 0), axis=0, keepdims=True) - 1
    shape = (groups * chans, LANES)
    r, c = iota(shape, 0), iota(shape, 1)
    hit = (shift(r, chans) == shift(c, cap)) & ((r & (chans - 1)) == found)
    picker = jnp.where(hit, 1.0, 0.0).astype(BF)

    mine = pl.multiple_of(core * half, half)
    other = pl.multiple_of((1 - core) * half, half)
    outs = []
    for j in range(chunks):
        for copy in ins[4 * j : 4 * j + 4]:
            copy.wait()
        for i in range(wc):
            w = j * wc + i
            if groups == 4:
                turns, places = [[(w, 0), (w, 1), (wp + w, 0), (wp + w, 1)]], [w]
            else:
                turns, places = [[(w, 0), (w, 1)], [(wp + w, 0), (wp + w, 1)]], [w, wp + w]
            for start, dest in ((other, send_buf), (mine, keep_buf)):
                for turn, place in zip(turns, places):
                    left = jnp.concatenate([buf[k, ww, pl.ds(start, half), :] for ww, k in turn], axis=1)
                    got = jnp.dot(left, picker, preferred_element_type=F32).astype(BF)
                    for p in range(pieces):
                        dest[p, place] = got[p * part : (p + 1) * part]
        for h in range(4 // groups if groups < 4 else 1):
            at = pl.ds(h * wp + j * wc, wc)
            for n, (dest, ref) in enumerate(((send_buf, send_ref), (keep_buf, keep_ref))):
                outs.append(pltpu.make_async_copy(dest.at[:, at], ref.at[:, at], out_sem.at[j, 2 * h + n]))
                outs[-1].start()
    for copy in outs:
        copy.wait()


def pick(spectra, src_ids, cap, pieces):
    _, windows, freqs, chans = spectra.shape
    half = freqs // 2
    rows = windows * cap * 2 // LANES
    chunks = 5 if (windows // 2) % 5 == 0 else 1
    shape = (pieces, rows, half // pieces, LANES)
    out = jax.ShapeDtypeStruct(shape, BF)
    return pl.pallas_call(
        functools.partial(pick_kernel, cap, pieces),
        in_specs=[VMEM, ANY],
        out_specs=[ANY, ANY],
        out_shape=[out, out],
        scratch_shapes=[
            pltpu.VMEM(spectra.shape, BF),
            pltpu.VMEM(shape, BF),
            pltpu.VMEM(shape, BF),
            pltpu.SemaphoreType.DMA((chunks, 4)),
            pltpu.SemaphoreType.DMA((chunks, 4)),
        ],
        compiler_params=params((spectra.shape, BF), (shape, BF), (shape, BF)),
        name="pick_sources",
    )(src_ids, spectra)


def prep_kernel(own_ref, got_ref, out_ref, own, got, in_sem):
    _, windows, half, chans = got.shape
    wp = windows // 2
    core = lax.axis_index("chan") & 1
    mine = pl.ds(pl.multiple_of(core * half, half), half)
    ins = []
    for k in range(2):
        ins.append(pltpu.make_async_copy(own_ref.at[k, :, mine], own.at[k], in_sem.at[k, 0]))
        ins.append(pltpu.make_async_copy(got_ref.at[k, :, mine], got.at[k], in_sem.at[k, 1]))
    for copy in ins:
        copy.start()
    turn = frequency_first(wp)
    for copy in ins:
        copy.wait()
    for b in range(half // FB):
        at = pl.ds(b * FB, FB)
        for k in range(2):
            for w2 in range(2):
                ws = pl.ds(w2 * wp, wp)
                both = jnp.concatenate([own[k, ws, at, :], got[k, ws, at, :]], axis=2).reshape(wp * FB, 2 * chans)
                moved = jnp.dot(turn, both, preferred_element_type=F32).astype(BF)
                out_ref[at, pl.ds((2 * k + w2) * WROWS, WROWS), :] = moved.reshape(FB, WROWS, 2 * chans)


def prep(spectra, got):
    _, windows, freqs, chans = spectra.shape
    half = freqs // 2
    shape = (half, 4 * WROWS, 2 * chans)
    side = (2, windows, half, chans)
    return pl.pallas_call(
        prep_kernel,
        in_specs=[ANY, ANY],
        out_specs=VMEM,
        out_shape=jax.ShapeDtypeStruct(shape, BF),
        scratch_shapes=[pltpu.VMEM(side, BF), pltpu.VMEM(side, BF), pltpu.SemaphoreType.DMA((2, 2))],
        compiler_params=params((side, BF), (side, BF)),
        name="frequency_major",
    )(spectra, got)


def onehot_kernel(nchan, own_ref, got_ref, slot_ref, out_ref, count_ref, pairs):
    slots, chans = own_ref.shape
    bins = slot_ref.shape[1]
    per = bins // nchan
    group = 8
    pairs[:, pl.ds(0, chans)] = own_ref[...]
    pairs[:, pl.ds(chans, chans)] = got_ref[...]
    slot_col = as_column(slot_ref[...])
    r = iota((1, bins), 1)
    block, rest = shift(r, per), r & (per - 1)
    core, chip = shift(block, nchan // 2), block & (nchan // 2 - 1)
    order = (chip * 2 + core) * per + rest
    named = jnp.sum(jnp.where(slot_col == order, iota((bins, 1), 0), 0), axis=0, keepdims=True)
    ones = jnp.ones((8, chans), BF)
    count_ref[...] = jnp.zeros_like(count_ref)

    def one_step(step, carry):
        block = jnp.transpose(pairs[pl.ds(pl.multiple_of(step * group, group), group), :])
        total = jnp.zeros((8, bins), F32)
        for s in range(group):
            hit = jnp.where(block[:, s : s + 1] == named, 1.0, 0.0).astype(BF)
            out_ref[step * group + s] = hit
            total = total + jnp.dot(ones, hit[:chans], preferred_element_type=F32)
        count_ref[...] += total
        return carry

    lax.fori_loop(0, slots // group, one_step, 0)


def onehot(own, got, slot_of_bin, nchan):
    slots, chans = own.shape
    bins = slot_of_bin.shape[0]
    shape = (slots, 2 * chans, bins)
    return pl.pallas_call(
        functools.partial(onehot_kernel, nchan),
        in_specs=[VMEM, VMEM, VMEM],
        out_specs=[VMEM, VMEM],
        out_shape=[jax.ShapeDtypeStruct(shape, BF), jax.ShapeDtypeStruct((8, bins), F32)],
        scratch_shapes=[pltpu.VMEM((slots, 2 * chans), I32)],
        compiler_params=params(((bins, bins), I32)),
        name="bin_onehot",
    )(own, got, slot_of_bin[None, :])


def cross_kernel(cap, chips, routes, *refs):
    pieces = len(routes)
    src_ref, recv, hot, cos_ref, sin_ref, count_ref = refs[:6]
    xrefs = refs[6 : 6 + pieces * chips]
    refs = refs[6 + pieces * chips :]
    outs, refs = refs[:2], refs[2:]
    xs, cross, sums, whole = refs
    rows, part, _ = xrefs[0].shape
    count, _, chans2 = recv.shape
    slots, _, bins = hot.shape
    wp = rows * LANES // (2 * cap) // 2
    groups = LANES // cap
    me = lax.axis_index("chan")
    row = source_row(src_ref)
    _, _, _, own_row, rank_row = chip_ranks(row, chans2)
    own_row = jnp.concatenate([own_row] * groups, axis=1)
    rank_row = jnp.concatenate([rank_row] * groups, axis=1)
    shape = (LANES, groups * slots)
    r, c = iota(shape, 0), iota(shape, 1)
    aligned = (shift(r, cap) == shift(c, slots)) & ((r & (cap - 1)) == rank_row)
    turn = frequency_first(wp)
    for p in range(pieces):
        place = jnp.concatenate(
            [jnp.where(aligned & (own_row == (shift(me, 2) ^ (routes[p][d] >> 1))), 1.0, 0.0).astype(BF) for d in range(chips)],
            axis=0,
        )
        for b in range(part // FB):
            at = pl.ds(b * FB, FB)
            sides = []
            for h in range(rows // wp):
                ws = pl.ds(h * wp, wp)
                got = jnp.concatenate([xrefs[p * chips + d][ws, at, :] for d in range(chips)], axis=2)
                got = got.reshape(wp * FB, chips * LANES)
                sides.append(jnp.dot(got, place, preferred_element_type=F32).astype(BF))
            moved = jnp.concatenate(sides, axis=1) if len(sides) > 1 else sides[0]
            xs[pl.ds((p * part + b * FB) * WROWS, FB * WROWS), :] = jnp.dot(turn, moved, preferred_element_type=F32)

    imag = iota((2 * WROWS, LANES), 1) >= slots
    quarter = shift(iota((1, 4 * 4 * WROWS), 1), 4 * WROWS)
    masks = [jnp.where(quarter == i, 1.0, 0.0).astype(BF) for i in range(4)]

    def one_group(step, carry):
        for sub in range(2 * min(GROUPS, count // 8)):
            g, q = step * min(GROUPS, count // 8) + sub // 2, sub % 2
            lefts = []
            for j in range(4 * q, 4 * q + 4):
                at = pl.ds(pl.multiple_of((g * 8 + j) * WROWS, WROWS), WROWS)
                x = xs[at, :]
                x = jnp.concatenate([x[:, :LANES], x[:, LANES:]], axis=0)
                upper = jnp.where(imag, -x, x)
                if j:
                    upper = pltpu.roll(upper, j, 1)
                lefts += [upper, pltpu.roll(x, slots + j, 1)]
            left = jnp.transpose(jnp.concatenate(lefts, axis=0)).astype(BF)
            left = jnp.concatenate([left * mask for mask in masks], axis=0)
            right = recv[pl.ds(g * 8 + 4 * q, 4)].reshape(4 * 4 * WROWS, chans2)
            got = jnp.dot(left, right, preferred_element_type=F32)
            for i in range(4):
                j = 4 * q + i
                base = pl.multiple_of(g * (8 * PITCH) + j * (PITCH - 1), 8)
                for h in range(2):
                    side = got[i * LANES : (i + 1) * LANES, h * LANES : (h + 1) * LANES]
                    cross[h, pl.ds(base, LANES), :] = side
                    if j:
                        cross[h, pl.ds(pl.multiple_of(base + LANES, 8), 8), :] = side[:8]
        return carry

    lax.fori_loop(0, count // (8 * min(GROUPS, count // 8)), one_group, 0)

    sums[...] = jnp.zeros_like(sums)

    def one_turn(step, carry):
        lefts = []
        for u in range(TURN):
            s = step * TURN + u
            parts = []
            for turn in range(2):
                at = pl.ds(s + turn * slots, count, stride=PITCH)
                parts.append(jnp.concatenate([cross[0, at, :], cross[1, at, :]], axis=1))
            x = jnp.concatenate(parts, axis=0)
            high = x.astype(BF)
            low = (x - high.astype(F32)).astype(BF)
            lefts.append(jnp.concatenate([high, low], axis=0))
        left = jnp.concatenate(lefts, axis=1)
        right = hot[pl.ds(step * TURN, TURN)].reshape(TURN * chans2, bins)
        sums[...] += jnp.dot(left, right, preferred_element_type=F32)
        return carry

    lax.fori_loop(0, slots // TURN, one_turn, 0)
    total = sums[pl.ds(0, 2 * count), :] + sums[pl.ds(2 * count, 2 * count), :]
    table = jnp.concatenate([cos_ref[...], sin_ref[...]], axis=0)
    whole[...] = lax.dot_general(total, table, (((0,), (0,)), ((), ())), precision=lax.Precision.HIGHEST, preferred_element_type=F32)
    core = me & 1
    blocks, padded, lags = outs[0].shape
    per = bins // (2 * blocks)
    crows = count_ref.shape[0]
    for which, dest in ((core, outs[0]), (1 - core, outs[1])):
        for d in range(blocks):
            start = pl.multiple_of((which * blocks + d) * per, per)
            dest[d, pl.ds(0, per), :] = whole[pl.ds(start, per), :]
            dest[d, pl.ds(per, crows), :] = count_ref[...]


def cross_and_bin(arrays, routes, src_ids, recv, hot, counts, cos, sin, cap, nchan):
    pieces, chips = len(arrays), len(arrays[0])
    rows, part, _ = arrays[0][0].shape
    _, chans2, bins = hot.shape
    lags = cos.shape[1]
    count = pieces * part
    per = bins // nchan
    out = jax.ShapeDtypeStruct((nchan // 2, per + 8, lags), F32)
    operands = [((pieces, chips, rows, part, LANES), BF), (recv.shape, BF), (hot.shape, BF)]
    buffers = [
        ((count * WROWS, 2 * LANES), F32),
        ((2, count * PITCH + 8, chans2 // 2), F32),
        ((4 * count, bins), F32),
        ((bins, lags), F32),
    ]
    return pl.pallas_call(
        functools.partial(cross_kernel, cap, chips, routes),
        in_specs=[VMEM] * (6 + pieces * chips),
        out_specs=[VMEM, VMEM],
        out_shape=[out, out],
        scratch_shapes=[pltpu.VMEM(shape, kind) for shape, kind in buffers],
        compiler_params=params(*buffers),
        name="cross_and_bin",
    )(src_ids, recv, hot, cos, sin, counts, *[x for held in arrays for x in held])


def swap(x, size, bit):
    return lax.ppermute(x, "chan", [(i, i ^ bit) for i in range(size)])


def sums(nchan, nfreq, cap, spectra, src_ids, pair_bin, slot_of_bin):
    _, windows, freqs, chans = spectra.shape
    half = freqs // 2
    bins = slot_of_bin.shape[0]
    slots = src_ids.shape[0] * src_ids.shape[1]
    me = lax.axis_index("chan")
    core = me & 1
    rest = [1 << k for k in range(1, nchan.bit_length() - 1)]
    pieces = 2

    pairs_own = pair_bin.reshape(slots, chans)
    got_pairs = swap(pairs_own, nchan, 1)
    keep, send = pick(spectra, src_ids, cap, pieces)
    got = swap(send, nchan, 1)
    chip = [keep[p] + got[p] for p in range(pieces)]
    orders = [rest if p % 2 == 0 else rest[::-1] for p in range(pieces)]
    arrays, routes = [[x] for x in chip], [[0] for _ in chip]
    early = [[] for _ in chip]
    for hop in range(len(rest)):
        if hop == len(rest) - 1:
            early = [[swap(chip[p], nchan, orders[p][hop])] for p in range(pieces)]
            hot, counts = onehot(pairs_own, got_pairs, slot_of_bin, nchan)
            later, early, counts = lax.optimization_barrier(([held[1:] for held in arrays], early, counts))
            arrays = [[held[0]] + rest_of for held, rest_of in zip(arrays, later)]
        for p in range(pieces):
            bit = orders[p][hop]
            arrays[p] = arrays[p] + early[p] + [swap(x, nchan, bit) for x in arrays[p][len(early[p]) :]]
            routes[p] = routes[p] + [name ^ bit for name in routes[p]]

    spectra_sent, got = lax.optimization_barrier((spectra, got))
    got_spec, counts = lax.optimization_barrier((swap(spectra_sent, nchan, 1), counts))
    recv = prep(spectra, got_spec)
    cos, sin = lag_basis(lax.axis_index("freq") * freqs + core * half, half, F, NLAG, windows)
    counts = counts[0].reshape(bins // NLAG, NLAG)
    out = cross_and_bin(arrays, routes, src_ids, recv, hot, counts, cos, sin, cap, nchan)
    mine, other = out

    per = bins // nchan
    mine = mine + swap(other, nchan, 1)
    at = me // 2
    if nchan // 2 <= 4:
        total = lax.dynamic_index_in_dim(mine, at, 0, keepdims=False)
        for move in range(1, nchan // 2):
            total = total + swap(lax.dynamic_index_in_dim(mine, at ^ move, 0, keepdims=False), nchan, 2 * move)
    else:
        for bit in rest[::-1]:
            size = mine.shape[0] // 2
            up = (me & bit) != 0
            low, high = mine[:size], mine[size:]
            mine = jnp.where(up, high, low) + swap(jnp.where(up, low, high), nchan, bit)
        total = mine[0]
    owned = total[:per]
    parts = [owned]
    if nfreq <= 4:
        parts += [lax.ppermute(owned, "freq", [(i, i ^ k) for i in range(nfreq)]) for k in range(nfreq - 1, 0, -1)]
    else:
        for k in range(nfreq.bit_length() - 1):
            owned = parts[0]
            parts = [owned + lax.ppermute(owned, "freq", [(i, i ^ (1 << k)) for i in range(nfreq)])]
    counted = total[per : per + bins // NLAG].reshape(bins)
    count = lax.dynamic_slice(counted, ((core * (nchan // 2) + at) * per,), (per,))
    return parts, count


def scaled(parts, count):
    total = parts[0]
    for part in parts[1:]:
        total = total + part
    return total / jnp.sqrt(jnp.maximum(count, 1.0))[:, None]


def body(nchan, nfreq, spectra, src_ids, pair_bin, slot_of_bin):
    args = (spectra, src_ids, pair_bin, slot_of_bin)
    slots = src_ids.shape[0] * src_ids.shape[1]
    cap = slots // 2
    owner = src_ids.reshape(-1) // (2 * spectra.shape[3])
    loads = jnp.sum((owner[None, :] == lax.iota(I32, nchan // 2)[:, None]).astype(I32), axis=1)
    fits = jnp.max(loads) <= cap
    parts, count = sums(nchan, nfreq, cap, *args)
    return lax.cond(
        fits,
        lambda parts, count, *args: scaled(parts, count),
        lambda parts, count, *args: scaled(*sums(nchan, nfreq, slots, *args)),
        parts,
        count,
        *args,
    )


def solution(mesh):
    return jax.shard_map(
        functools.partial(body, mesh.shape["chan"], mesh.shape["freq"]),
        mesh=mesh,
        in_specs=(P(None, None, "freq", "chan"), P(), P(None, None, "chan"), P()),
        out_specs=P("chan", None),
        check_vma=False,
    )
```

time: 103 us -> 60.8 us (0.59)
  Pallas kernels: 52.7 us -> 25.3 us
  starting transfers between devices: 23.3 us -> 18.4 us
  waiting for transfers between devices: 18.3 us -> 13.7 us
  other arithmetic: 4.32 us -> 1.61 us
  local copies, waits for them, and re-layouts: 2.85 us -> 0.74 us
    pallas_call x4 -> x3, Pallas kernels: 47.6 us -> 20.6 us  [the longest x1 12.2 us: cross_and_bin(): pl.pallas_call(functools.partial(cross_kernel, cap, chips, routes), in_sp...]
    ppermute x19 -> x13, starting transfers between devices: 18.8 us -> 14 us  [swap(): return lax.ppermute(x, 'chan', [(i, i ^ bit) for i in range(size)])]
    ppermute x19 -> x13, waiting for transfers between devices: 14.2 us -> 11.1 us  [swap(): return lax.ppermute(x, 'chan', [(i, i ^ bit) for i in range(size)])]
    ppermute x3, waiting for transfers between devices: 4.08 us -> 2.65 us  [sums(): lax.ppermute(owned, 'freq', [(i, i ^ k) for i in range(nfreq)])]
    unnamed x44 -> x8, local copies, waits for them, and re-layouts: 2.03 us -> 0.63 us
    add x1, other arithmetic: 1.13 us -> 0.05 us  [sums(): chip = [keep[p] + got[p] for p in range(pieces)]]
  transfers between devices with their start and end apart: 22 -> 16, of which waited for: 14 -> 9; matrix products, arithmetic and copies ran while one was open for 4% -> 2% of each run, Pallas kernels for 30% -> 14%
where the time goes in v1:
time: 60.8 us; the launch traced here: 60.6 us
  Pallas kernels  25.3 us (42%)
  starting transfers between devices  18.4 us (30%)
  waiting for transfers between devices  13.7 us (23%)
  other arithmetic  1.61 us (3%)
  between operations  0.8 us (1%)
  local copies, waits for them, and re-layouts  0.74 us (1%)
    ppermute x13, starting transfers between devices, swap(): return lax.ppermute(x, 'chan', [(i, i ^ bit) for i in range(size)])  14 us
    pallas_call x1, Pallas kernels, cross_and_bin(): pl.pallas_call(functools.partial(cross_kernel, cap, chips, routes), in_sp...  12.2 us
    ppermute x13, waiting for transfers between devices, swap(): return lax.ppermute(x, 'chan', [(i, i ^ bit) for i in range(size)])  11.1 us
    pallas_call x1, Pallas kernels, onehot(): pl.pallas_call(functools.partial(onehot_kernel, nchan), in_specs=[VMEM, V...  4.95 us
    pallas_call x1, Pallas kernels, pick(): pl.pallas_call(functools.partial(pick_kernel, cap, pieces), in_specs=[VME...  4.67 us
    ppermute x3, starting transfers between devices, sums(): lax.ppermute(owned, 'freq', [(i, i ^ k) for i in range(nfreq)])  4.45 us
    pallas_call x1, Pallas kernels, prep(): pl.pallas_call(prep_kernel, in_specs=[ANY, ANY], out_specs=VMEM, out_shap...  3.45 us
    ppermute x3, waiting for transfers between devices, sums(): lax.ppermute(owned, 'freq', [(i, i ^ k) for i in range(nfreq)])  2.65 us
  transfers between devices with their start and end apart: 16, of which 9 were waited for; matrix products, arithmetic and copies ran while one was open for 2% of the time, Pallas kernels for 14%

profile of v1, /device:TPU:0, one launch (start us, length us, event | category | flops | bytes accessed | tf_op | source)
XLA Modules:
  0.0 60.6 jit_solution(11356706304751869858)
XLA Ops:
  0.0 0.0 copy-start.3
  0.0 0.0 copy-start.8
  0.0 4.7 %pick_sources.3 = (bf16[2,15,64,128]{3,2,1,0:T(8,128)(2,1)S(1)}, bf16[2,15,64,128]{3,2,1,0:T(8,128)(2,1)S(1)}) custom-call(s32[2,32]{1,0:T(2,128)} %refs_0_.1, bf16[2,30,256,128]{3,2,1,0:T(8,128)(2,1)} %own_ref.1), custom_call_target="tpu_custom_call" | custom-call | tf_op jit(solution)/shard_map/pick_sources/pallas_call | solution.py:143
  4.7 0.5 collective-permute-start.16
  5.2 1.5 %collective-permute-done.16 = bf16[2,15,64,128]{3,2,1,0:T(8,128)(2,1)S(1)} collective-permute-done((bf16[2,15,64,128]{3,2,1,0:T(8,128)(2,1)S(1)}, bf16[2,15,64,128]{3,2,1,0:T(8,128)(2,1)S(1)}, u32[]{:S(2)}, u32[]{:S(2)}) %collective-permute-start.16) | collective-permute-done | bytes 491552 | tf_op jit(solution)/shard_map/ppermute | solution.py:374
  6.7 0.4 collective-permute-start.17
  7.1 0.1 collective-permute-start.22
  7.2 0.1 fusion.10
  7.3 2.9 %collective-permute-start.18 = (bf16[15,64,128]{2,1,0:T(8,128)(2,1)S(1)}, bf16[15,64,128]{2,1,0:T(8,128)(2,1)S(1)}, u32[]{:S(2)}, u32[]{:S(2)}) collective-permute-start(bf16[15,64,128]{2,1,0:T(8,128)(2,1)S(1)} %get-tuple-element.108.refs_6_), channel_id=1, source_target_pairs={{0,8},{4,12},{8,0},{12,4},{16,24},{20,28},{24,16},{28,20},{1,9},{5... | collective-permute-start | bytes 737288 | tf_op jit(solution)/shard_map/ppermute | solution.py:374
  10.2 1.5 %collective-permute-start.20 = (bf16[15,64,128]{2,1,0:T(8,128)(2,1)S(1)}, bf16[15,64,128]{2,1,0:T(8,128)(2,1)S(1)}, u32[]{:S(2)}, u32[]{:S(2)}) collective-permute-start(bf16[15,64,128]{2,1,0:T(8,128)(2,1)S(1)} %get-tuple-element.108.refs_6_), channel_id=1, source_target_pairs={{0,16},{4,20},{8,24},{12,28},{16,0},{20,4},{24,8},{28,12},{1,17},{... | collective-permute-start | bytes 737288 | tf_op jit(solution)/shard_map/ppermute | solution.py:374
  11.7 0.5 collective-permute-start.19
  12.2 0.0 collective-permute-done.22.got_ref
  12.2 2.3 %collective-permute-start.21 = (bf16[15,64,128]{2,1,0:T(8,128)(2,1)S(1)}, bf16[15,64,128]{2,1,0:T(8,128)(2,1)S(1)}, u32[]{:S(2)}, u32[]{:S(2)}) collective-permute-start(bf16[15,64,128]{2,1,0:T(8,128)(2,1)S(1)} %get-tuple-element.107.refs_10_), channel_id=1, source_target_pairs={{0,8},{4,12},{8,0},{12,4},{16,24},{20,28},{24,16},{28,20},{1,9},{5... | collective-permute-start | bytes 737288 | tf_op jit(solution)/shard_map/ppermute | solution.py:374
  14.5 0.0 copy-done.3
  14.5 0.0 copy-done.8
  14.5 4.9 %bin_onehot.3 = (bf16[64,256,256]{2,1,0:T(8,128)(2,1)S(1)}, f32[8,256]{1,0:T(8,128)S(1)}) custom-call(s32[64,128]{1,0:T(8,128)S(1)} %bitcast.41, s32[64,128]{1,0:T(8,128)S(1)} %collective-permute-done.22.got_ref, s32[1,256]{1,0:T(1,128)S(1)} %bitcast.44), custom_call_target="tpu_custom_call" | custom-call | tf_op jit(solution)/shard_map/bin_onehot/pallas_call | solution.py:233
  19.5 0.0 collective-permute-done.18.refs_7_
  19.5 3.7 %collective-permute-done.19.refs_11_ = bf16[15,64,128]{2,1,0:T(8,128)(2,1)S(1)} collective-permute-done((bf16[15,64,128]{2,1,0:T(8,128)(2,1)S(1)}, bf16[15,64,128]{2,1,0:T(8,128)(2,1)S(1)}, u32[]{:S(2)}, u32[]{:S(2)}) %collective-permute-start.19) | collective-permute-done | bytes 245792 | tf_op jit(solution)/shard_map/ppermute | solution.py:374
  23.2 0.0 collective-permute-done.20.refs_8_
  23.2 0.0 collective-permute-done.21.refs_12_
  23.2 1.5 %collective-permute-start.23 = (bf16[15,64,128]{2,1,0:T(8,128)(2,1)S(1)}, bf16[15,64,128]{2,1,0:T(8,128)(2,1)S(1)}, u32[]{:S(2)}, u32[]{:S(2)}) collective-permute-start(bf16[15,64,128]{2,1,0:T(8,128)(2,1)S(1)} %collective-permute-done.18.refs_7_), channel_id=1, source_target_pairs={{0,16},{4,20},{8,24},{12,28},{16,0},{20,4},{24,8},{28,12},{1,17},{... | collective-permute-start | bytes 737288 | tf_op jit(solution)/shard_map/ppermute | solution.py:374
  24.7 0.5 collective-permute-start.24
  25.2 0.6 negate_multiply_fusion.1
  25.8 0.0 copy-start.5
  25.9 0.0 collective-permute-done.17.got_ref
  25.9 3.5 %frequency_major.3.refs_1_ = bf16[128,64,256]{2,1,0:T(8,128)(2,1)S(1)} custom-call(bf16[2,30,256,128]{3,2,1,0:T(8,128)(2,1)} %own_ref.1, bf16[2,30,256,128]{3,2,1,0:T(8,128)(2,1)} %collective-permute-done.17.got_ref), custom_call_target="tpu_custom_call" | custom-call | tf_op jit(solution)/shard_map/frequency_major/pallas_call | solution.py:189
  29.3 0.7 %collective-permute-done.23.refs_9_ = bf16[15,64,128]{2,1,0:T(8,128)(2,1)S(1)} collective-permute-done((bf16[15,64,128]{2,1,0:T(8,128)(2,1)S(1)}, bf16[15,64,128]{2,1,0:T(8,128)(2,1)S(1)}, u32[]{:S(2)}, u32[]{:S(2)}) %collective-permute-start.23) | collective-permute-done | bytes 245792 | tf_op jit(solution)/shard_map/ppermute | solution.py:374
  30.0 1.2 %collective-permute-done.24.refs_13_ = bf16[15,64,128]{2,1,0:T(8,128)(2,1)S(1)} collective-permute-done((bf16[15,64,128]{2,1,0:T(8,128)(2,1)S(1)}, bf16[15,64,128]{2,1,0:T(8,128)(2,1)S(1)}, u32[]{:S(2)}, u32[]{:S(2)}) %collective-permute-start.24) | collective-permute-done | bytes 245792 | tf_op jit(solution)/shard_map/ppermute | solution.py:374
  31.3 0.0 copy-done.5
  31.3 12.2 %cross_and_bin.3 = (f32[4,40,256]{2,1,0:T(8,128)S(1)}, f32[4,40,256]{2,1,0:T(8,128)S(1)}) custom-call(s32[2,32]{1,0:T(2,128)S(1)} %copy-done.5, bf16[128,64,256]{2,1,0:T(8,128)(2,1)S(1)} %frequency_major.3.refs_1_, bf16[64,256,256]{2,1,0:T(8,128)(2,1)S(1)} %get-tuple-element.91.refs_2_, f32[128,256]{1,0:T(8,128)S(1)} %get-tuple-element.113.refs_3_, ...), custom_call_target="tpu_custom_call" | custom-call | tf_op jit(solution)/shard_map/cross_and_bin/pallas_call | solution.py:362
  43.5 0.1 collective-permute-start.25
  43.6 0.1 reshape.75
  43.7 1.3 %collective-permute-done.25 = f32[4,40,256]{2,1,0:T(8,128)S(1)} collective-permute-done((f32[4,40,256]{2,1,0:T(8,128)S(1)}, f32[4,40,256]{2,1,0:T(8,128)S(1)}, u32[]{:S(2)}, u32[]{:S(2)}) %collective-permute-start.25) | collective-permute-done | bytes 163872 | tf_op jit(solution)/shard_map/ppermute | solution.py:374
  45.0 0.8 %collective-permute-start.26 = (f32[40,256]{1,0:T(8,128)S(1)}, f32[40,256]{1,0:T(8,128)S(1)}, u32[]{:S(2)}, u32[]{:S(2)}) collective-permute-start(f32[40,256]{1,0:T(8,128)S(1)} %get-tuple-element.109), channel_id=1, source_target_pairs={{0,8},{4,12},{8,0},{12,4},{16,24},{20,28},{24,16},{28,20},{1,9},{5... | collective-permute-start | bytes 122888 | tf_op jit(solution)/shard_map/ppermute | solution.py:374
  45.8 0.5 collective-permute-start.27
  46.3 2.2 %collective-permute-start.28 = (f32[40,256]{1,0:T(8,128)S(1)}, f32[40,256]{1,0:T(8,128)S(1)}, u32[]{:S(2)}, u32[]{:S(2)}) collective-permute-start(f32[40,256]{1,0:T(8,128)S(1)} %get-tuple-element.110), channel_id=1, source_target_pairs={{0,24},{4,28},{8,16},{12,20},{16,8},{20,12},{24,0},{28,4},{1,25},{... | collective-permute-start | bytes 122888 | tf_op jit(solution)/shard_map/ppermute | solution.py:374
  48.6 0.5 collective-permute-done.26
  49.1 1.2 %collective-permute-done.27 = f32[40,256]{1,0:T(8,128)S(1)} collective-permute-done((f32[40,256]{1,0:T(8,128)S(1)}, f32[40,256]{1,0:T(8,128)S(1)}, u32[]{:S(2)}, u32[]{:S(2)}) %collective-permute-start.27) | collective-permute-done | bytes 40992 | tf_op jit(solution)/shard_map/ppermute | solution.py:374
  50.3 1.0 %collective-permute-done.28 = f32[40,256]{1,0:T(8,128)S(1)} collective-permute-done((f32[40,256]{1,0:T(8,128)S(1)}, f32[40,256]{1,0:T(8,128)S(1)}, u32[]{:S(2)}, u32[]{:S(2)}) %collective-permute-start.28) | collective-permute-done | bytes 40992 | tf_op jit(solution)/shard_map/ppermute | solution.py:374
  51.3 3.7 %collective-permute-start.29 = (f32[32,256]{1,0:T(8,128)S(1)}, f32[32,256]{1,0:T(8,128)S(1)}, u32[]{:S(2)}, u32[]{:S(2)}) collective-permute-start(f32[32,256]{1,0:T(8,128)S(1)} %slice.55), channel_id=1, source_target_pairs={{0,3},{1,2},{2,1},{3,0},{4,7},{5,6},{6,5},{7,4},{8,11},{9,10},{10,... | collective-permute-start | bytes 98312 | tf_op jit(solution)/shard_map/ppermute | solution.py:431
  55.0 0.0 collective-permute-start.30
  55.0 0.7 %collective-permute-start.31 = (f32[32,256]{1,0:T(8,128)S(1)}, f32[32,256]{1,0:T(8,128)S(1)}, u32[]{:S(2)}, u32[]{:S(2)}) collective-permute-start(f32[32,256]{1,0:T(8,128)S(1)} %slice.55), channel_id=1, source_target_pairs={{0,1},{1,0},{2,3},{3,2},{4,5},{5,4},{6,7},{7,6},{8,9},{9,8},{10,11... | collective-permute-start | bytes 98312 | tf_op jit(solution)/shard_map/ppermute | solution.py:431
  55.7 0.1 convert_reduce_fusion
  55.8 0.6 %reduce_max.9 = s32[]{:T(128)} reduce(s32[4]{0:T(128)S(1)} %convert_reduce_fusion, s32[]{:T(128)} %constant.138.clone.1), dimensions={0}, to_apply=%region_1.2 | reduce | flops 3 | bytes 24 | tf_op jit(solution)/shard_map/reduce_max | solution.py:454
  57.1 0.0 collective-permute-done.29
  57.1 2.6 %collective-permute-done.30 = f32[32,256]{1,0:T(8,128)S(1)} collective-permute-done((f32[32,256]{1,0:T(8,128)S(1)}, f32[32,256]{1,0:T(8,128)S(1)}, u32[]{:S(2)}, u32[]{:S(2)}) %collective-permute-start.30) | collective-permute-done | bytes 32800 | tf_op jit(solution)/shard_map/ppermute | solution.py:431
  59.8 0.0 collective-permute-done.31
  59.8 0.2 conditional.1
  59.8 0.1 sqrt_bitcast_fusion
  59.9 0.1 add_divide_fusion.1
  60.0 0.0 copy-start.4
  60.0 0.6 %copy-done.4 = f32[32,256]{1,0:T(8,128)} copy-done((f32[32,256]{1,0:T(8,128)}, f32[32,256]{1,0:T(8,128)S(1)}, u32[]{:S(2)}) %copy-start.4) | copy-done | bytes 32792
  (9 shorter events, 0.1 us)
Async XLA Ops:
  0.0 14.5 %copy-start.3 = (s32[2,32,128]{2,1,0:T(8,128)S(1)}, s32[2,32,128]{2,1,0:T(8,128)}, u32[]{:S(2)}) copy-start(s32[2,32,128]{2,1,0:T(8,128)} %param.8) | copy-start | bytes 98308
  0.0 14.5 %copy-start.8 = (s32[256]{0:T(256)S(1)}, s32[256]{0:T(256)}, u32[]{:S(2)}) copy-start(s32[256]{0:T(256)} %param.9) | copy-start | bytes 3076
  4.7 2.0 %collective-permute-start.16 = (bf16[2,15,64,128]{3,2,1,0:T(8,128)(2,1)S(1)}, bf16[2,15,64,128]{3,2,1,0:T(8,128)(2,1)S(1)}, u32[]{:S(2)}, u32[]{:S(2)}) collective-permute-start(bf16[2,15,64,128]{3,2,1,0:T(8,128)(2,1)S(1)} %get-tuple-element.85), channel_id=1, source_target_pairs={{0,4},{4,0},{8,12},{12,8},{16,20},{20,16},{24,28},{28,24},{1,5},{5... | collective-permute-start | bytes 1474568 | tf_op jit(solution)/shard_map/ppermute | solution.py:374
  6.7 19.2 %collective-permute-start.17 = (bf16[2,30,256,128]{3,2,1,0:T(8,128)(2,1)}, bf16[2,30,256,128]{3,2,1,0:T(8,128)(2,1)}, u32[]{:S(2)}, u32[]{:S(2)}) collective-permute-start(bf16[2,30,256,128]{3,2,1,0:T(8,128)(2,1)} %own_ref.1), channel_id=1, source_target_pairs={{0,4},{4,0},{8,12},{12,8},{16,20},{20,16},{24,28},{28,24},{1,5},{5... | collective-permute-start | bytes 11796488 | tf_op jit(solution)/shard_map/ppermute | solution.py:374
  7.1 5.1 %collective-permute-start.22 = (s32[64,128]{1,0:T(8,128)}, s32[64,128]{1,0:T(8,128)S(1)}, u32[]{:S(2)}, u32[]{:S(2)}) collective-permute-start(s32[64,128]{1,0:T(8,128)} %bitcast.40), channel_id=1, source_target_pairs={{0,4},{4,0},{8,12},{12,8},{16,20},{20,16},{24,28},{28,24},{1,5},{5... | collective-permute-start | bytes 98312 | tf_op jit(solution)/shard_map/ppermute | solution.py:374
  7.3 12.2 %collective-permute-start.18 = (bf16[15,64,128]{2,1,0:T(8,128)(2,1)S(1)}, bf16[15,64,128]{2,1,0:T(8,128)(2,1)S(1)}, u32[]{:S(2)}, u32[]{:S(2)}) collective-permute-start(bf16[15,64,128]{2,1,0:T(8,128)(2,1)S(1)} %get-tuple-element.108.refs_6_), channel_id=1, source_target_pairs={{0,8},{4,12},{8,0},{12,4},{16,24},{20,28},{24,16},{28,20},{1,9},{5... | collective-permute-start | bytes 737288 | tf_op jit(solution)/shard_map/ppermute | solution.py:374
  10.2 13.0 %collective-permute-start.20 = (bf16[15,64,128]{2,1,0:T(8,128)(2,1)S(1)}, bf16[15,64,128]{2,1,0:T(8,128)(2,1)S(1)}, u32[]{:S(2)}, u32[]{:S(2)}) collective-permute-start(bf16[15,64,128]{2,1,0:T(8,128)(2,1)S(1)} %get-tuple-element.108.refs_6_), channel_id=1, source_target_pairs={{0,16},{4,20},{8,24},{12,28},{16,0},{20,4},{24,8},{28,12},{1,17},{... | collective-permute-start | bytes 737288 | tf_op jit(solution)/shard_map/ppermute | solution.py:374
  11.7 11.5 %collective-permute-start.19 = (bf16[15,64,128]{2,1,0:T(8,128)(2,1)S(1)}, bf16[15,64,128]{2,1,0:T(8,128)(2,1)S(1)}, u32[]{:S(2)}, u32[]{:S(2)}) collective-permute-start(bf16[15,64,128]{2,1,0:T(8,128)(2,1)S(1)} %get-tuple-element.107.refs_10_), channel_id=1, source_target_pairs={{0,16},{4,20},{8,24},{12,28},{16,0},{20,4},{24,8},{28,12},{1,17},{... | collective-permute-start | bytes 737288 | tf_op jit(solution)/shard_map/ppermute | solution.py:374
  12.2 11.0 %collective-permute-start.21 = (bf16[15,64,128]{2,1,0:T(8,128)(2,1)S(1)}, bf16[15,64,128]{2,1,0:T(8,128)(2,1)S(1)}, u32[]{:S(2)}, u32[]{:S(2)}) collective-permute-start(bf16[15,64,128]{2,1,0:T(8,128)(2,1)S(1)} %get-tuple-element.107.refs_10_), channel_id=1, source_target_pairs={{0,8},{4,12},{8,0},{12,4},{16,24},{20,28},{24,16},{28,20},{1,9},{5... | collective-permute-start | bytes 737288 | tf_op jit(solution)/shard_map/ppermute | solution.py:374
  23.2 6.9 %collective-permute-start.23 = (bf16[15,64,128]{2,1,0:T(8,128)(2,1)S(1)}, bf16[15,64,128]{2,1,0:T(8,128)(2,1)S(1)}, u32[]{:S(2)}, u32[]{:S(2)}) collective-permute-start(bf16[15,64,128]{2,1,0:T(8,128)(2,1)S(1)} %collective-permute-done.18.refs_7_), channel_id=1, source_target_pairs={{0,16},{4,20},{8,24},{12,28},{16,0},{20,4},{24,8},{28,12},{1,17},{... | collective-permute-start | bytes 737288 | tf_op jit(solution)/shard_map/ppermute | solution.py:374
  24.7 6.6 %collective-permute-start.24 = (bf16[15,64,128]{2,1,0:T(8,128)(2,1)S(1)}, bf16[15,64,128]{2,1,0:T(8,128)(2,1)S(1)}, u32[]{:S(2)}, u32[]{:S(2)}) collective-permute-start(bf16[15,64,128]{2,1,0:T(8,128)(2,1)S(1)} %collective-permute-done.19.refs_11_), channel_id=1, source_target_pairs={{0,8},{4,12},{8,0},{12,4},{16,24},{20,28},{24,16},{28,20},{1,9},{5... | collective-permute-start | bytes 737288 | tf_op jit(solution)/shard_map/ppermute | solution.py:374
  25.8 5.4 %copy-start.5 = (s32[2,32]{1,0:T(2,128)S(1)}, s32[2,32]{1,0:T(2,128)}, u32[]{:S(2)}) copy-start(s32[2,32]{1,0:T(2,128)} %refs_0_.1) | copy-start | bytes 772
  43.5 1.5 %collective-permute-start.25 = (f32[4,40,256]{2,1,0:T(8,128)S(1)}, f32[4,40,256]{2,1,0:T(8,128)S(1)}, u32[]{:S(2)}, u32[]{:S(2)}) collective-permute-start(f32[4,40,256]{2,1,0:T(8,128)S(1)} %get-tuple-element.98), channel_id=1, source_target_pairs={{0,4},{4,0},{8,12},{12,8},{16,20},{20,16},{24,28},{28,24},{1,5},{5... | collective-permute-start | bytes 491528 | tf_op jit(solution)/shard_map/ppermute | solution.py:374
  45.0 4.1 %collective-permute-start.26 = (f32[40,256]{1,0:T(8,128)S(1)}, f32[40,256]{1,0:T(8,128)S(1)}, u32[]{:S(2)}, u32[]{:S(2)}) collective-permute-start(f32[40,256]{1,0:T(8,128)S(1)} %get-tuple-element.109), channel_id=1, source_target_pairs={{0,8},{4,12},{8,0},{12,4},{16,24},{20,28},{24,16},{28,20},{1,9},{5... | collective-permute-start | bytes 122888 | tf_op jit(solution)/shard_map/ppermute | solution.py:374
  45.8 4.4 %collective-permute-start.27 = (f32[40,256]{1,0:T(8,128)S(1)}, f32[40,256]{1,0:T(8,128)S(1)}, u32[]{:S(2)}, u32[]{:S(2)}) collective-permute-start(f32[40,256]{1,0:T(8,128)S(1)} %get-tuple-element.111), channel_id=1, source_target_pairs={{0,16},{4,20},{8,24},{12,28},{16,0},{20,4},{24,8},{28,12},{1,17},{... | collective-permute-start | bytes 122888 | tf_op jit(solution)/shard_map/ppermute | solution.py:374
  46.3 4.9 %collective-permute-start.28 = (f32[40,256]{1,0:T(8,128)S(1)}, f32[40,256]{1,0:T(8,128)S(1)}, u32[]{:S(2)}, u32[]{:S(2)}) collective-permute-start(f32[40,256]{1,0:T(8,128)S(1)} %get-tuple-element.110), channel_id=1, source_target_pairs={{0,24},{4,28},{8,16},{12,20},{16,8},{20,12},{24,0},{28,4},{1,25},{... | collective-permute-start | bytes 122888 | tf_op jit(solution)/shard_map/ppermute | solution.py:374
  51.3 5.9 %collective-permute-start.29 = (f32[32,256]{1,0:T(8,128)S(1)}, f32[32,256]{1,0:T(8,128)S(1)}, u32[]{:S(2)}, u32[]{:S(2)}) collective-permute-start(f32[32,256]{1,0:T(8,128)S(1)} %slice.55), channel_id=1, source_target_pairs={{0,3},{1,2},{2,1},{3,0},{4,7},{5,6},{6,5},{7,4},{8,11},{9,10},{10,... | collective-permute-start | bytes 98312 | tf_op jit(solution)/shard_map/ppermute | solution.py:431
  55.0 4.8 %collective-permute-start.30 = (f32[32,256]{1,0:T(8,128)S(1)}, f32[32,256]{1,0:T(8,128)S(1)}, u32[]{:S(2)}, u32[]{:S(2)}) collective-permute-start(f32[32,256]{1,0:T(8,128)S(1)} %slice.55), channel_id=1, source_target_pairs={{0,2},{1,3},{2,0},{3,1},{4,6},{5,7},{6,4},{7,5},{8,10},{9,11},{10,... | collective-permute-start | bytes 98312 | tf_op jit(solution)/shard_map/ppermute | solution.py:431
  55.0 4.8 %collective-permute-start.31 = (f32[32,256]{1,0:T(8,128)S(1)}, f32[32,256]{1,0:T(8,128)S(1)}, u32[]{:S(2)}, u32[]{:S(2)}) collective-permute-start(f32[32,256]{1,0:T(8,128)S(1)} %slice.55), channel_id=1, source_target_pairs={{0,1},{1,0},{2,3},{3,2},{4,5},{5,4},{6,7},{7,6},{8,9},{9,8},{10,11... | collective-permute-start | bytes 98312 | tf_op jit(solution)/shard_map/ppermute | solution.py:431
  60.0 0.6 %copy-start.4 = (f32[32,256]{1,0:T(8,128)}, f32[32,256]{1,0:T(8,128)S(1)}, u32[]{:S(2)}) copy-start(f32[32,256]{1,0:T(8,128)S(1)} %get-tuple-element.173) | copy-start | bytes 98308

commit v2 on v1

--- a/solution.py
+++ b/solution.py
@@ -18,8 +18,9 @@
 LANES = 128
 SLACK = 6 * 1024 * 1024
 PITCH = LANES + 9
-TURN = 8
-GROUPS = 4
+TURN = 16
+GROUPS = 16
+GROUP = 8
 ANY = pl.BlockSpec(memory_space=pl.ANY)
 VMEM = pl.BlockSpec(memory_space=pltpu.VMEM)
 
@@ -157,17 +158,48 @@
     )(src_ids, spectra)
 
 
-def prep_kernel(own_ref, got_ref, out_ref, own, got, in_sem):
+def tables_kernel(
+    nchan, spec_ref, got_ref, own_pairs, got_pairs, slot_ref, recv_ref, hot_ref, count_ref, own, got, named, tally, in_sem
+):
     _, windows, half, chans = got.shape
+    slots = own_pairs.shape[0]
+    bins = slot_ref.shape[1]
+    per = bins // nchan
     wp = windows // 2
     core = lax.axis_index("chan") & 1
     mine = pl.ds(pl.multiple_of(core * half, half), half)
     ins = []
     for k in range(2):
-        ins.append(pltpu.make_async_copy(own_ref.at[k, :, mine], own.at[k], in_sem.at[k, 0]))
+        ins.append(pltpu.make_async_copy(spec_ref.at[k, :, mine], own.at[k], in_sem.at[k, 0]))
         ins.append(pltpu.make_async_copy(got_ref.at[k, :, mine], got.at[k], in_sem.at[k, 1]))
     for copy in ins:
         copy.start()
+
+    r = iota((bins, 1), 0)
+    block, rest = shift(r, per), r & (per - 1)
+    side, chip = shift(block, nchan // 2), block & (nchan // 2 - 1)
+    order = (chip * 2 + side) * per + rest
+    row_bin = jnp.sum(jnp.where(slot_ref[...] == order, iota((1, bins), 1), 0), axis=1, keepdims=True)
+    named[...] = jnp.broadcast_to(row_bin, named.shape)
+    tally[...] = jnp.zeros_like(tally)
+
+    def one_step(step, carry):
+        total = tally[...]
+        for u in range(GROUP):
+            s = step * GROUP + u
+            bin_of = named[...]
+            mine_hit = jnp.where(own_pairs[pl.ds(s, 1), :] == bin_of, 1.0, 0.0)
+            hot_ref[s, :, pl.ds(0, chans)] = mine_hit.astype(BF)
+            hot_ref[s, :, pl.ds(chans, chans)] = jnp.where(got_pairs[pl.ds(s, 1), :] == bin_of, 1.0, 0.0).astype(BF)
+            total = total + mine_hit
+        tally[...] = total
+        return carry
+
+    lax.fori_loop(0, slots // GROUP, one_step, 0)
+    count_ref[...] = lax.dot_general(
+        jnp.ones((8, chans), BF), tally[...].astype(BF), (((1,), (1,)), ((), ())), preferred_element_type=F32
+    )
+
     turn = frequency_first(wp)
     for copy in ins:
         copy.wait()
@@ -178,71 +210,38 @@
                 ws = pl.ds(w2 * wp, wp)
                 both = jnp.concatenate([own[k, ws, at, :], got[k, ws, at, :]], axis=2).reshape(wp * FB, 2 * chans)
                 moved = jnp.dot(turn, both, preferred_element_type=F32).astype(BF)
-                out_ref[at, pl.ds((2 * k + w2) * WROWS, WROWS), :] = moved.reshape(FB, WROWS, 2 * chans)
-
-
-def prep(spectra, got):
+                recv_ref[at, pl.ds((2 * k + w2) * WROWS, WROWS), :] = moved.reshape(FB, WROWS, 2 * chans)
+
+
+def tables(spectra, got, own_pairs, got_pairs, slot_of_bin, nchan):
     _, windows, freqs, chans = spectra.shape
     half = freqs // 2
-    shape = (half, 4 * WROWS, 2 * chans)
-    side = (2, windows, half, chans)
+    slots = own_pairs.shape[0]
+    bins = slot_of_bin.shape[0]
+    side = ((2, windows, half, chans), BF)
+    square = ((bins, chans), I32)
     return pl.pallas_call(
-        prep_kernel,
-        in_specs=[ANY, ANY],
-        out_specs=VMEM,
-        out_shape=jax.ShapeDtypeStruct(shape, BF),
-        scratch_shapes=[pltpu.VMEM(side, BF), pltpu.VMEM(side, BF), pltpu.SemaphoreType.DMA((2, 2))],
-        compiler_params=params((side, BF), (side, BF)),
-        name="frequency_major",
-    )(spectra, got)
-
-
-def onehot_kernel(nchan, own_ref, got_ref, slot_ref, out_ref, count_ref, pairs):
-    slots, chans = own_ref.shape
-    bins = slot_ref.shape[1]
-    per = bins // nchan
-    group = 8
-    pairs[:, pl.ds(0, chans)] = own_ref[...]
-    pairs[:, pl.ds(chans, chans)] = got_ref[...]
-    slot_col = as_column(slot_ref[...])
-    r = iota((1, bins), 1)
-    block, rest = shift(r, per), r & (per - 1)
-    core, chip = shift(block, nchan // 2), block & (nchan // 2 - 1)
-    order = (chip * 2 + core) * per + rest
-    named = jnp.sum(jnp.where(slot_col == order, iota((bins, 1), 0), 0), axis=0, keepdims=True)
-    ones = jnp.ones((8, chans), BF)
-    count_ref[...] = jnp.zeros_like(count_ref)
-
-    def one_step(step, carry):
-        block = jnp.transpose(pairs[pl.ds(pl.multiple_of(step * group, group), group), :])
-        total = jnp.zeros((8, bins), F32)
-        for s in range(group):
-            hit = jnp.where(block[:, s : s + 1] == named, 1.0, 0.0).astype(BF)
-            out_ref[step * group + s] = hit
-            total = total + jnp.dot(ones, hit[:chans], preferred_element_type=F32)
-        count_ref[...] += total
-        return carry
-
-    lax.fori_loop(0, slots // group, one_step, 0)
-
-
-def onehot(own, got, slot_of_bin, nchan):
-    slots, chans = own.shape
-    bins = slot_of_bin.shape[0]
-    shape = (slots, 2 * chans, bins)
-    return pl.pallas_call(
-        functools.partial(onehot_kernel, nchan),
-        in_specs=[VMEM, VMEM, VMEM],
-        out_specs=[VMEM, VMEM],
-        out_shape=[jax.ShapeDtypeStruct(shape, BF), jax.ShapeDtypeStruct((8, bins), F32)],
-        scratch_shapes=[pltpu.VMEM((slots, 2 * chans), I32)],
-        compiler_params=params(((bins, bins), I32)),
-        name="bin_onehot",
-    )(own, got, slot_of_bin[None, :])
-
-
-def cross_kernel(cap, chips, routes, *refs):
-    pieces = len(routes)
+        functools.partial(tables_kernel, nchan),
+        in_specs=[ANY, ANY, VMEM, VMEM, VMEM],
+        out_specs=[VMEM, VMEM, VMEM],
+        out_shape=[
+            jax.ShapeDtypeStruct((half, 4 * WROWS, 2 * chans), BF),
+            jax.ShapeDtypeStruct((slots, bins, 2 * chans), BF),
+            jax.ShapeDtypeStruct((8, bins), F32),
+        ],
+        scratch_shapes=[
+            pltpu.VMEM(*side),
+            pltpu.VMEM(*side),
+            pltpu.VMEM(*square),
+            pltpu.VMEM((bins, chans), F32),
+            pltpu.SemaphoreType.DMA((2, 2)),
+        ],
+        compiler_params=params(side, side, square, square, ((bins, bins), I32)),
+        name="tables",
+    )(spectra, got, own_pairs, got_pairs, slot_of_bin[None, :])
+
+
+def cross_kernel(cap, chips, pieces, *refs):
     src_ref, recv, hot, cos_ref, sin_ref, count_ref = refs[:6]
     xrefs = refs[6 : 6 + pieces * chips]
     refs = refs[6 + pieces * chips :]
@@ -250,7 +249,7 @@
     xs, cross, sums, whole = refs
     rows, part, _ = xrefs[0].shape
     count, _, chans2 = recv.shape
-    slots, _, bins = hot.shape
+    slots, bins, _ = hot.shape
     wp = rows * LANES // (2 * cap) // 2
     groups = LANES // cap
     me = lax.axis_index("chan")
@@ -262,11 +261,10 @@
     r, c = iota(shape, 0), iota(shape, 1)
     aligned = (shift(r, cap) == shift(c, slots)) & ((r & (cap - 1)) == rank_row)
     turn = frequency_first(wp)
+    place = jnp.concatenate(
+        [jnp.where(aligned & (own_row == (shift(me, 2) ^ d)), 1.0, 0.0).astype(BF) for d in range(chips)], axis=0
+    )
     for p in range(pieces):
-        place = jnp.concatenate(
-            [jnp.where(aligned & (own_row == (shift(me, 2) ^ (routes[p][d] >> 1))), 1.0, 0.0).astype(BF) for d in range(chips)],
-            axis=0,
-        )
         for b in range(part // FB):
             at = pl.ds(b * FB, FB)
             sides = []
@@ -325,8 +323,8 @@
             low = (x - high.astype(F32)).astype(BF)
             lefts.append(jnp.concatenate([high, low], axis=0))
         left = jnp.concatenate(lefts, axis=1)
-        right = hot[pl.ds(step * TURN, TURN)].reshape(TURN * chans2, bins)
-        sums[...] += jnp.dot(left, right, preferred_element_type=F32)
+        right = jnp.concatenate([hot[step * TURN + u] for u in range(TURN)], axis=1)
+        sums[...] += lax.dot_general(left, right, (((1,), (1,)), ((), ())), preferred_element_type=F32)
         return carry
 
     lax.fori_loop(0, slots // TURN, one_turn, 0)
@@ -344,10 +342,10 @@
             dest[d, pl.ds(per, crows), :] = count_ref[...]
 
 
-def cross_and_bin(arrays, routes, src_ids, recv, hot, counts, cos, sin, cap, nchan):
+def cross_and_bin(arrays, src_ids, recv, hot, counts, cos, sin, cap, nchan):
     pieces, chips = len(arrays), len(arrays[0])
     rows, part, _ = arrays[0][0].shape
-    _, chans2, bins = hot.shape
+    _, bins, chans2 = hot.shape
     lags = cos.shape[1]
     count = pieces * part
     per = bins // nchan
@@ -360,7 +358,7 @@
         ((bins, lags), F32),
     ]
     return pl.pallas_call(
-        functools.partial(cross_kernel, cap, chips, routes),
+        functools.partial(cross_kernel, cap, chips, pieces),
         in_specs=[VMEM] * (6 + pieces * chips),
         out_specs=[VMEM, VMEM],
         out_shape=[out, out],
@@ -388,6 +386,8 @@
     got_pairs = swap(pairs_own, nchan, 1)
     keep, send = pick(spectra, src_ids, cap, pieces)
     got = swap(send, nchan, 1)
+    spectra_sent, got, got_pairs = lax.optimization_barrier((spectra, got, got_pairs))
+    got_spec = swap(spectra_sent, nchan, 1)
     chip = [keep[p] + got[p] for p in range(pieces)]
     orders = [rest if p % 2 == 0 else rest[::-1] for p in range(pieces)]
     arrays, routes = [[x] for x in chip], [[0] for _ in chip]
@@ -395,20 +395,16 @@
     for hop in range(len(rest)):
         if hop == len(rest) - 1:
             early = [[swap(chip[p], nchan, orders[p][hop])] for p in range(pieces)]
-            hot, counts = onehot(pairs_own, got_pairs, slot_of_bin, nchan)
-            later, early, counts = lax.optimization_barrier(([held[1:] for held in arrays], early, counts))
-            arrays = [[held[0]] + rest_of for held, rest_of in zip(arrays, later)]
         for p in range(pieces):
             bit = orders[p][hop]
             arrays[p] = arrays[p] + early[p] + [swap(x, nchan, bit) for x in arrays[p][len(early[p]) :]]
             routes[p] = routes[p] + [name ^ bit for name in routes[p]]
 
-    spectra_sent, got = lax.optimization_barrier((spectra, got))
-    got_spec, counts = lax.optimization_barrier((swap(spectra_sent, nchan, 1), counts))
-    recv = prep(spectra, got_spec)
+    recv, hot, counts = tables(spectra, got_spec, pairs_own, got_pairs, slot_of_bin, nchan)
     cos, sin = lag_basis(lax.axis_index("freq") * freqs + core * half, half, F, NLAG, windows)
     counts = counts[0].reshape(bins // NLAG, NLAG)
-    out = cross_and_bin(arrays, routes, src_ids, recv, hot, counts, cos, sin, cap, nchan)
+    arrays = [[held[names.index(2 * d)] for d in range(len(held))] for held, names in zip(arrays, routes)]
+    out = cross_and_bin(arrays, src_ids, recv, hot, counts, cos, sin, cap, nchan)
     mine, other = out
 
     per = bins // nchan

time: 60.8 us -> 57.1 us (0.939)
  Pallas kernels: 25.3 us -> 19 us
  waiting for transfers between devices: 13.7 us -> 17.4 us
  starting transfers between devices: 18.4 us -> 17.3 us
    pallas_call x3 -> x2, Pallas kernels: 20.6 us -> 14.3 us  [the longest x1 10.5 us: cross_and_bin(): pl.pallas_call(functools.partial(cross_kernel, cap, chips, pieces), in_sp...]
    ppermute x13, waiting for transfers between devices: 11.1 us -> 14.8 us  [swap(): return lax.ppermute(x, 'chan', [(i, i ^ bit) for i in range(size)])]
    ppermute x13, starting transfers between devices: 14 us -> 12.9 us  [swap(): return lax.ppermute(x, 'chan', [(i, i ^ bit) for i in range(size)])]
  transfers between devices with their start and end apart: 16 -> 16, of which waited for: 9 -> 8; matrix products, arithmetic and copies ran while one was open for 2% -> 3% of each run, Pallas kernels for 14% -> 7%
where the time goes in v2:
time: 57.1 us; the launch traced here: 56.9 us
  Pallas kernels  19 us (33%)
  waiting for transfers between devices  17.4 us (30%)
  starting transfers between devices  17.3 us (30%)
  other arithmetic  1.61 us (3%)
  between operations  0.82 us (1%)
  local copies, waits for them, and re-layouts  0.74 us (1%)
    ppermute x13, waiting for transfers between devices, swap(): return lax.ppermute(x, 'chan', [(i, i ^ bit) for i in range(size)])  14.8 us
    ppermute x13, starting transfers between devices, swap(): return lax.ppermute(x, 'chan', [(i, i ^ bit) for i in range(size)])  12.9 us
    pallas_call x1, Pallas kernels, cross_and_bin(): pl.pallas_call(functools.partial(cross_kernel, cap, chips, pieces), in_sp...  10.5 us
    pallas_call x1, Pallas kernels, pick(): pl.pallas_call(functools.partial(pick_kernel, cap, pieces), in_specs=[VME...  4.67 us
    ppermute x3, starting transfers between devices, sums(): lax.ppermute(owned, 'freq', [(i, i ^ k) for i in range(nfreq)])  4.45 us
    pallas_call x1, Pallas kernels, tables(): pl.pallas_call(functools.partial(tables_kernel, nchan), in_specs=[ANY, AN...  3.81 us
    ppermute x3, waiting for transfers between devices, sums(): lax.ppermute(owned, 'freq', [(i, i ^ k) for i in range(nfreq)])  2.61 us
  transfers between devices with their start and end apart: 16, of which 8 were waited for; matrix products, arithmetic and copies ran while one was open for 3% of the time, Pallas kernels for 7%

profile of v2, /device:TPU:0, one launch (start us, length us, event | category | flops | bytes accessed | tf_op | source)
XLA Modules:
  0.0 56.9 jit_solution(10894025485052772841)
XLA Ops:
  0.0 0.0 copy-start.1
  0.0 0.0 copy-start.4
  0.0 4.7 %pick_sources.3 = (bf16[2,15,64,128]{3,2,1,0:T(8,128)(2,1)S(1)}, bf16[2,15,64,128]{3,2,1,0:T(8,128)(2,1)S(1)}) custom-call(s32[2,32]{1,0:T(2,128)} %refs_0_.1, bf16[2,30,256,128]{3,2,1,0:T(8,128)(2,1)} %spec_ref.3), custom_call_target="tpu_custom_call" | custom-call | tf_op jit(solution)/shard_map/pick_sources/pallas_call | solution.py:144
  4.7 0.5 collective-permute-start.16
  5.2 0.1 collective-permute-start.17
  5.3 1.7 %collective-permute-done.17.got_pairs = s32[64,128]{1,0:T(8,128)S(1)} collective-permute-done((s32[64,128]{1,0:T(8,128)}, s32[64,128]{1,0:T(8,128)S(1)}, u32[]{:S(2)}, u32[]{:S(2)}) %collective-permute-start.17) | collective-permute-done | bytes 32800 | tf_op jit(solution)/shard_map/ppermute | solution.py:372
  6.9 0.0 collective-permute-done.16
  6.9 0.4 collective-permute-start.18
  7.3 0.1 add_bitcast_fusion.2
  7.4 0.0 copy-start.3
  7.4 2.7 %collective-permute-start.19 = (bf16[15,64,128]{2,1,0:T(8,128)(2,1)S(1)}, bf16[15,64,128]{2,1,0:T(8,128)(2,1)S(1)}, u32[]{:S(2)}, u32[]{:S(2)}) collective-permute-start(bf16[15,64,128]{2,1,0:T(8,128)(2,1)S(1)} %get-tuple-element.96.refs_6_), channel_id=1, source_target_pairs={{0,8},{4,12},{8,0},{12,4},{16,24},{20,28},{24,16},{28,20},{1,9},{5... | collective-permute-start | bytes 737288 | tf_op jit(solution)/shard_map/ppermute | solution.py:372
  10.1 1.5 %collective-permute-start.23 = (bf16[15,64,128]{2,1,0:T(8,128)(2,1)S(1)}, bf16[15,64,128]{2,1,0:T(8,128)(2,1)S(1)}, u32[]{:S(2)}, u32[]{:S(2)}) collective-permute-start(bf16[15,64,128]{2,1,0:T(8,128)(2,1)S(1)} %get-tuple-element.95.refs_10_), channel_id=1, source_target_pairs={{0,16},{4,20},{8,24},{12,28},{16,0},{20,4},{24,8},{28,12},{1,17},{... | collective-permute-start | bytes 737288 | tf_op jit(solution)/shard_map/ppermute | solution.py:372
  11.6 0.5 collective-permute-start.20
  12.1 0.1 collective-permute-start.22
  12.2 4.7 %collective-permute-done.19.refs_7_ = bf16[15,64,128]{2,1,0:T(8,128)(2,1)S(1)} collective-permute-done((bf16[15,64,128]{2,1,0:T(8,128)(2,1)S(1)}, bf16[15,64,128]{2,1,0:T(8,128)(2,1)S(1)}, u32[]{:S(2)}, u32[]{:S(2)}) %collective-permute-start.19) | collective-permute-done | bytes 245792 | tf_op jit(solution)/shard_map/ppermute | solution.py:372
  16.9 2.0 %collective-permute-start.21 = (bf16[15,64,128]{2,1,0:T(8,128)(2,1)S(1)}, bf16[15,64,128]{2,1,0:T(8,128)(2,1)S(1)}, u32[]{:S(2)}, u32[]{:S(2)}) collective-permute-start(bf16[15,64,128]{2,1,0:T(8,128)(2,1)S(1)} %collective-permute-done.19.refs_7_), channel_id=1, source_target_pairs={{0,16},{4,20},{8,24},{12,28},{16,0},{20,4},{24,8},{28,12},{1,17},{... | collective-permute-start | bytes 737288 | tf_op jit(solution)/shard_map/ppermute | solution.py:372
  18.9 0.0 collective-permute-done.23.refs_12_
  18.9 1.5 %collective-permute-start.24 = (bf16[15,64,128]{2,1,0:T(8,128)(2,1)S(1)}, bf16[15,64,128]{2,1,0:T(8,128)(2,1)S(1)}, u32[]{:S(2)}, u32[]{:S(2)}) collective-permute-start(bf16[15,64,128]{2,1,0:T(8,128)(2,1)S(1)} %collective-permute-done.23.refs_12_), channel_id=1, source_target_pairs={{0,8},{4,12},{8,0},{12,4},{16,24},{20,28},{24,16},{28,20},{1,9},{5... | collective-permute-start | bytes 737288 | tf_op jit(solution)/shard_map/ppermute | solution.py:372
  20.4 0.6 %negate_multiply_fusion.1 = (f32[128,256]{1,0:T(8,128)S(1)}, f32[128,256]{1,0:T(8,128)S(1)}) fusion(s32[256]{0:T(256)S(1)} %iota_add_fusion.2, s32[128]{0:T(128)S(1)} %iota_add_fusion.3), kind=kLoop, calls=%fused_computation.37 | loop fusion | flops 557056 | bytes 263680 | tf_op jit(solution)/shard_map/mul | solution.py:34
  21.0 0.0 collective-permute-done.18.got_ref
  21.0 0.0 copy-done.1
  21.0 0.0 copy-done.4
  21.0 3.8 %tables.3 = (bf16[128,64,256]{2,1,0:T(8,128)(2,1)S(1)}, bf16[64,256,256]{2,1,0:T(8,128)(2,1)S(1)}, f32[8,256]{1,0:T(8,128)S(1)}) custom-call(bf16[2,30,256,128]{3,2,1,0:T(8,128)(2,1)} %spec_ref.3, bf16[2,30,256,128]{3,2,1,0:T(8,128)(2,1)} %collective-permute-done.18.got_ref, s32[64,128]{1,0:T(8,128)S(1)} %bitcast.41, ...), custom_call_target="tpu_custom_call" | custom-call | tf_op jit(solution)/shard_map/tables/pallas_call | solution.py:223
  24.9 0.0 collective-permute-done.20.refs_8_
  24.9 0.0 collective-permute-done.22.refs_11_
  24.9 3.7 %collective-permute-done.21.refs_9_ = bf16[15,64,128]{2,1,0:T(8,128)(2,1)S(1)} collective-permute-done((bf16[15,64,128]{2,1,0:T(8,128)(2,1)S(1)}, bf16[15,64,128]{2,1,0:T(8,128)(2,1)S(1)}, u32[]{:S(2)}, u32[]{:S(2)}) %collective-permute-start.21) | collective-permute-done | bytes 245792 | tf_op jit(solution)/shard_map/ppermute | solution.py:372
  28.6 0.0 collective-permute-done.24.refs_13_
  28.6 0.0 copy-done.3
  28.6 10.5 %cross_and_bin.3 = (f32[4,40,256]{2,1,0:T(8,128)S(1)}, f32[4,40,256]{2,1,0:T(8,128)S(1)}) custom-call(s32[2,32]{1,0:T(2,128)S(1)} %copy-done.3, bf16[128,64,256]{2,1,0:T(8,128)(2,1)S(1)} %get-tuple-element.80.refs_1_, bf16[64,256,256]{2,1,0:T(8,128)(2,1)S(1)} %get-tuple-element.81.refs_2_, f32[128,256]{1,0:T(8,128)S(1)} %get-tuple-element.101.refs_3_, ...), custom_call_target="tpu_custom_call" | custom-call | tf_op jit(solution)/shard_map/cross_and_bin/pallas_call | solution.py:360
  39.1 0.1 collective-permute-start.25
  39.2 0.1 reshape.75
  39.3 1.3 %collective-permute-done.25 = f32[4,40,256]{2,1,0:T(8,128)S(1)} collective-permute-done((f32[4,40,256]{2,1,0:T(8,128)S(1)}, f32[4,40,256]{2,1,0:T(8,128)S(1)}, u32[]{:S(2)}, u32[]{:S(2)}) %collective-permute-start.25) | collective-permute-done | bytes 163872 | tf_op jit(solution)/shard_map/ppermute | solution.py:372
  40.6 0.4 collective-permute-start.26
  41.0 1.7 %collective-permute-start.27 = (f32[40,256]{1,0:T(8,128)S(1)}, f32[40,256]{1,0:T(8,128)S(1)}, u32[]{:S(2)}, u32[]{:S(2)}) collective-permute-start(f32[40,256]{1,0:T(8,128)S(1)} %get-tuple-element.99), channel_id=1, source_target_pairs={{0,16},{4,20},{8,24},{12,28},{16,0},{20,4},{24,8},{28,12},{1,17},{... | collective-permute-start | bytes 122888 | tf_op jit(solution)/shard_map/ppermute | solution.py:372
  42.7 1.4 %collective-permute-start.28 = (f32[40,256]{1,0:T(8,128)S(1)}, f32[40,256]{1,0:T(8,128)S(1)}, u32[]{:S(2)}, u32[]{:S(2)}) collective-permute-start(f32[40,256]{1,0:T(8,128)S(1)} %get-tuple-element.98), channel_id=1, source_target_pairs={{0,24},{4,28},{8,16},{12,20},{16,8},{20,12},{24,0},{28,4},{1,25},{... | collective-permute-start | bytes 122888 | tf_op jit(solution)/shard_map/ppermute | solution.py:372
  44.2 0.5 collective-permute-done.26
  44.7 0.4 collective-permute-done.27
  45.0 2.6 %collective-permute-done.28 = f32[40,256]{1,0:T(8,128)S(1)} collective-permute-done((f32[40,256]{1,0:T(8,128)S(1)}, f32[40,256]{1,0:T(8,128)S(1)}, u32[]{:S(2)}, u32[]{:S(2)}) %collective-permute-start.28) | collective-permute-done | bytes 40992 | tf_op jit(solution)/shard_map/ppermute | solution.py:372
  47.7 3.7 %collective-permute-start.29 = (f32[32,256]{1,0:T(8,128)S(1)}, f32[32,256]{1,0:T(8,128)S(1)}, u32[]{:S(2)}, u32[]{:S(2)}) collective-permute-start(f32[32,256]{1,0:T(8,128)S(1)} %slice.51), channel_id=1, source_target_pairs={{0,3},{1,2},{2,1},{3,0},{4,7},{5,6},{6,5},{7,4},{8,11},{9,10},{10,... | collective-permute-start | bytes 98312 | tf_op jit(solution)/shard_map/ppermute | solution.py:427
  51.3 0.0 collective-permute-start.30
  51.3 0.8 %collective-permute-start.31 = (f32[32,256]{1,0:T(8,128)S(1)}, f32[32,256]{1,0:T(8,128)S(1)}, u32[]{:S(2)}, u32[]{:S(2)}) collective-permute-start(f32[32,256]{1,0:T(8,128)S(1)} %slice.51), channel_id=1, source_target_pairs={{0,1},{1,0},{2,3},{3,2},{4,5},{5,4},{6,7},{7,6},{8,9},{9,8},{10,11... | collective-permute-start | bytes 98312 | tf_op jit(solution)/shard_map/ppermute | solution.py:427
  52.1 0.1 convert_reduce_fusion
  52.2 0.6 %reduce_max.9 = s32[]{:T(128)} reduce(s32[4]{0:T(128)S(1)} %convert_reduce_fusion, s32[]{:T(128)} %constant.138.clone.1), dimensions={0}, to_apply=%region_1.2 | reduce | flops 3 | bytes 24 | tf_op jit(solution)/shard_map/reduce_max | solution.py:450
  53.5 0.0 collective-permute-done.29
  53.5 2.6 %collective-permute-done.30 = f32[32,256]{1,0:T(8,128)S(1)} collective-permute-done((f32[32,256]{1,0:T(8,128)S(1)}, f32[32,256]{1,0:T(8,128)S(1)}, u32[]{:S(2)}, u32[]{:S(2)}) %collective-permute-start.30) | collective-permute-done | bytes 32800 | tf_op jit(solution)/shard_map/ppermute | solution.py:427
  56.1 0.0 collective-permute-done.31
  56.1 0.2 conditional.1
  56.1 0.1 sqrt_bitcast_fusion
  56.2 0.1 add_divide_fusion.1
  56.3 0.0 copy-start.2
  56.3 0.6 %copy-done.2 = f32[32,256]{1,0:T(8,128)} copy-done((f32[32,256]{1,0:T(8,128)}, f32[32,256]{1,0:T(8,128)S(1)}, u32[]{:S(2)}) %copy-start.2) | copy-done | bytes 32792
  (9 shorter events, 0.1 us)
Async XLA Ops:
  0.0 21.0 %copy-start.1 = (s32[2,32,128]{2,1,0:T(8,128)S(1)}, s32[2,32,128]{2,1,0:T(8,128)}, u32[]{:S(2)}) copy-start(s32[2,32,128]{2,1,0:T(8,128)} %param.8) | copy-start | bytes 98308
  0.0 21.0 %copy-start.4 = (s32[256]{0:T(256)S(1)}, s32[256]{0:T(256)}, u32[]{:S(2)}) copy-start(s32[256]{0:T(256)} %param.9) | copy-start | bytes 3076
  4.7 2.3 %collective-permute-start.16 = (bf16[2,15,64,128]{3,2,1,0:T(8,128)(2,1)S(1)}, bf16[2,15,64,128]{3,2,1,0:T(8,128)(2,1)S(1)}, u32[]{:S(2)}, u32[]{:S(2)}) collective-permute-start(bf16[2,15,64,128]{3,2,1,0:T(8,128)(2,1)S(1)} %get-tuple-element.77), channel_id=1, source_target_pairs={{0,4},{4,0},{8,12},{12,8},{16,20},{20,16},{24,28},{28,24},{1,5},{5... | collective-permute-start | bytes 1474568 | tf_op jit(solution)/shard_map/ppermute | solution.py:372
  5.2 1.7 %collective-permute-start.17 = (s32[64,128]{1,0:T(8,128)}, s32[64,128]{1,0:T(8,128)S(1)}, u32[]{:S(2)}, u32[]{:S(2)}) collective-permute-start(s32[64,128]{1,0:T(8,128)} %bitcast.40), channel_id=1, source_target_pairs={{0,4},{4,0},{8,12},{12,8},{16,20},{20,16},{24,28},{28,24},{1,5},{5... | collective-permute-start | bytes 98312 | tf_op jit(solution)/shard_map/ppermute | solution.py:372
  6.9 14.0 %collective-permute-start.18 = (bf16[2,30,256,128]{3,2,1,0:T(8,128)(2,1)}, bf16[2,30,256,128]{3,2,1,0:T(8,128)(2,1)}, u32[]{:S(2)}, u32[]{:S(2)}) collective-permute-start(bf16[2,30,256,128]{3,2,1,0:T(8,128)(2,1)} %spec_ref.3), channel_id=1, source_target_pairs={{0,4},{4,0},{8,12},{12,8},{16,20},{20,16},{24,28},{28,24},{1,5},{5... | collective-permute-start | bytes 11796488 | tf_op jit(solution)/shard_map/ppermute | solution.py:372
  7.4 21.2 %copy-start.3 = (s32[2,32]{1,0:T(2,128)S(1)}, s32[2,32]{1,0:T(2,128)}, u32[]{:S(2)}) copy-start(s32[2,32]{1,0:T(2,128)} %refs_0_.1) | copy-start | bytes 772
  7.4 9.5 %collective-permute-start.19 = (bf16[15,64,128]{2,1,0:T(8,128)(2,1)S(1)}, bf16[15,64,128]{2,1,0:T(8,128)(2,1)S(1)}, u32[]{:S(2)}, u32[]{:S(2)}) collective-permute-start(bf16[15,64,128]{2,1,0:T(8,128)(2,1)S(1)} %get-tuple-element.96.refs_6_), channel_id=1, source_target_pairs={{0,8},{4,12},{8,0},{12,4},{16,24},{20,28},{24,16},{28,20},{1,9},{5... | collective-permute-start | bytes 737288 | tf_op jit(solution)/shard_map/ppermute | solution.py:372
  10.1 8.8 %collective-permute-start.23 = (bf16[15,64,128]{2,1,0:T(8,128)(2,1)S(1)}, bf16[15,64,128]{2,1,0:T(8,128)(2,1)S(1)}, u32[]{:S(2)}, u32[]{:S(2)}) collective-permute-start(bf16[15,64,128]{2,1,0:T(8,128)(2,1)S(1)} %get-tuple-element.95.refs_10_), channel_id=1, source_target_pairs={{0,16},{4,20},{8,24},{12,28},{16,0},{20,4},{24,8},{28,12},{1,17},{... | collective-permute-start | bytes 737288 | tf_op jit(solution)/shard_map/ppermute | solution.py:372
  11.6 13.2 %collective-permute-start.20 = (bf16[15,64,128]{2,1,0:T(8,128)(2,1)S(1)}, bf16[15,64,128]{2,1,0:T(8,128)(2,1)S(1)}, u32[]{:S(2)}, u32[]{:S(2)}) collective-permute-start(bf16[15,64,128]{2,1,0:T(8,128)(2,1)S(1)} %get-tuple-element.96.refs_6_), channel_id=1, source_target_pairs={{0,16},{4,20},{8,24},{12,28},{16,0},{20,4},{24,8},{28,12},{1,17},{... | collective-permute-start | bytes 737288 | tf_op jit(solution)/shard_map/ppermute | solution.py:372
  12.1 12.7 %collective-permute-start.22 = (bf16[15,64,128]{2,1,0:T(8,128)(2,1)S(1)}, bf16[15,64,128]{2,1,0:T(8,128)(2,1)S(1)}, u32[]{:S(2)}, u32[]{:S(2)}) collective-permute-start(bf16[15,64,128]{2,1,0:T(8,128)(2,1)S(1)} %get-tuple-element.95.refs_10_), channel_id=1, source_target_pairs={{0,8},{4,12},{8,0},{12,4},{16,24},{20,28},{24,16},{28,20},{1,9},{5... | collective-permute-start | bytes 737288 | tf_op jit(solution)/shard_map/ppermute | solution.py:372
  16.9 11.7 %collective-permute-start.21 = (bf16[15,64,128]{2,1,0:T(8,128)(2,1)S(1)}, bf16[15,64,128]{2,1,0:T(8,128)(2,1)S(1)}, u32[]{:S(2)}, u32[]{:S(2)}) collective-permute-start(bf16[15,64,128]{2,1,0:T(8,128)(2,1)S(1)} %collective-permute-done.19.refs_7_), channel_id=1, source_target_pairs={{0,16},{4,20},{8,24},{12,28},{16,0},{20,4},{24,8},{28,12},{1,17},{... | collective-permute-start | bytes 737288 | tf_op jit(solution)/shard_map/ppermute | solution.py:372
  18.9 9.7 %collective-permute-start.24 = (bf16[15,64,128]{2,1,0:T(8,128)(2,1)S(1)}, bf16[15,64,128]{2,1,0:T(8,128)(2,1)S(1)}, u32[]{:S(2)}, u32[]{:S(2)}) collective-permute-start(bf16[15,64,128]{2,1,0:T(8,128)(2,1)S(1)} %collective-permute-done.23.refs_12_), channel_id=1, source_target_pairs={{0,8},{4,12},{8,0},{12,4},{16,24},{20,28},{24,16},{28,20},{1,9},{5... | collective-permute-start | bytes 737288 | tf_op jit(solution)/shard_map/ppermute | solution.py:372
  39.1 1.5 %collective-permute-start.25 = (f32[4,40,256]{2,1,0:T(8,128)S(1)}, f32[4,40,256]{2,1,0:T(8,128)S(1)}, u32[]{:S(2)}, u32[]{:S(2)}) collective-permute-start(f32[4,40,256]{2,1,0:T(8,128)S(1)} %get-tuple-element.86), channel_id=1, source_target_pairs={{0,4},{4,0},{8,12},{12,8},{16,20},{20,16},{24,28},{28,24},{1,5},{5... | collective-permute-start | bytes 491528 | tf_op jit(solution)/shard_map/ppermute | solution.py:372
  40.6 4.1 %collective-permute-start.26 = (f32[40,256]{1,0:T(8,128)S(1)}, f32[40,256]{1,0:T(8,128)S(1)}, u32[]{:S(2)}, u32[]{:S(2)}) collective-permute-start(f32[40,256]{1,0:T(8,128)S(1)} %get-tuple-element.97), channel_id=1, source_target_pairs={{0,8},{4,12},{8,0},{12,4},{16,24},{20,28},{24,16},{28,20},{1,9},{5... | collective-permute-start | bytes 122888 | tf_op jit(solution)/shard_map/ppermute | solution.py:372
  41.0 4.0 %collective-permute-start.27 = (f32[40,256]{1,0:T(8,128)S(1)}, f32[40,256]{1,0:T(8,128)S(1)}, u32[]{:S(2)}, u32[]{:S(2)}) collective-permute-start(f32[40,256]{1,0:T(8,128)S(1)} %get-tuple-element.99), channel_id=1, source_target_pairs={{0,16},{4,20},{8,24},{12,28},{16,0},{20,4},{24,8},{28,12},{1,17},{... | collective-permute-start | bytes 122888 | tf_op jit(solution)/shard_map/ppermute | solution.py:372
  42.7 4.9 %collective-permute-start.28 = (f32[40,256]{1,0:T(8,128)S(1)}, f32[40,256]{1,0:T(8,128)S(1)}, u32[]{:S(2)}, u32[]{:S(2)}) collective-permute-start(f32[40,256]{1,0:T(8,128)S(1)} %get-tuple-element.98), channel_id=1, source_target_pairs={{0,24},{4,28},{8,16},{12,20},{16,8},{20,12},{24,0},{28,4},{1,25},{... | collective-permute-start | bytes 122888 | tf_op jit(solution)/shard_map/ppermute | solution.py:372
  47.7 5.9 %collective-permute-start.29 = (f32[32,256]{1,0:T(8,128)S(1)}, f32[32,256]{1,0:T(8,128)S(1)}, u32[]{:S(2)}, u32[]{:S(2)}) collective-permute-start(f32[32,256]{1,0:T(8,128)S(1)} %slice.51), channel_id=1, source_target_pairs={{0,3},{1,2},{2,1},{3,0},{4,7},{5,6},{6,5},{7,4},{8,11},{9,10},{10,... | collective-permute-start | bytes 98312 | tf_op jit(solution)/shard_map/ppermute | solution.py:427
  51.3 4.8 %collective-permute-start.30 = (f32[32,256]{1,0:T(8,128)S(1)}, f32[32,256]{1,0:T(8,128)S(1)}, u32[]{:S(2)}, u32[]{:S(2)}) collective-permute-start(f32[32,256]{1,0:T(8,128)S(1)} %slice.51), channel_id=1, source_target_pairs={{0,2},{1,3},{2,0},{3,1},{4,6},{5,7},{6,4},{7,5},{8,10},{9,11},{10,... | collective-permute-start | bytes 98312 | tf_op jit(solution)/shard_map/ppermute | solution.py:427
  51.3 4.8 %collective-permute-start.31 = (f32[32,256]{1,0:T(8,128)S(1)}, f32[32,256]{1,0:T(8,128)S(1)}, u32[]{:S(2)}, u32[]{:S(2)}) collective-permute-start(f32[32,256]{1,0:T(8,128)S(1)} %slice.51), channel_id=1, source_target_pairs={{0,1},{1,0},{2,3},{3,2},{4,5},{5,4},{6,7},{7,6},{8,9},{9,8},{10,11... | collective-permute-start | bytes 98312 | tf_op jit(solution)/shard_map/ppermute | solution.py:427
  56.3 0.6 %copy-start.2 = (f32[32,256]{1,0:T(8,128)}, f32[32,256]{1,0:T(8,128)S(1)}, u32[]{:S(2)}) copy-start(f32[32,256]{1,0:T(8,128)S(1)} %get-tuple-element.161) | copy-start | bytes 98308

commit v3 on v2

--- a/solution.py
+++ b/solution.py
@@ -19,6 +19,10 @@
 SLACK = 6 * 1024 * 1024
 PITCH = LANES + 9
 TURN = 16
+BIG = 8 * 1024 * 1024
+CAP = 25
+PACK = 2 * LANES
+XPITCH = 2 * WROWS + 1
 GROUPS = 16
 GROUP = 8
 ANY = pl.BlockSpec(memory_space=pl.ANY)
@@ -69,6 +73,14 @@
     return col, own_col, rank_col, own_row, rank_row
 
 
+def packed(cap, shape, dim):
+    lane = iota(shape, dim)
+    group = jnp.zeros(shape, I32)
+    for j in range(1, PACK // cap + 1):
+        group = group + jnp.where(lane >= j * cap, 1, 0)
+    return group, lane - group * cap
+
+
 def frequency_first(rows):
     shape = (FB * WROWS, rows * FB)
     r, c = iota(shape, 0), iota(shape, 1)
@@ -76,82 +88,71 @@
     return jnp.where(hit, 1.0, 0.0).astype(BF)
 
 
-def pick_kernel(cap, pieces, src_ref, spec_ref, keep_ref, send_ref, buf, keep_buf, send_buf, in_sem, out_sem):
-    _, windows, freqs, chans = spec_ref.shape
-    wp = windows // 2
+def pick_kernel(cap, src_ref, spec_ref, keep_ref, send_ref, buf, res, in_sem, out_sem):
+    _, _, freqs, chans = spec_ref.shape
     half = freqs // 2
-    part = half // pieces
-    groups = LANES // cap
+    wg = PACK // (2 * cap)
+    groups = in_sem.shape[0]
     me = lax.axis_index("chan")
     core = me & 1
-    chunks = in_sem.shape[0]
-    wc = wp // chunks
     ins = []
-    for j in range(chunks):
+    for b in range(groups):
         for k in range(2):
-            for w2 in range(2):
-                at = pl.ds(w2 * wp + j * wc, wc)
-                ins.append(pltpu.make_async_copy(spec_ref.at[k, at], buf.at[k, at], in_sem.at[j, 2 * k + w2]))
+            at = pl.ds(b * wg, wg)
+            ins.append(pltpu.make_async_copy(spec_ref.at[k, at], buf.at[k, at], in_sem.at[b, k]))
     for copy in ins:
         copy.start()
 
     row = source_row(src_ref)
     col, own_col, rank_col, _, _ = chip_ranks(row, 2 * chans)
     slots = row.shape[1]
-    lane_r = iota((slots, LANES), 1) & (cap - 1)
+    _, lane_r = packed(cap, (slots, PACK), 1)
     match = (own_col == shift(me, 2)) & (rank_col == lane_r)
     local = col - me * chans
     found = jnp.sum(jnp.where(match, local + 1, 0), axis=0, keepdims=True) - 1
-    shape = (groups * chans, LANES)
-    r, c = iota(shape, 0), iota(shape, 1)
-    hit = (shift(r, chans) == shift(c, cap)) & ((r & (chans - 1)) == found)
-    picker = jnp.where(hit, 1.0, 0.0).astype(BF)
+    shape = (2 * wg * chans, PACK)
+    lane_g, _ = packed(cap, (1, PACK), 1)
+    r = iota(shape, 0)
+    picker = jnp.where((shift(r, chans) == lane_g) & ((r & (chans - 1)) == found), 1.0, 0.0).astype(BF)
 
     mine = pl.multiple_of(core * half, half)
     other = pl.multiple_of((1 - core) * half, half)
     outs = []
-    for j in range(chunks):
-        for copy in ins[4 * j : 4 * j + 4]:
-            copy.wait()
-        for i in range(wc):
-            w = j * wc + i
-            if groups == 4:
-                turns, places = [[(w, 0), (w, 1), (wp + w, 0), (wp + w, 1)]], [w]
-            else:
-                turns, places = [[(w, 0), (w, 1)], [(wp + w, 0), (wp + w, 1)]], [w, wp + w]
-            for start, dest in ((other, send_buf), (mine, keep_buf)):
-                for turn, place in zip(turns, places):
-                    left = jnp.concatenate([buf[k, ww, pl.ds(start, half), :] for ww, k in turn], axis=1)
-                    got = jnp.dot(left, picker, preferred_element_type=F32).astype(BF)
-                    for p in range(pieces):
-                        dest[p, place] = got[p * part : (p + 1) * part]
-        for h in range(4 // groups if groups < 4 else 1):
-            at = pl.ds(h * wp + j * wc, wc)
-            for n, (dest, ref) in enumerate(((send_buf, send_ref), (keep_buf, keep_ref))):
-                outs.append(pltpu.make_async_copy(dest.at[:, at], ref.at[:, at], out_sem.at[j, 2 * h + n]))
-                outs[-1].start()
+    turn = 2 if groups % 2 == 0 else 1
+    for b0 in range(0, groups, turn):
+        lefts = []
+        for b in range(b0, b0 + turn):
+            for copy in ins[2 * b : 2 * b + 2]:
+                copy.wait()
+            lefts.append(jnp.concatenate([buf[k, b * wg + i] for i in range(wg) for k in range(2)], axis=1))
+        left = jnp.concatenate(lefts, axis=0)
+        got = jnp.dot(left, picker, preferred_element_type=F32).astype(BF)
+        for b in range(b0, b0 + turn):
+            res[b] = got[(b - b0) * freqs : (b - b0 + 1) * freqs]
+        for n, (start, ref) in enumerate(((other, send_ref), (mine, keep_ref))):
+            at = pl.ds(b0, turn)
+            outs.append(pltpu.make_async_copy(res.at[at, pl.ds(start, half)], ref.at[at], out_sem.at[b0, n]))
+            outs[-1].start()
     for copy in outs:
         copy.wait()
 
 
-def pick(spectra, src_ids, cap, pieces):
+def pick(spectra, src_ids, cap):
     _, windows, freqs, chans = spectra.shape
     half = freqs // 2
-    rows = windows * cap * 2 // LANES
-    chunks = 5 if (windows // 2) % 5 == 0 else 1
-    shape = (pieces, rows, half // pieces, LANES)
+    groups = windows // (PACK // (2 * cap))
+    shape = (groups, half, PACK)
     out = jax.ShapeDtypeStruct(shape, BF)
     return pl.pallas_call(
-        functools.partial(pick_kernel, cap, pieces),
+        functools.partial(pick_kernel, cap),
         in_specs=[VMEM, ANY],
         out_specs=[ANY, ANY],
         out_shape=[out, out],
         scratch_shapes=[
             pltpu.VMEM(spectra.shape, BF),
-            pltpu.VMEM(shape, BF),
-            pltpu.VMEM(shape, BF),
-            pltpu.SemaphoreType.DMA((chunks, 4)),
-            pltpu.SemaphoreType.DMA((chunks, 4)),
+            pltpu.VMEM((groups, freqs, PACK), BF),
+            pltpu.SemaphoreType.DMA((groups, 2)),
+            pltpu.SemaphoreType.DMA((groups, 2)),
         ],
         compiler_params=params((spectra.shape, BF), (shape, BF), (shape, BF)),
         name="pick_sources",
@@ -247,34 +248,34 @@
     refs = refs[6 + pieces * chips :]
     outs, refs = refs[:2], refs[2:]
     xs, cross, sums, whole = refs
-    rows, part, _ = xrefs[0].shape
+    groups, part, _ = xrefs[0].shape
     count, _, chans2 = recv.shape
     slots, bins, _ = hot.shape
-    wp = rows * LANES // (2 * cap) // 2
-    groups = LANES // cap
+    wg = PACK // (2 * cap)
+    wp = groups * wg // 2
+
     me = lax.axis_index("chan")
     row = source_row(src_ref)
     _, _, _, own_row, rank_row = chip_ranks(row, chans2)
-    own_row = jnp.concatenate([own_row] * groups, axis=1)
-    rank_row = jnp.concatenate([rank_row] * groups, axis=1)
-    shape = (LANES, groups * slots)
-    r, c = iota(shape, 0), iota(shape, 1)
-    aligned = (shift(r, cap) == shift(c, slots)) & ((r & (cap - 1)) == rank_row)
-    turn = frequency_first(wp)
+    own_row = jnp.concatenate([own_row] * (2 * wg), axis=1)
+    rank_row = jnp.concatenate([rank_row] * (2 * wg), axis=1)
+    lane_g, lane_r = packed(cap, (PACK, 1), 0)
+    wide = 2 * wg * slots
+    aligned = (lane_g == shift(iota((1, wide), 1), slots)) & (lane_r == rank_row)
     place = jnp.concatenate(
         [jnp.where(aligned & (own_row == (shift(me, 2) ^ d)), 1.0, 0.0).astype(BF) for d in range(chips)], axis=0
     )
     for p in range(pieces):
-        for b in range(part // FB):
-            at = pl.ds(b * FB, FB)
-            sides = []
-            for h in range(rows // wp):
-                ws = pl.ds(h * wp, wp)
-                got = jnp.concatenate([xrefs[p * chips + d][ws, at, :] for d in range(chips)], axis=2)
-                got = got.reshape(wp * FB, chips * LANES)
-                sides.append(jnp.dot(got, place, preferred_element_type=F32).astype(BF))
-            moved = jnp.concatenate(sides, axis=1) if len(sides) > 1 else sides[0]
-            xs[pl.ds((p * part + b * FB) * WROWS, FB * WROWS), :] = jnp.dot(turn, moved, preferred_element_type=F32)
+        got = jnp.concatenate([xrefs[p * chips + d][...] for d in range(chips)], axis=2)
+        got = jnp.dot(got.reshape(groups * part, chips * PACK), place, preferred_element_type=F32)
+        for w in range(2 * wp):
+            b, i = w // wg, w % wg
+            at = pl.ds(p * part * XPITCH + (w // wp) * WROWS + w % wp, part, stride=XPITCH)
+            xs[at, :] = got[b * part : (b + 1) * part, i * LANES : (i + 1) * LANES]
+        for w2 in range(2):
+            for w in range(wp, WROWS):
+                at = pl.ds(p * part * XPITCH + w2 * WROWS + w, part, stride=XPITCH)
+                xs[at, :] = jnp.zeros((part, LANES), F32)
 
     imag = iota((2 * WROWS, LANES), 1) >= slots
     quarter = shift(iota((1, 4 * 4 * WROWS), 1), 4 * WROWS)
@@ -285,9 +286,7 @@
             g, q = step * min(GROUPS, count // 8) + sub // 2, sub % 2
             lefts = []
             for j in range(4 * q, 4 * q + 4):
-                at = pl.ds(pl.multiple_of((g * 8 + j) * WROWS, WROWS), WROWS)
-                x = xs[at, :]
-                x = jnp.concatenate([x[:, :LANES], x[:, LANES:]], axis=0)
+                x = xs[pl.ds((g * 8 + j) * XPITCH, 2 * WROWS), :]
                 upper = jnp.where(imag, -x, x)
                 if j:
                     upper = pltpu.roll(upper, j, 1)
@@ -344,26 +343,28 @@
 
 def cross_and_bin(arrays, src_ids, recv, hot, counts, cos, sin, cap, nchan):
     pieces, chips = len(arrays), len(arrays[0])
-    rows, part, _ = arrays[0][0].shape
+    groups, part, _ = arrays[0][0].shape
     _, bins, chans2 = hot.shape
     lags = cos.shape[1]
     count = pieces * part
     per = bins // nchan
     out = jax.ShapeDtypeStruct((nchan // 2, per + 8, lags), F32)
-    operands = [((pieces, chips, rows, part, LANES), BF), (recv.shape, BF), (hot.shape, BF)]
     buffers = [
-        ((count * WROWS, 2 * LANES), F32),
+        ((count * XPITCH + 8, LANES), F32),
+        ((groups * part, 4 * PACK), F32),
+        ((chips * PACK, 4 * PACK), F32),
         ((2, count * PITCH + 8, chans2 // 2), F32),
         ((4 * count, bins), F32),
         ((bins, lags), F32),
     ]
+    scratch = [buffers[0]] + buffers[3:]
     return pl.pallas_call(
         functools.partial(cross_kernel, cap, chips, pieces),
         in_specs=[VMEM] * (6 + pieces * chips),
         out_specs=[VMEM, VMEM],
         out_shape=[out, out],
-        scratch_shapes=[pltpu.VMEM(shape, kind) for shape, kind in buffers],
-        compiler_params=params(*buffers),
+        scratch_shapes=[pltpu.VMEM(shape, kind) for shape, kind in scratch],
+        compiler_params=params(*buffers, *([(hot.shape, BF)] if hot.size > BIG else [])),
         name="cross_and_bin",
     )(src_ids, recv, hot, cos, sin, counts, *[x for held in arrays for x in held])
 
@@ -372,38 +373,42 @@
     return lax.ppermute(x, "chan", [(i, i ^ bit) for i in range(size)])
 
 
-def sums(nchan, nfreq, cap, spectra, src_ids, pair_bin, slot_of_bin):
+def gathered(nchan, pieces, chip):
+    rest = [1 << k for k in range(1, nchan.bit_length() - 1)]
+    result = []
+    held = [[x] for x in chip]
+    names = [[0] for _ in chip]
+    for hop in range(len(rest)):
+        bits = [rest[hop] if p % 2 == 0 else rest[-1 - hop] for p in range(pieces)]
+        early = [swap(chip[p], nchan, bits[p]) for p in range(pieces)]
+        for p, bit in enumerate(bits):
+            held[p] = held[p] + [early[p]] + [swap(x, nchan, bit) for x in held[p][1:]]
+            names[p] = names[p] + [name ^ bit for name in names[p]]
+    for p in range(pieces):
+        result.append([held[p][names[p].index(2 * d)] for d in range(len(held[p]))])
+    return result
+
+
+def chip_sources(nchan, cap, pieces, spectra, src_ids):
+    keep, send = pick(spectra, src_ids, cap)
+    got = swap(send, nchan, 1)
+    part = keep.shape[1] // pieces
+    return [keep[:, p * part : (p + 1) * part] + got[:, p * part : (p + 1) * part] for p in range(pieces)]
+
+
+def finish(nchan, nfreq, cap, chip, spectra, src_ids, pairs_own, got_pairs, slot_of_bin):
     _, windows, freqs, chans = spectra.shape
     half = freqs // 2
     bins = slot_of_bin.shape[0]
-    slots = src_ids.shape[0] * src_ids.shape[1]
     me = lax.axis_index("chan")
     core = me & 1
     rest = [1 << k for k in range(1, nchan.bit_length() - 1)]
-    pieces = 2
-
-    pairs_own = pair_bin.reshape(slots, chans)
-    got_pairs = swap(pairs_own, nchan, 1)
-    keep, send = pick(spectra, src_ids, cap, pieces)
-    got = swap(send, nchan, 1)
-    spectra_sent, got, got_pairs = lax.optimization_barrier((spectra, got, got_pairs))
+    arrays = gathered(nchan, len(chip), chip)
+    spectra_sent, chip = lax.optimization_barrier((spectra, chip))
     got_spec = swap(spectra_sent, nchan, 1)
-    chip = [keep[p] + got[p] for p in range(pieces)]
-    orders = [rest if p % 2 == 0 else rest[::-1] for p in range(pieces)]
-    arrays, routes = [[x] for x in chip], [[0] for _ in chip]
-    early = [[] for _ in chip]
-    for hop in range(len(rest)):
-        if hop == len(rest) - 1:
-            early = [[swap(chip[p], nchan, orders[p][hop])] for p in range(pieces)]
-        for p in range(pieces):
-            bit = orders[p][hop]
-            arrays[p] = arrays[p] + early[p] + [swap(x, nchan, bit) for x in arrays[p][len(early[p]) :]]
-            routes[p] = routes[p] + [name ^ bit for name in routes[p]]
-
     recv, hot, counts = tables(spectra, got_spec, pairs_own, got_pairs, slot_of_bin, nchan)
     cos, sin = lag_basis(lax.axis_index("freq") * freqs + core * half, half, F, NLAG, windows)
     counts = counts[0].reshape(bins // NLAG, NLAG)
-    arrays = [[held[names.index(2 * d)] for d in range(len(held))] for held, names in zip(arrays, routes)]
     out = cross_and_bin(arrays, src_ids, recv, hot, counts, cos, sin, cap, nchan)
     mine, other = out
 
@@ -442,21 +447,26 @@
 
 
 def body(nchan, nfreq, spectra, src_ids, pair_bin, slot_of_bin):
-    args = (spectra, src_ids, pair_bin, slot_of_bin)
+    chans = spectra.shape[3]
     slots = src_ids.shape[0] * src_ids.shape[1]
-    cap = slots // 2
-    owner = src_ids.reshape(-1) // (2 * spectra.shape[3])
-    loads = jnp.sum((owner[None, :] == lax.iota(I32, nchan // 2)[:, None]).astype(I32), axis=1)
-    fits = jnp.max(loads) <= cap
-    parts, count = sums(nchan, nfreq, cap, *args)
-    return lax.cond(
-        fits,
-        lambda parts, count, *args: scaled(parts, count),
-        lambda parts, count, *args: scaled(*sums(nchan, nfreq, slots, *args)),
-        parts,
-        count,
-        *args,
-    )
+    pieces = 2
+    pairs_own = pair_bin.reshape(slots, chans)
+    got_pairs = swap(pairs_own, nchan, 1)
+    chip = lax.optimization_barrier(chip_sources(nchan, CAP, pieces, spectra, src_ids))
+    owner = src_ids // (2 * chans)
+    loads = jnp.sum((owner[None] == lax.iota(I32, nchan // 2)[:, None, None]).astype(I32), axis=(1, 2))
+    fits = jnp.max(loads) <= CAP
+
+    def small(parts, count, *args):
+        return scaled(parts, count)
+
+    def large(parts, count, *args):
+        chip = chip_sources(nchan, slots, pieces, *args[:2])
+        return scaled(*finish(nchan, nfreq, slots, chip, *args))
+
+    args = (spectra, src_ids, pairs_own, got_pairs, slot_of_bin)
+    parts, count = finish(nchan, nfreq, CAP, chip, *args)
+    return lax.cond(fits, small, large, parts, count, *args)
 
 
 def solution(mesh):

time: 57.1 us -> 52.9 us (0.926)
  waiting for transfers between devices: 17.4 us -> 12.7 us
  starting transfers between devices: 17.3 us -> 18.7 us
  Pallas kernels: 19 us -> 18.2 us
    ppermute x13, waiting for transfers between devices: 14.8 us -> 10.1 us  [swap(): return lax.ppermute(x, 'chan', [(i, i ^ bit) for i in range(size)])]
    ppermute x13, starting transfers between devices: 12.9 us -> 14.3 us  [swap(): return lax.ppermute(x, 'chan', [(i, i ^ bit) for i in range(size)])]
    pallas_call x1, Pallas kernels: 10.5 us -> 9.5 us  [cross_and_bin(): pl.pallas_call(functools.partial(cross_kernel, cap, chips, pieces), in_sp...]
  transfers between devices with their start and end apart: 16 -> 16, of which waited for: 8 -> 9; matrix products, arithmetic and copies ran while one was open for 3% -> 3% of each run, Pallas kernels for 7% -> 7%
where the time goes in v3:
time: 52.9 us; the launch traced here: 52.7 us
  starting transfers between devices  18.7 us (35%)
  Pallas kernels  18.2 us (34%)
  waiting for transfers between devices  12.7 us (24%)
  other arithmetic  1.6 us (3%)
  between operations  0.82 us (2%)
  local copies, waits for them, and re-layouts  0.66 us (1%)
    ppermute x13, starting transfers between devices, swap(): return lax.ppermute(x, 'chan', [(i, i ^ bit) for i in range(size)])  14.3 us
    ppermute x13, waiting for transfers between devices, swap(): return lax.ppermute(x, 'chan', [(i, i ^ bit) for i in range(size)])  10.1 us
    pallas_call x1, Pallas kernels, cross_and_bin(): pl.pallas_call(functools.partial(cross_kernel, cap, chips, pieces), in_sp...  9.5 us
    pallas_call x1, Pallas kernels, pick(): pl.pallas_call(functools.partial(pick_kernel, cap), in_specs=[VMEM, ANY],...  4.85 us
    ppermute x3, starting transfers between devices, finish(): lax.ppermute(owned, 'freq', [(i, i ^ k) for i in range(nfreq)])  4.45 us
    pallas_call x1, Pallas kernels, tables(): pl.pallas_call(functools.partial(tables_kernel, nchan), in_specs=[ANY, AN...  3.82 us
    ppermute x3, waiting for transfers between devices, finish(): lax.ppermute(owned, 'freq', [(i, i ^ k) for i in range(nfreq)])  2.63 us
  transfers between devices with their start and end apart: 16, of which 9 were waited for; matrix products, arithmetic and copies ran while one was open for 3% of the time, Pallas kernels for 7%

profile of v3, /device:TPU:0, one launch (start us, length us, event | category | flops | bytes accessed | tf_op | source)
XLA Modules:
  0.0 52.7 jit_solution(12695783994192917384)
XLA Ops:
  0.0 0.0 copy-start.1
  0.0 0.0 copy-start.4
  0.0 4.8 %pick_sources.3 = (bf16[6,128,256]{2,1,0:T(8,128)(2,1)S(1)}, bf16[6,128,256]{2,1,0:T(8,128)(2,1)S(1)}) custom-call(s32[2,32]{1,0:T(2,128)} %refs_0_.1, bf16[2,30,256,128]{3,2,1,0:T(8,128)(2,1)} %spec_ref.3), custom_call_target="tpu_custom_call" | custom-call | tf_op jit(solution)/shard_map/pick_sources/pallas_call | solution.py:146
  4.9 0.5 collective-permute-start.16
  5.4 1.3 %collective-permute-done.16 = bf16[6,128,256]{2,1,0:T(8,128)(2,1)S(1)} collective-permute-done((bf16[6,128,256]{2,1,0:T(8,128)(2,1)S(1)}, bf16[6,128,256]{2,1,0:T(8,128)(2,1)S(1)}, u32[]{:S(2)}, u32[]{:S(2)}) %collective-permute-start.16) | collective-permute-done | bytes 393248 | tf_op jit(solution)/shard_map/ppermute | solution.py:373
  6.8 0.0 copy-start.3
  6.8 0.4 collective-permute-start.17
  7.2 0.0 copy-done.1
  7.2 0.1 collective-permute-start.15
  7.4 2.9 %collective-permute-start.18 = (bf16[6,64,256]{2,1,0:T(8,128)(2,1)S(1)}, bf16[6,64,256]{2,1,0:T(8,128)(2,1)S(1)}, u32[]{:S(2)}, u32[]{:S(2)}) collective-permute-start(bf16[6,64,256]{2,1,0:T(8,128)(2,1)S(1)} %get-tuple-element.80.refs_6_), channel_id=1, source_target_pairs={{0,8},{4,12},{8,0},{12,4},{16,24},{20,28},{24,16},{28,20},{1,9},{5... | collective-permute-start | bytes 589832 | tf_op jit(solution)/shard_map/ppermute | solution.py:373
  10.2 1.5 %collective-permute-start.22 = (bf16[6,64,256]{2,1,0:T(8,128)(2,1)S(1)}, bf16[6,64,256]{2,1,0:T(8,128)(2,1)S(1)}, u32[]{:S(2)}, u32[]{:S(2)}) collective-permute-start(bf16[6,64,256]{2,1,0:T(8,128)(2,1)S(1)} %get-tuple-element.81.refs_10_), channel_id=1, source_target_pairs={{0,16},{4,20},{8,24},{12,28},{16,0},{20,4},{24,8},{28,12},{1,17},{... | collective-permute-start | bytes 589832 | tf_op jit(solution)/shard_map/ppermute | solution.py:373
  11.7 0.5 collective-permute-start.19
  12.3 0.0 collective-permute-done.15.got_pairs
  12.3 2.2 %collective-permute-start.21 = (bf16[6,64,256]{2,1,0:T(8,128)(2,1)S(1)}, bf16[6,64,256]{2,1,0:T(8,128)(2,1)S(1)}, u32[]{:S(2)}, u32[]{:S(2)}) collective-permute-start(bf16[6,64,256]{2,1,0:T(8,128)(2,1)S(1)} %get-tuple-element.81.refs_10_), channel_id=1, source_target_pairs={{0,8},{4,12},{8,0},{12,4},{16,24},{20,28},{24,16},{28,20},{1,9},{5... | collective-permute-start | bytes 589832 | tf_op jit(solution)/shard_map/ppermute | solution.py:373
  14.5 0.9 %collective-permute-done.18.refs_7_ = bf16[6,64,256]{2,1,0:T(8,128)(2,1)S(1)} collective-permute-done((bf16[6,64,256]{2,1,0:T(8,128)(2,1)S(1)}, bf16[6,64,256]{2,1,0:T(8,128)(2,1)S(1)}, u32[]{:S(2)}, u32[]{:S(2)}) %collective-permute-start.18) | collective-permute-done | bytes 196640 | tf_op jit(solution)/shard_map/ppermute | solution.py:373
  15.4 1.8 %collective-permute-start.20 = (bf16[6,64,256]{2,1,0:T(8,128)(2,1)S(1)}, bf16[6,64,256]{2,1,0:T(8,128)(2,1)S(1)}, u32[]{:S(2)}, u32[]{:S(2)}) collective-permute-start(bf16[6,64,256]{2,1,0:T(8,128)(2,1)S(1)} %collective-permute-done.18.refs_7_), channel_id=1, source_target_pairs={{0,16},{4,20},{8,24},{12,28},{16,0},{20,4},{24,8},{28,12},{1,17},{... | collective-permute-start | bytes 589832 | tf_op jit(solution)/shard_map/ppermute | solution.py:373
  17.2 0.8 %collective-permute-done.22.refs_12_ = bf16[6,64,256]{2,1,0:T(8,128)(2,1)S(1)} collective-permute-done((bf16[6,64,256]{2,1,0:T(8,128)(2,1)S(1)}, bf16[6,64,256]{2,1,0:T(8,128)(2,1)S(1)}, u32[]{:S(2)}, u32[]{:S(2)}) %collective-permute-start.22) | collective-permute-done | bytes 196640 | tf_op jit(solution)/shard_map/ppermute | solution.py:373
  18.0 0.7 %collective-permute-start.23 = (bf16[6,64,256]{2,1,0:T(8,128)(2,1)S(1)}, bf16[6,64,256]{2,1,0:T(8,128)(2,1)S(1)}, u32[]{:S(2)}, u32[]{:S(2)}) collective-permute-start(bf16[6,64,256]{2,1,0:T(8,128)(2,1)S(1)} %collective-permute-done.22.refs_12_), channel_id=1, source_target_pairs={{0,8},{4,12},{8,0},{12,4},{16,24},{20,28},{24,16},{28,20},{1,9},{5... | collective-permute-start | bytes 589832 | tf_op jit(solution)/shard_map/ppermute | solution.py:373
  18.7 0.6 %negate_multiply_fusion.1 = (f32[128,256]{1,0:T(8,128)S(1)}, f32[128,256]{1,0:T(8,128)S(1)}) fusion(s32[256]{0:T(256)S(1)} %iota_add_fusion.2, s32[128]{0:T(128)S(1)} %iota_add_fusion.3), kind=kLoop, calls=%fused_computation.37 | loop fusion | flops 557056 | bytes 263680 | tf_op jit(solution)/shard_map/mul | solution.py:38
  19.3 0.0 collective-permute-done.17.got_ref
  19.3 0.0 copy-done.4
  19.3 3.8 %tables.3 = (bf16[128,64,256]{2,1,0:T(8,128)(2,1)S(1)}, bf16[64,256,256]{2,1,0:T(8,128)(2,1)S(1)}, f32[8,256]{1,0:T(8,128)S(1)}) custom-call(bf16[2,30,256,128]{3,2,1,0:T(8,128)(2,1)} %spec_ref.3, bf16[2,30,256,128]{3,2,1,0:T(8,128)(2,1)} %collective-permute-done.17.got_ref, s32[64,128]{1,0:T(8,128)S(1)} %bitcast.32, ...), custom_call_target="tpu_custom_call" | custom-call | tf_op jit(solution)/shard_map/tables/pallas_call | solution.py:224
  23.1 0.0 collective-permute-done.19.refs_8_
  23.2 0.0 collective-permute-done.21.refs_11_
  23.2 2.2 %collective-permute-done.20.refs_9_ = bf16[6,64,256]{2,1,0:T(8,128)(2,1)S(1)} collective-permute-done((bf16[6,64,256]{2,1,0:T(8,128)(2,1)S(1)}, bf16[6,64,256]{2,1,0:T(8,128)(2,1)S(1)}, u32[]{:S(2)}, u32[]{:S(2)}) %collective-permute-start.20) | collective-permute-done | bytes 196640 | tf_op jit(solution)/shard_map/ppermute | solution.py:373
  25.3 0.0 collective-permute-done.23.refs_13_
  25.3 0.0 copy-done.3
  25.3 9.5 %cross_and_bin.3 = (f32[4,40,256]{2,1,0:T(8,128)S(1)}, f32[4,40,256]{2,1,0:T(8,128)S(1)}) custom-call(s32[2,32]{1,0:T(2,128)S(1)} %copy-done.3, bf16[128,64,256]{2,1,0:T(8,128)(2,1)S(1)} %get-tuple-element.83.refs_1_, bf16[64,256,256]{2,1,0:T(8,128)(2,1)S(1)} %get-tuple-element.84.refs_2_, f32[128,256]{1,0:T(8,128)S(1)} %get-tuple-element.102.refs_3_, ...), custom_call_target="tpu_custom_call" | custom-call | tf_op jit(solution)/shard_map/cross_and_bin/pallas_call | solution.py:361
  34.8 0.1 collective-permute-start.24
  34.9 1.4 %collective-permute-done.24 = f32[4,40,256]{2,1,0:T(8,128)S(1)} collective-permute-done((f32[4,40,256]{2,1,0:T(8,128)S(1)}, f32[4,40,256]{2,1,0:T(8,128)S(1)}, u32[]{:S(2)}, u32[]{:S(2)}) %collective-permute-start.24) | collective-permute-done | bytes 163872 | tf_op jit(solution)/shard_map/ppermute | solution.py:373
  36.3 0.6 %collective-permute-start.25 = (f32[40,256]{1,0:T(8,128)S(1)}, f32[40,256]{1,0:T(8,128)S(1)}, u32[]{:S(2)}, u32[]{:S(2)}) collective-permute-start(f32[40,256]{1,0:T(8,128)S(1)} %get-tuple-element.98), channel_id=1, source_target_pairs={{0,8},{4,12},{8,0},{12,4},{16,24},{20,28},{24,16},{28,20},{1,9},{5... | collective-permute-start | bytes 122888 | tf_op jit(solution)/shard_map/ppermute | solution.py:373
  36.9 1.6 %collective-permute-start.26 = (f32[40,256]{1,0:T(8,128)S(1)}, f32[40,256]{1,0:T(8,128)S(1)}, u32[]{:S(2)}, u32[]{:S(2)}) collective-permute-start(f32[40,256]{1,0:T(8,128)S(1)} %get-tuple-element.100), channel_id=1, source_target_pairs={{0,16},{4,20},{8,24},{12,28},{16,0},{20,4},{24,8},{28,12},{1,17},{... | collective-permute-start | bytes 122888 | tf_op jit(solution)/shard_map/ppermute | solution.py:373
  38.5 1.4 %collective-permute-start.27 = (f32[40,256]{1,0:T(8,128)S(1)}, f32[40,256]{1,0:T(8,128)S(1)}, u32[]{:S(2)}, u32[]{:S(2)}) collective-permute-start(f32[40,256]{1,0:T(8,128)S(1)} %get-tuple-element.99), channel_id=1, source_target_pairs={{0,24},{4,28},{8,16},{12,20},{16,8},{20,12},{24,0},{28,4},{1,25},{... | collective-permute-start | bytes 122888 | tf_op jit(solution)/shard_map/ppermute | solution.py:373
  39.9 0.5 collective-permute-done.25
  40.4 0.5 %collective-permute-done.26 = f32[40,256]{1,0:T(8,128)S(1)} collective-permute-done((f32[40,256]{1,0:T(8,128)S(1)}, f32[40,256]{1,0:T(8,128)S(1)}, u32[]{:S(2)}, u32[]{:S(2)}) %collective-permute-start.26) | collective-permute-done | bytes 40992 | tf_op jit(solution)/shard_map/ppermute | solution.py:373
  40.9 2.5 %collective-permute-done.27 = f32[40,256]{1,0:T(8,128)S(1)} collective-permute-done((f32[40,256]{1,0:T(8,128)S(1)}, f32[40,256]{1,0:T(8,128)S(1)}, u32[]{:S(2)}, u32[]{:S(2)}) %collective-permute-start.27) | collective-permute-done | bytes 40992 | tf_op jit(solution)/shard_map/ppermute | solution.py:373
  43.4 3.7 %collective-permute-start.28 = (f32[32,256]{1,0:T(8,128)S(1)}, f32[32,256]{1,0:T(8,128)S(1)}, u32[]{:S(2)}, u32[]{:S(2)}) collective-permute-start(f32[32,256]{1,0:T(8,128)S(1)} %slice.55), channel_id=1, source_target_pairs={{0,3},{1,2},{2,1},{3,0},{4,7},{5,6},{6,5},{7,4},{8,11},{9,10},{10,... | collective-permute-start | bytes 98312 | tf_op jit(solution)/shard_map/ppermute | solution.py:432
  47.1 0.0 collective-permute-start.29
  47.1 0.8 %collective-permute-start.30 = (f32[32,256]{1,0:T(8,128)S(1)}, f32[32,256]{1,0:T(8,128)S(1)}, u32[]{:S(2)}, u32[]{:S(2)}) collective-permute-start(f32[32,256]{1,0:T(8,128)S(1)} %slice.55), channel_id=1, source_target_pairs={{0,1},{1,0},{2,3},{3,2},{4,5},{5,4},{6,7},{7,6},{8,9},{9,8},{10,11... | collective-permute-start | bytes 98312 | tf_op jit(solution)/shard_map/ppermute | solution.py:432
  47.9 0.1 convert_reduce_fusion
  48.0 0.6 %reduce_max.9 = s32[]{:T(128)} reduce(s32[4]{0:T(128)S(1)} %convert_reduce_fusion, s32[]{:T(128)} %constant.140.clone.1), dimensions={0}, to_apply=%region_1.2 | reduce | flops 3 | bytes 24 | tf_op jit(solution)/shard_map/reduce_max | solution.py:458
  49.3 0.0 collective-permute-done.28
  49.3 2.6 %collective-permute-done.29 = f32[32,256]{1,0:T(8,128)S(1)} collective-permute-done((f32[32,256]{1,0:T(8,128)S(1)}, f32[32,256]{1,0:T(8,128)S(1)}, u32[]{:S(2)}, u32[]{:S(2)}) %collective-permute-start.29) | collective-permute-done | bytes 32800 | tf_op jit(solution)/shard_map/ppermute | solution.py:432
  51.9 0.0 collective-permute-done.30
  51.9 0.2 conditional.1
  51.9 0.1 sqrt_bitcast_fusion
  52.0 0.1 add_divide_fusion.1
  52.1 0.0 copy-start.2
  52.1 0.6 %copy-done.2 = f32[32,256]{1,0:T(8,128)} copy-done((f32[32,256]{1,0:T(8,128)}, f32[32,256]{1,0:T(8,128)S(1)}, u32[]{:S(2)}) %copy-start.2) | copy-done | bytes 32792
  (10 shorter events, 0.1 us)
Async XLA Ops:
  0.0 7.2 %copy-start.1 = (s32[2,32,128]{2,1,0:T(8,128)S(1)}, s32[2,32,128]{2,1,0:T(8,128)}, u32[]{:S(2)}) copy-start(s32[2,32,128]{2,1,0:T(8,128)} %param.8) | copy-start | bytes 98308
  0.0 19.3 %copy-start.4 = (s32[256]{0:T(256)S(1)}, s32[256]{0:T(256)}, u32[]{:S(2)}) copy-start(s32[256]{0:T(256)} %param.9) | copy-start | bytes 3076
  4.9 1.9 %collective-permute-start.16 = (bf16[6,128,256]{2,1,0:T(8,128)(2,1)S(1)}, bf16[6,128,256]{2,1,0:T(8,128)(2,1)S(1)}, u32[]{:S(2)}, u32[]{:S(2)}) collective-permute-start(bf16[6,128,256]{2,1,0:T(8,128)(2,1)S(1)} %get-tuple-element.79), channel_id=1, source_target_pairs={{0,4},{4,0},{8,12},{12,8},{16,20},{20,16},{24,28},{28,24},{1,5},{5... | collective-permute-start | bytes 1179656 | tf_op jit(solution)/shard_map/ppermute | solution.py:373
  6.8 18.5 %copy-start.3 = (s32[2,32]{1,0:T(2,128)S(1)}, s32[2,32]{1,0:T(2,128)}, u32[]{:S(2)}) copy-start(s32[2,32]{1,0:T(2,128)} %refs_0_.1) | copy-start | bytes 772
  6.8 12.5 %collective-permute-start.17 = (bf16[2,30,256,128]{3,2,1,0:T(8,128)(2,1)}, bf16[2,30,256,128]{3,2,1,0:T(8,128)(2,1)}, u32[]{:S(2)}, u32[]{:S(2)}) collective-permute-start(bf16[2,30,256,128]{3,2,1,0:T(8,128)(2,1)} %spec_ref.3), channel_id=1, source_target_pairs={{0,4},{4,0},{8,12},{12,8},{16,20},{20,16},{24,28},{28,24},{1,5},{5... | collective-permute-start | bytes 11796488 | tf_op jit(solution)/shard_map/ppermute | solution.py:373
  7.2 5.0 %collective-permute-start.15 = (s32[64,128]{1,0:T(8,128)S(1)}, s32[64,128]{1,0:T(8,128)S(1)}, u32[]{:S(2)}, u32[]{:S(2)}) collective-permute-start(s32[64,128]{1,0:T(8,128)S(1)} %bitcast.31), channel_id=1, source_target_pairs={{0,4},{4,0},{8,12},{12,8},{16,20},{20,16},{24,28},{28,24},{1,5},{5... | collective-permute-start | bytes 98312 | tf_op jit(solution)/shard_map/ppermute | solution.py:373
  7.4 8.1 %collective-permute-start.18 = (bf16[6,64,256]{2,1,0:T(8,128)(2,1)S(1)}, bf16[6,64,256]{2,1,0:T(8,128)(2,1)S(1)}, u32[]{:S(2)}, u32[]{:S(2)}) collective-permute-start(bf16[6,64,256]{2,1,0:T(8,128)(2,1)S(1)} %get-tuple-element.80.refs_6_), channel_id=1, source_target_pairs={{0,8},{4,12},{8,0},{12,4},{16,24},{20,28},{24,16},{28,20},{1,9},{5... | collective-permute-start | bytes 589832 | tf_op jit(solution)/shard_map/ppermute | solution.py:373
  10.2 7.8 %collective-permute-start.22 = (bf16[6,64,256]{2,1,0:T(8,128)(2,1)S(1)}, bf16[6,64,256]{2,1,0:T(8,128)(2,1)S(1)}, u32[]{:S(2)}, u32[]{:S(2)}) collective-permute-start(bf16[6,64,256]{2,1,0:T(8,128)(2,1)S(1)} %get-tuple-element.81.refs_10_), channel_id=1, source_target_pairs={{0,16},{4,20},{8,24},{12,28},{16,0},{20,4},{24,8},{28,12},{1,17},{... | collective-permute-start | bytes 589832 | tf_op jit(solution)/shard_map/ppermute | solution.py:373
  11.7 11.4 %collective-permute-start.19 = (bf16[6,64,256]{2,1,0:T(8,128)(2,1)S(1)}, bf16[6,64,256]{2,1,0:T(8,128)(2,1)S(1)}, u32[]{:S(2)}, u32[]{:S(2)}) collective-permute-start(bf16[6,64,256]{2,1,0:T(8,128)(2,1)S(1)} %get-tuple-element.80.refs_6_), channel_id=1, source_target_pairs={{0,16},{4,20},{8,24},{12,28},{16,0},{20,4},{24,8},{28,12},{1,17},{... | collective-permute-start | bytes 589832 | tf_op jit(solution)/shard_map/ppermute | solution.py:373
  12.3 10.9 %collective-permute-start.21 = (bf16[6,64,256]{2,1,0:T(8,128)(2,1)S(1)}, bf16[6,64,256]{2,1,0:T(8,128)(2,1)S(1)}, u32[]{:S(2)}, u32[]{:S(2)}) collective-permute-start(bf16[6,64,256]{2,1,0:T(8,128)(2,1)S(1)} %get-tuple-element.81.refs_10_), channel_id=1, source_target_pairs={{0,8},{4,12},{8,0},{12,4},{16,24},{20,28},{24,16},{28,20},{1,9},{5... | collective-permute-start | bytes 589832 | tf_op jit(solution)/shard_map/ppermute | solution.py:373
  15.4 9.9 %collective-permute-start.20 = (bf16[6,64,256]{2,1,0:T(8,128)(2,1)S(1)}, bf16[6,64,256]{2,1,0:T(8,128)(2,1)S(1)}, u32[]{:S(2)}, u32[]{:S(2)}) collective-permute-start(bf16[6,64,256]{2,1,0:T(8,128)(2,1)S(1)} %collective-permute-done.18.refs_7_), channel_id=1, source_target_pairs={{0,16},{4,20},{8,24},{12,28},{16,0},{20,4},{24,8},{28,12},{1,17},{... | collective-permute-start | bytes 589832 | tf_op jit(solution)/shard_map/ppermute | solution.py:373
  18.0 7.3 %collective-permute-start.23 = (bf16[6,64,256]{2,1,0:T(8,128)(2,1)S(1)}, bf16[6,64,256]{2,1,0:T(8,128)(2,1)S(1)}, u32[]{:S(2)}, u32[]{:S(2)}) collective-permute-start(bf16[6,64,256]{2,1,0:T(8,128)(2,1)S(1)} %collective-permute-done.22.refs_12_), channel_id=1, source_target_pairs={{0,8},{4,12},{8,0},{12,4},{16,24},{20,28},{24,16},{28,20},{1,9},{5... | collective-permute-start | bytes 589832 | tf_op jit(solution)/shard_map/ppermute | solution.py:373
  34.8 1.5 %collective-permute-start.24 = (f32[4,40,256]{2,1,0:T(8,128)S(1)}, f32[4,40,256]{2,1,0:T(8,128)S(1)}, u32[]{:S(2)}, u32[]{:S(2)}) collective-permute-start(f32[4,40,256]{2,1,0:T(8,128)S(1)} %get-tuple-element.87), channel_id=1, source_target_pairs={{0,4},{4,0},{8,12},{12,8},{16,20},{20,16},{24,28},{28,24},{1,5},{5... | collective-permute-start | bytes 491528 | tf_op jit(solution)/shard_map/ppermute | solution.py:373
  36.3 4.1 %collective-permute-start.25 = (f32[40,256]{1,0:T(8,128)S(1)}, f32[40,256]{1,0:T(8,128)S(1)}, u32[]{:S(2)}, u32[]{:S(2)}) collective-permute-start(f32[40,256]{1,0:T(8,128)S(1)} %get-tuple-element.98), channel_id=1, source_target_pairs={{0,8},{4,12},{8,0},{12,4},{16,24},{20,28},{24,16},{28,20},{1,9},{5... | collective-permute-start | bytes 122888 | tf_op jit(solution)/shard_map/ppermute | solution.py:373
  36.9 4.0 %collective-permute-start.26 = (f32[40,256]{1,0:T(8,128)S(1)}, f32[40,256]{1,0:T(8,128)S(1)}, u32[]{:S(2)}, u32[]{:S(2)}) collective-permute-start(f32[40,256]{1,0:T(8,128)S(1)} %get-tuple-element.100), channel_id=1, source_target_pairs={{0,16},{4,20},{8,24},{12,28},{16,0},{20,4},{24,8},{28,12},{1,17},{... | collective-permute-start | bytes 122888 | tf_op jit(solution)/shard_map/ppermute | solution.py:373
  38.5 4.9 %collective-permute-start.27 = (f32[40,256]{1,0:T(8,128)S(1)}, f32[40,256]{1,0:T(8,128)S(1)}, u32[]{:S(2)}, u32[]{:S(2)}) collective-permute-start(f32[40,256]{1,0:T(8,128)S(1)} %get-tuple-element.99), channel_id=1, source_target_pairs={{0,24},{4,28},{8,16},{12,20},{16,8},{20,12},{24,0},{28,4},{1,25},{... | collective-permute-start | bytes 122888 | tf_op jit(solution)/shard_map/ppermute | solution.py:373
  43.4 5.9 %collective-permute-start.28 = (f32[32,256]{1,0:T(8,128)S(1)}, f32[32,256]{1,0:T(8,128)S(1)}, u32[]{:S(2)}, u32[]{:S(2)}) collective-permute-start(f32[32,256]{1,0:T(8,128)S(1)} %slice.55), channel_id=1, source_target_pairs={{0,3},{1,2},{2,1},{3,0},{4,7},{5,6},{6,5},{7,4},{8,11},{9,10},{10,... | collective-permute-start | bytes 98312 | tf_op jit(solution)/shard_map/ppermute | solution.py:432
  47.1 4.8 %collective-permute-start.29 = (f32[32,256]{1,0:T(8,128)S(1)}, f32[32,256]{1,0:T(8,128)S(1)}, u32[]{:S(2)}, u32[]{:S(2)}) collective-permute-start(f32[32,256]{1,0:T(8,128)S(1)} %slice.55), channel_id=1, source_target_pairs={{0,2},{1,3},{2,0},{3,1},{4,6},{5,7},{6,4},{7,5},{8,10},{9,11},{10,... | collective-permute-start | bytes 98312 | tf_op jit(solution)/shard_map/ppermute | solution.py:432
  47.1 4.8 %collective-permute-start.30 = (f32[32,256]{1,0:T(8,128)S(1)}, f32[32,256]{1,0:T(8,128)S(1)}, u32[]{:S(2)}, u32[]{:S(2)}) collective-permute-start(f32[32,256]{1,0:T(8,128)S(1)} %slice.55), channel_id=1, source_target_pairs={{0,1},{1,0},{2,3},{3,2},{4,5},{5,4},{6,7},{7,6},{8,9},{9,8},{10,11... | collective-permute-start | bytes 98312 | tf_op jit(solution)/shard_map/ppermute | solution.py:432
  52.1 0.6 %copy-start.2 = (f32[32,256]{1,0:T(8,128)}, f32[32,256]{1,0:T(8,128)S(1)}, u32[]{:S(2)}) copy-start(f32[32,256]{1,0:T(8,128)S(1)} %get-tuple-element.158) | copy-start | bytes 98308

commit v4 on v3

--- a/solution.py
+++ b/solution.py
@@ -157,6 +157,35 @@
         compiler_params=params((spectra.shape, BF), (shape, BF), (shape, BF)),
         name="pick_sources",
     )(src_ids, spectra)
+
+
+def place_sources(cap, names, src_ref, per_chip, xrefs, xs):
+    chips = len(names)
+    groups, part, _ = xrefs[0].shape
+    wg = PACK // (2 * cap)
+    wp = groups * wg // 2
+    me = lax.axis_index("chan")
+    row = source_row(src_ref)
+    slots = row.shape[1]
+    _, _, _, own_row, rank_row = chip_ranks(row, per_chip)
+    own_row = jnp.concatenate([own_row] * (2 * wg), axis=1)
+    rank_row = jnp.concatenate([rank_row] * (2 * wg), axis=1)
+    lane_g, lane_r = packed(cap, (PACK, 1), 0)
+    wide = 2 * wg * slots
+    aligned = (lane_g == shift(iota((1, wide), 1), slots)) & (lane_r == rank_row)
+    place = [jnp.where(aligned & (own_row == (shift(me, 2) ^ d)), 1.0, 0.0).astype(BF) for d in names]
+    place = jnp.concatenate(place, axis=0)
+    for p in range(len(xrefs) // chips):
+        got = jnp.concatenate([xrefs[p * chips + n][...] for n in range(chips)], axis=2)
+        got = jnp.dot(got.reshape(groups * part, chips * PACK), place, preferred_element_type=F32)
+        for w in range(2 * wp):
+            b, i = w // wg, w % wg
+            at = pl.ds(p * part * XPITCH + (w // wp) * WROWS + w % wp, part, stride=XPITCH)
+            xs[at, :] = got[b * part : (b + 1) * part, i * LANES : (i + 1) * LANES]
+        for w2 in range(2):
+            for w in range(wp, WROWS):
+                at = pl.ds(p * part * XPITCH + w2 * WROWS + w, part, stride=XPITCH)
+                xs[at, :] = jnp.zeros((part, LANES), F32)
 
 
 def tables_kernel(
@@ -242,41 +271,33 @@
     )(spectra, got, own_pairs, got_pairs, slot_of_bin[None, :])
 
 
-def cross_kernel(cap, chips, pieces, *refs):
-    src_ref, recv, hot, cos_ref, sin_ref, count_ref = refs[:6]
-    xrefs = refs[6 : 6 + pieces * chips]
-    refs = refs[6 + pieces * chips :]
+def early_kernel(cap, names, per_chip, src_ref, *refs):
+    place_sources(cap, names, src_ref, per_chip, refs[:-1], refs[-1])
+
+
+def place_early(arrays, names, src_ids, cap, per_chip):
+    groups, part, _ = arrays[0].shape
+    count = len(arrays) // len(names) * part
+    shape = (count * XPITCH + 8, LANES)
+    return pl.pallas_call(
+        functools.partial(early_kernel, cap, names, per_chip),
+        in_specs=[VMEM] * (1 + len(arrays)),
+        out_specs=VMEM,
+        out_shape=jax.ShapeDtypeStruct(shape, F32),
+        compiler_params=params(*staging(arrays, names)),
+        name="place_early",
+    )(src_ids, *arrays)
+
+
+def cross_kernel(cap, names, pieces, *refs):
+    src_ref, recv, hot, cos_ref, sin_ref, count_ref, xs_early = refs[:7]
+    xrefs = refs[7 : 7 + pieces * len(names)]
+    refs = refs[7 + pieces * len(names) :]
     outs, refs = refs[:2], refs[2:]
     xs, cross, sums, whole = refs
-    groups, part, _ = xrefs[0].shape
     count, _, chans2 = recv.shape
     slots, bins, _ = hot.shape
-    wg = PACK // (2 * cap)
-    wp = groups * wg // 2
-
-    me = lax.axis_index("chan")
-    row = source_row(src_ref)
-    _, _, _, own_row, rank_row = chip_ranks(row, chans2)
-    own_row = jnp.concatenate([own_row] * (2 * wg), axis=1)
-    rank_row = jnp.concatenate([rank_row] * (2 * wg), axis=1)
-    lane_g, lane_r = packed(cap, (PACK, 1), 0)
-    wide = 2 * wg * slots
-    aligned = (lane_g == shift(iota((1, wide), 1), slots)) & (lane_r == rank_row)
-    place = jnp.concatenate(
-        [jnp.where(aligned & (own_row == (shift(me, 2) ^ d)), 1.0, 0.0).astype(BF) for d in range(chips)], axis=0
-    )
-    for p in range(pieces):
-        got = jnp.concatenate([xrefs[p * chips + d][...] for d in range(chips)], axis=2)
-        got = jnp.dot(got.reshape(groups * part, chips * PACK), place, preferred_element_type=F32)
-        for w in range(2 * wp):
-            b, i = w // wg, w % wg
-            at = pl.ds(p * part * XPITCH + (w // wp) * WROWS + w % wp, part, stride=XPITCH)
-            xs[at, :] = got[b * part : (b + 1) * part, i * LANES : (i + 1) * LANES]
-        for w2 in range(2):
-            for w in range(wp, WROWS):
-                at = pl.ds(p * part * XPITCH + w2 * WROWS + w, part, stride=XPITCH)
-                xs[at, :] = jnp.zeros((part, LANES), F32)
-
+    place_sources(cap, names, src_ref, chans2, xrefs, xs)
     imag = iota((2 * WROWS, LANES), 1) >= slots
     quarter = shift(iota((1, 4 * 4 * WROWS), 1), 4 * WROWS)
     masks = [jnp.where(quarter == i, 1.0, 0.0).astype(BF) for i in range(4)]
@@ -286,7 +307,8 @@
             g, q = step * min(GROUPS, count // 8) + sub // 2, sub % 2
             lefts = []
             for j in range(4 * q, 4 * q + 4):
-                x = xs[pl.ds((g * 8 + j) * XPITCH, 2 * WROWS), :]
+                at = pl.ds((g * 8 + j) * XPITCH, 2 * WROWS)
+                x = xs_early[at, :] + xs[at, :]
                 upper = jnp.where(imag, -x, x)
                 if j:
                     upper = pltpu.roll(upper, j, 1)
@@ -330,8 +352,8 @@
     total = sums[pl.ds(0, 2 * count), :] + sums[pl.ds(2 * count, 2 * count), :]
     table = jnp.concatenate([cos_ref[...], sin_ref[...]], axis=0)
     whole[...] = lax.dot_general(total, table, (((0,), (0,)), ((), ())), precision=lax.Precision.HIGHEST, preferred_element_type=F32)
-    core = me & 1
-    blocks, padded, lags = outs[0].shape
+    core = lax.axis_index("chan") & 1
+    blocks = outs[0].shape[0]
     per = bins // (2 * blocks)
     crows = count_ref.shape[0]
     for which, dest in ((core, outs[0]), (1 - core, outs[1])):
@@ -341,32 +363,34 @@
             dest[d, pl.ds(per, crows), :] = count_ref[...]
 
 
-def cross_and_bin(arrays, src_ids, recv, hot, counts, cos, sin, cap, nchan):
-    pieces, chips = len(arrays), len(arrays[0])
-    groups, part, _ = arrays[0][0].shape
+def staging(arrays, names):
+    groups, part, _ = arrays[0].shape
+    chips = len(names)
+    return [((groups * part, 4 * PACK), F32), ((groups * part, chips * PACK), BF), ((chips * PACK, 4 * PACK), F32)]
+
+
+def cross_and_bin(arrays, names, xs_early, src_ids, recv, hot, counts, cos, sin, cap, nchan):
     _, bins, chans2 = hot.shape
     lags = cos.shape[1]
-    count = pieces * part
+    count = recv.shape[0]
     per = bins // nchan
     out = jax.ShapeDtypeStruct((nchan // 2, per + 8, lags), F32)
-    buffers = [
-        ((count * XPITCH + 8, LANES), F32),
-        ((groups * part, 4 * PACK), F32),
-        ((chips * PACK, 4 * PACK), F32),
+    scratch = [
+        (xs_early.shape, F32),
         ((2, count * PITCH + 8, chans2 // 2), F32),
         ((4 * count, bins), F32),
         ((bins, lags), F32),
     ]
-    scratch = [buffers[0]] + buffers[3:]
+    buffers = scratch + staging(arrays, names)
     return pl.pallas_call(
-        functools.partial(cross_kernel, cap, chips, pieces),
-        in_specs=[VMEM] * (6 + pieces * chips),
+        functools.partial(cross_kernel, cap, names, len(arrays) // len(names)),
+        in_specs=[VMEM] * (7 + len(arrays)),
         out_specs=[VMEM, VMEM],
         out_shape=[out, out],
         scratch_shapes=[pltpu.VMEM(shape, kind) for shape, kind in scratch],
         compiler_params=params(*buffers, *([(hot.shape, BF)] if hot.size > BIG else [])),
         name="cross_and_bin",
-    )(src_ids, recv, hot, cos, sin, counts, *[x for held in arrays for x in held])
+    )(src_ids, recv, hot, cos, sin, counts, xs_early, *arrays)
 
 
 def swap(x, size, bit):
@@ -406,10 +430,16 @@
     arrays = gathered(nchan, len(chip), chip)
     spectra_sent, chip = lax.optimization_barrier((spectra, chip))
     got_spec = swap(spectra_sent, nchan, 1)
+    chips = len(arrays[0])
+    early, late = list(range(chips - chips // 4)), list(range(chips - chips // 4, chips))
+    first = [held[d] for held in arrays for d in early]
     recv, hot, counts = tables(spectra, got_spec, pairs_own, got_pairs, slot_of_bin, nchan)
+    counts, first = lax.optimization_barrier((counts, first))
+    xs_early = place_early(first, early, src_ids, cap, 2 * chans)
     cos, sin = lag_basis(lax.axis_index("freq") * freqs + core * half, half, F, NLAG, windows)
     counts = counts[0].reshape(bins // NLAG, NLAG)
-    out = cross_and_bin(arrays, src_ids, recv, hot, counts, cos, sin, cap, nchan)
+    last = [held[d] for held in arrays for d in late]
+    out = cross_and_bin(last, late, xs_early, src_ids, recv, hot, counts, cos, sin, cap, nchan)
     mine, other = out
 
     per = bins // nchan

time: 52.9 us -> 52.2 us (0.987)
  waiting for transfers between devices: 12.7 us -> 11.3 us
  Pallas kernels: 18.2 us -> 18.8 us
    ppermute x13, waiting for transfers between devices: 10.1 us -> 8.72 us  [swap(): return lax.ppermute(x, 'chan', [(i, i ^ bit) for i in range(size)])]
    pallas_call x1 -> x2, Pallas kernels: 9.5 us -> 10.1 us  [the longest x1 8.8 us: cross_and_bin(): pl.pallas_call(functools.partial(cross_kernel, cap, names, len(arrays) //...]
  transfers between devices with their start and end apart: 16 -> 16, of which waited for: 9 -> 9; matrix products, arithmetic and copies ran while one was open for 3% -> 3% of each run, Pallas kernels for 7% -> 10%
where the time goes in v4:
time: 52.2 us; the launch traced here: 52 us
  Pallas kernels  18.8 us (36%)
  starting transfers between devices  18.7 us (36%)
  waiting for transfers between devices  11.3 us (22%)
  other arithmetic  1.6 us (3%)
  between operations  0.83 us (2%)
  local copies, waits for them, and re-layouts  0.66 us (1%)
    ppermute x13, starting transfers between devices, swap(): return lax.ppermute(x, 'chan', [(i, i ^ bit) for i in range(size)])  14.3 us
    pallas_call x1, Pallas kernels, cross_and_bin(): pl.pallas_call(functools.partial(cross_kernel, cap, names, len(arrays) //...  8.8 us
    ppermute x13, waiting for transfers between devices, swap(): return lax.ppermute(x, 'chan', [(i, i ^ bit) for i in range(size)])  8.72 us
    pallas_call x1, Pallas kernels, pick(): pl.pallas_call(functools.partial(pick_kernel, cap), in_specs=[VMEM, ANY],...  4.85 us
    ppermute x3, starting transfers between devices, finish(): lax.ppermute(owned, 'freq', [(i, i ^ k) for i in range(nfreq)])  4.45 us
    pallas_call x1, Pallas kernels, tables(): pl.pallas_call(functools.partial(tables_kernel, nchan), in_specs=[ANY, AN...  3.82 us
    ppermute x3, waiting for transfers between devices, finish(): lax.ppermute(owned, 'freq', [(i, i ^ k) for i in range(nfreq)])  2.63 us
    pallas_call x1, Pallas kernels, place_early(): pl.pallas_call(functools.partial(early_kernel, cap, names, per_chip), in_...  1.35 us
  transfers between devices with their start and end apart: 16, of which 9 were waited for; matrix products, arithmetic and copies ran while one was open for 3% of the time, Pallas kernels for 10%

profile of v4, /device:TPU:0, one launch (start us, length us, event | category | flops | bytes accessed | tf_op | source)
XLA Modules:
  0.0 52.0 jit_solution(17718802096530038484)
XLA Ops:
  0.0 0.0 copy-start
  0.0 0.0 copy-start.3
  0.0 4.8 %pick_sources.3 = (bf16[6,128,256]{2,1,0:T(8,128)(2,1)S(1)}, bf16[6,128,256]{2,1,0:T(8,128)(2,1)S(1)}) custom-call(s32[2,32]{1,0:T(2,128)} %refs_0_.1, bf16[2,30,256,128]{3,2,1,0:T(8,128)(2,1)} %spec_ref.3), custom_call_target="tpu_custom_call" | custom-call | tf_op jit(solution)/shard_map/pick_sources/pallas_call | solution.py:146
  4.9 0.5 %collective-permute-start.16 = (bf16[6,128,256]{2,1,0:T(8,128)(2,1)S(1)}, bf16[6,128,256]{2,1,0:T(8,128)(2,1)S(1)}, u32[]{:S(2)}, u32[]{:S(2)}) collective-permute-start(bf16[6,128,256]{2,1,0:T(8,128)(2,1)S(1)} %get-tuple-element.93), channel_id=1, source_target_pairs={{0,4},{4,0},{8,12},{12,8},{16,20},{20,16},{24,28},{28,24},{1,5},{5... | collective-permute-start | bytes 1179656 | tf_op jit(solution)/shard_map/ppermute | solution.py:397
  5.4 1.3 %collective-permute-done.16 = bf16[6,128,256]{2,1,0:T(8,128)(2,1)S(1)} collective-permute-done((bf16[6,128,256]{2,1,0:T(8,128)(2,1)S(1)}, bf16[6,128,256]{2,1,0:T(8,128)(2,1)S(1)}, u32[]{:S(2)}, u32[]{:S(2)}) %collective-permute-start.16) | collective-permute-done | bytes 393248 | tf_op jit(solution)/shard_map/ppermute | solution.py:397
  6.8 0.4 collective-permute-start.17
  7.2 0.0 copy-done
  7.2 0.1 collective-permute-start.15
  7.4 2.9 %collective-permute-start.18 = (bf16[6,64,256]{2,1,0:T(8,128)(2,1)S(1)}, bf16[6,64,256]{2,1,0:T(8,128)(2,1)S(1)}, u32[]{:S(2)}, u32[]{:S(2)}) collective-permute-start(bf16[6,64,256]{2,1,0:T(8,128)(2,1)S(1)} %get-tuple-element.101.refs_0_), channel_id=1, source_target_pairs={{0,8},{4,12},{8,0},{12,4},{16,24},{20,28},{24,16},{28,20},{1,9},{5... | collective-permute-start | bytes 589832 | tf_op jit(solution)/shard_map/ppermute | solution.py:397
  10.2 1.5 %collective-permute-start.21 = (bf16[6,64,256]{2,1,0:T(8,128)(2,1)S(1)}, bf16[6,64,256]{2,1,0:T(8,128)(2,1)S(1)}, u32[]{:S(2)}, u32[]{:S(2)}) collective-permute-start(bf16[6,64,256]{2,1,0:T(8,128)(2,1)S(1)} %get-tuple-element.104.refs_3_), channel_id=1, source_target_pairs={{0,16},{4,20},{8,24},{12,28},{16,0},{20,4},{24,8},{28,12},{1,17},{... | collective-permute-start | bytes 589832 | tf_op jit(solution)/shard_map/ppermute | solution.py:397
  11.7 0.5 collective-permute-start.19
  12.2 0.0 collective-permute-done.15.got_pairs
  12.3 2.2 %collective-permute-start.20 = (bf16[6,64,256]{2,1,0:T(8,128)(2,1)S(1)}, bf16[6,64,256]{2,1,0:T(8,128)(2,1)S(1)}, u32[]{:S(2)}, u32[]{:S(2)}) collective-permute-start(bf16[6,64,256]{2,1,0:T(8,128)(2,1)S(1)} %get-tuple-element.104.refs_3_), channel_id=1, source_target_pairs={{0,8},{4,12},{8,0},{12,4},{16,24},{20,28},{24,16},{28,20},{1,9},{5... | collective-permute-start | bytes 589832 | tf_op jit(solution)/shard_map/ppermute | solution.py:397
  14.5 0.9 %collective-permute-done.18.refs_1_ = bf16[6,64,256]{2,1,0:T(8,128)(2,1)S(1)} collective-permute-done((bf16[6,64,256]{2,1,0:T(8,128)(2,1)S(1)}, bf16[6,64,256]{2,1,0:T(8,128)(2,1)S(1)}, u32[]{:S(2)}, u32[]{:S(2)}) %collective-permute-start.18) | collective-permute-done | bytes 196640 | tf_op jit(solution)/shard_map/ppermute | solution.py:397
  15.4 1.8 %collective-permute-start.22 = (bf16[6,64,256]{2,1,0:T(8,128)(2,1)S(1)}, bf16[6,64,256]{2,1,0:T(8,128)(2,1)S(1)}, u32[]{:S(2)}, u32[]{:S(2)}) collective-permute-start(bf16[6,64,256]{2,1,0:T(8,128)(2,1)S(1)} %collective-permute-done.18.refs_1_), channel_id=1, source_target_pairs={{0,16},{4,20},{8,24},{12,28},{16,0},{20,4},{24,8},{28,12},{1,17},{... | collective-permute-start | bytes 589832 | tf_op jit(solution)/shard_map/ppermute | solution.py:397
  17.2 0.8 %collective-permute-done.21.refs_5_ = bf16[6,64,256]{2,1,0:T(8,128)(2,1)S(1)} collective-permute-done((bf16[6,64,256]{2,1,0:T(8,128)(2,1)S(1)}, bf16[6,64,256]{2,1,0:T(8,128)(2,1)S(1)}, u32[]{:S(2)}, u32[]{:S(2)}) %collective-permute-start.21) | collective-permute-done | bytes 196640 | tf_op jit(solution)/shard_map/ppermute | solution.py:397
  18.0 0.7 %collective-permute-start.23 = (bf16[6,64,256]{2,1,0:T(8,128)(2,1)S(1)}, bf16[6,64,256]{2,1,0:T(8,128)(2,1)S(1)}, u32[]{:S(2)}, u32[]{:S(2)}) collective-permute-start(bf16[6,64,256]{2,1,0:T(8,128)(2,1)S(1)} %collective-permute-done.21.refs_5_), channel_id=1, source_target_pairs={{0,8},{4,12},{8,0},{12,4},{16,24},{20,28},{24,16},{28,20},{1,9},{5... | collective-permute-start | bytes 589832 | tf_op jit(solution)/shard_map/ppermute | solution.py:397
  18.7 0.6 %negate_multiply_fusion.1 = (f32[128,256]{1,0:T(8,128)S(1)}, f32[128,256]{1,0:T(8,128)S(1)}) fusion(s32[256]{0:T(256)S(1)} %iota_add_fusion.2, s32[128]{0:T(128)S(1)} %iota_add_fusion.3), kind=kLoop, calls=%fused_computation.37 | loop fusion | flops 557056 | bytes 263680 | tf_op jit(solution)/shard_map/mul | solution.py:38
  19.3 0.0 collective-permute-done.17.got_ref
  19.3 0.0 copy-done.3
  19.3 0.0 copy-start.1
  19.3 3.8 %tables.3 = (bf16[128,64,256]{2,1,0:T(8,128)(2,1)S(1)}, bf16[64,256,256]{2,1,0:T(8,128)(2,1)S(1)}, f32[8,256]{1,0:T(8,128)S(1)}) custom-call(bf16[2,30,256,128]{3,2,1,0:T(8,128)(2,1)} %spec_ref.3, bf16[2,30,256,128]{3,2,1,0:T(8,128)(2,1)} %collective-permute-done.17.got_ref, s32[64,128]{1,0:T(8,128)S(1)} %bitcast.32, ...), custom_call_target="tpu_custom_call" | custom-call | tf_op jit(solution)/shard_map/tables/pallas_call | solution.py:253
  23.1 0.0 collective-permute-done.19.refs_2_
  23.1 0.0 collective-permute-done.20.refs_4_
  23.2 0.0 copy-done.1
  23.2 1.3 %place_early.3.refs_6_ = f32[4232,128]{1,0:T(8,128)S(1)} custom-call(s32[2,32]{1,0:T(2,128)S(1)} %copy-done.1, bf16[6,64,256]{2,1,0:T(8,128)(2,1)S(1)} %get-tuple-element.101.refs_0_, bf16[6,64,256]{2,1,0:T(8,128)(2,1)S(1)} %collective-permute-done.18.refs_1_, bf16[6,64,256]{2,1,0:T(8,128)(2,1)S(1)} %collective-permute-done.19.refs_2_, ...), custom_call_target="tpu_custom_call" | custom-call | tf_op jit(solution)/shard_map/place_early/pallas_call | solution.py:282
  24.5 0.8 %collective-permute-done.22.refs_7_ = bf16[6,64,256]{2,1,0:T(8,128)(2,1)S(1)} collective-permute-done((bf16[6,64,256]{2,1,0:T(8,128)(2,1)S(1)}, bf16[6,64,256]{2,1,0:T(8,128)(2,1)S(1)}, u32[]{:S(2)}, u32[]{:S(2)}) %collective-permute-start.22) | collective-permute-done | bytes 196640 | tf_op jit(solution)/shard_map/ppermute | solution.py:397
  25.3 0.0 collective-permute-done.23.refs_8_
  25.3 8.8 %cross_and_bin.3 = (f32[4,40,256]{2,1,0:T(8,128)S(1)}, f32[4,40,256]{2,1,0:T(8,128)S(1)}) custom-call(s32[2,32]{1,0:T(2,128)S(1)} %copy-done.1, bf16[128,64,256]{2,1,0:T(8,128)(2,1)S(1)} %get-tuple-element.97.refs_1_, bf16[64,256,256]{2,1,0:T(8,128)(2,1)S(1)} %get-tuple-element.98.refs_2_, f32[128,256]{1,0:T(8,128)S(1)} %get-tuple-element.123.refs_3_, ...), custom_call_target="tpu_custom_call" | custom-call | tf_op jit(solution)/shard_map/cross_and_bin/pallas_call | solution.py:385
  34.1 0.1 collective-permute-start.24
  34.2 1.4 %collective-permute-done.24 = f32[4,40,256]{2,1,0:T(8,128)S(1)} collective-permute-done((f32[4,40,256]{2,1,0:T(8,128)S(1)}, f32[4,40,256]{2,1,0:T(8,128)S(1)}, u32[]{:S(2)}, u32[]{:S(2)}) %collective-permute-start.24) | collective-permute-done | bytes 163872 | tf_op jit(solution)/shard_map/ppermute | solution.py:397
  35.6 0.7 %collective-permute-start.25 = (f32[40,256]{1,0:T(8,128)S(1)}, f32[40,256]{1,0:T(8,128)S(1)}, u32[]{:S(2)}, u32[]{:S(2)}) collective-permute-start(f32[40,256]{1,0:T(8,128)S(1)} %get-tuple-element.119), channel_id=1, source_target_pairs={{0,8},{4,12},{8,0},{12,4},{16,24},{20,28},{24,16},{28,20},{1,9},{5... | collective-permute-start | bytes 122888 | tf_op jit(solution)/shard_map/ppermute | solution.py:397
  36.3 1.5 %collective-permute-start.26 = (f32[40,256]{1,0:T(8,128)S(1)}, f32[40,256]{1,0:T(8,128)S(1)}, u32[]{:S(2)}, u32[]{:S(2)}) collective-permute-start(f32[40,256]{1,0:T(8,128)S(1)} %get-tuple-element.121), channel_id=1, source_target_pairs={{0,16},{4,20},{8,24},{12,28},{16,0},{20,4},{24,8},{28,12},{1,17},{... | collective-permute-start | bytes 122888 | tf_op jit(solution)/shard_map/ppermute | solution.py:397
  37.8 1.4 %collective-permute-start.27 = (f32[40,256]{1,0:T(8,128)S(1)}, f32[40,256]{1,0:T(8,128)S(1)}, u32[]{:S(2)}, u32[]{:S(2)}) collective-permute-start(f32[40,256]{1,0:T(8,128)S(1)} %get-tuple-element.120), channel_id=1, source_target_pairs={{0,24},{4,28},{8,16},{12,20},{16,8},{20,12},{24,0},{28,4},{1,25},{... | collective-permute-start | bytes 122888 | tf_op jit(solution)/shard_map/ppermute | solution.py:397
  39.2 0.5 collective-permute-done.25
  39.7 0.6 %collective-permute-done.26 = f32[40,256]{1,0:T(8,128)S(1)} collective-permute-done((f32[40,256]{1,0:T(8,128)S(1)}, f32[40,256]{1,0:T(8,128)S(1)}, u32[]{:S(2)}, u32[]{:S(2)}) %collective-permute-start.26) | collective-permute-done | bytes 40992 | tf_op jit(solution)/shard_map/ppermute | solution.py:397
  40.3 2.4 %collective-permute-done.27 = f32[40,256]{1,0:T(8,128)S(1)} collective-permute-done((f32[40,256]{1,0:T(8,128)S(1)}, f32[40,256]{1,0:T(8,128)S(1)}, u32[]{:S(2)}, u32[]{:S(2)}) %collective-permute-start.27) | collective-permute-done | bytes 40992 | tf_op jit(solution)/shard_map/ppermute | solution.py:397
  42.7 3.7 %collective-permute-start.28 = (f32[32,256]{1,0:T(8,128)S(1)}, f32[32,256]{1,0:T(8,128)S(1)}, u32[]{:S(2)}, u32[]{:S(2)}) collective-permute-start(f32[32,256]{1,0:T(8,128)S(1)} %slice.55), channel_id=1, source_target_pairs={{0,3},{1,2},{2,1},{3,0},{4,7},{5,6},{6,5},{7,4},{8,11},{9,10},{10,... | collective-permute-start | bytes 98312 | tf_op jit(solution)/shard_map/ppermute | solution.py:462
  46.4 0.0 collective-permute-start.29
  46.4 0.8 %collective-permute-start.30 = (f32[32,256]{1,0:T(8,128)S(1)}, f32[32,256]{1,0:T(8,128)S(1)}, u32[]{:S(2)}, u32[]{:S(2)}) collective-permute-start(f32[32,256]{1,0:T(8,128)S(1)} %slice.55), channel_id=1, source_target_pairs={{0,1},{1,0},{2,3},{3,2},{4,5},{5,4},{6,7},{7,6},{8,9},{9,8},{10,11... | collective-permute-start | bytes 98312 | tf_op jit(solution)/shard_map/ppermute | solution.py:462
  47.2 0.1 convert_reduce_fusion
  47.3 0.6 %reduce_max.9 = s32[]{:T(128)} reduce(s32[4]{0:T(128)S(1)} %convert_reduce_fusion, s32[]{:T(128)} %constant.140.clone.1), dimensions={0}, to_apply=%region_1.2 | reduce | flops 3 | bytes 24 | tf_op jit(solution)/shard_map/reduce_max | solution.py:488
  48.6 0.0 collective-permute-done.28
  48.6 2.6 %collective-permute-done.29 = f32[32,256]{1,0:T(8,128)S(1)} collective-permute-done((f32[32,256]{1,0:T(8,128)S(1)}, f32[32,256]{1,0:T(8,128)S(1)}, u32[]{:S(2)}, u32[]{:S(2)}) %collective-permute-start.29) | collective-permute-done | bytes 32800 | tf_op jit(solution)/shard_map/ppermute | solution.py:462
  51.2 0.0 collective-permute-done.30
  51.2 0.2 conditional.1
  51.2 0.1 sqrt_bitcast_fusion
  51.3 0.1 add_divide_fusion.1
  51.4 0.0 copy-start.2
  51.4 0.6 %copy-done.2 = f32[32,256]{1,0:T(8,128)} copy-done((f32[32,256]{1,0:T(8,128)}, f32[32,256]{1,0:T(8,128)S(1)}, u32[]{:S(2)}) %copy-start.2) | copy-done | bytes 32792
  (10 shorter events, 0.1 us)
Async XLA Ops:
  0.0 7.2 %copy-start = (s32[2,32,128]{2,1,0:T(8,128)S(1)}, s32[2,32,128]{2,1,0:T(8,128)}, u32[]{:S(2)}) copy-start(s32[2,32,128]{2,1,0:T(8,128)} %param.8) | copy-start | bytes 98308
  0.0 19.3 %copy-start.3 = (s32[256]{0:T(256)S(1)}, s32[256]{0:T(256)}, u32[]{:S(2)}) copy-start(s32[256]{0:T(256)} %param.9) | copy-start | bytes 3076
  4.9 1.9 %collective-permute-start.16 = (bf16[6,128,256]{2,1,0:T(8,128)(2,1)S(1)}, bf16[6,128,256]{2,1,0:T(8,128)(2,1)S(1)}, u32[]{:S(2)}, u32[]{:S(2)}) collective-permute-start(bf16[6,128,256]{2,1,0:T(8,128)(2,1)S(1)} %get-tuple-element.93), channel_id=1, source_target_pairs={{0,4},{4,0},{8,12},{12,8},{16,20},{20,16},{24,28},{28,24},{1,5},{5... | collective-permute-start | bytes 1179656 | tf_op jit(solution)/shard_map/ppermute | solution.py:397
  6.8 12.5 %collective-permute-start.17 = (bf16[2,30,256,128]{3,2,1,0:T(8,128)(2,1)}, bf16[2,30,256,128]{3,2,1,0:T(8,128)(2,1)}, u32[]{:S(2)}, u32[]{:S(2)}) collective-permute-start(bf16[2,30,256,128]{3,2,1,0:T(8,128)(2,1)} %spec_ref.3), channel_id=1, source_target_pairs={{0,4},{4,0},{8,12},{12,8},{16,20},{20,16},{24,28},{28,24},{1,5},{5... | collective-permute-start | bytes 11796488 | tf_op jit(solution)/shard_map/ppermute | solution.py:397
  7.2 5.0 %collective-permute-start.15 = (s32[64,128]{1,0:T(8,128)S(1)}, s32[64,128]{1,0:T(8,128)S(1)}, u32[]{:S(2)}, u32[]{:S(2)}) collective-permute-start(s32[64,128]{1,0:T(8,128)S(1)} %bitcast.31), channel_id=1, source_target_pairs={{0,4},{4,0},{8,12},{12,8},{16,20},{20,16},{24,28},{28,24},{1,5},{5... | collective-permute-start | bytes 98312 | tf_op jit(solution)/shard_map/ppermute | solution.py:397
  7.4 8.1 %collective-permute-start.18 = (bf16[6,64,256]{2,1,0:T(8,128)(2,1)S(1)}, bf16[6,64,256]{2,1,0:T(8,128)(2,1)S(1)}, u32[]{:S(2)}, u32[]{:S(2)}) collective-permute-start(bf16[6,64,256]{2,1,0:T(8,128)(2,1)S(1)} %get-tuple-element.101.refs_0_), channel_id=1, source_target_pairs={{0,8},{4,12},{8,0},{12,4},{16,24},{20,28},{24,16},{28,20},{1,9},{5... | collective-permute-start | bytes 589832 | tf_op jit(solution)/shard_map/ppermute | solution.py:397
  10.2 7.8 %collective-permute-start.21 = (bf16[6,64,256]{2,1,0:T(8,128)(2,1)S(1)}, bf16[6,64,256]{2,1,0:T(8,128)(2,1)S(1)}, u32[]{:S(2)}, u32[]{:S(2)}) collective-permute-start(bf16[6,64,256]{2,1,0:T(8,128)(2,1)S(1)} %get-tuple-element.104.refs_3_), channel_id=1, source_target_pairs={{0,16},{4,20},{8,24},{12,28},{16,0},{20,4},{24,8},{28,12},{1,17},{... | collective-permute-start | bytes 589832 | tf_op jit(solution)/shard_map/ppermute | solution.py:397
  11.7 11.4 %collective-permute-start.19 = (bf16[6,64,256]{2,1,0:T(8,128)(2,1)S(1)}, bf16[6,64,256]{2,1,0:T(8,128)(2,1)S(1)}, u32[]{:S(2)}, u32[]{:S(2)}) collective-permute-start(bf16[6,64,256]{2,1,0:T(8,128)(2,1)S(1)} %get-tuple-element.101.refs_0_), channel_id=1, source_target_pairs={{0,16},{4,20},{8,24},{12,28},{16,0},{20,4},{24,8},{28,12},{1,17},{... | collective-permute-start | bytes 589832 | tf_op jit(solution)/shard_map/ppermute | solution.py:397
  12.3 10.9 %collective-permute-start.20 = (bf16[6,64,256]{2,1,0:T(8,128)(2,1)S(1)}, bf16[6,64,256]{2,1,0:T(8,128)(2,1)S(1)}, u32[]{:S(2)}, u32[]{:S(2)}) collective-permute-start(bf16[6,64,256]{2,1,0:T(8,128)(2,1)S(1)} %get-tuple-element.104.refs_3_), channel_id=1, source_target_pairs={{0,8},{4,12},{8,0},{12,4},{16,24},{20,28},{24,16},{28,20},{1,9},{5... | collective-permute-start | bytes 589832 | tf_op jit(solution)/shard_map/ppermute | solution.py:397
  15.4 9.9 %collective-permute-start.22 = (bf16[6,64,256]{2,1,0:T(8,128)(2,1)S(1)}, bf16[6,64,256]{2,1,0:T(8,128)(2,1)S(1)}, u32[]{:S(2)}, u32[]{:S(2)}) collective-permute-start(bf16[6,64,256]{2,1,0:T(8,128)(2,1)S(1)} %collective-permute-done.18.refs_1_), channel_id=1, source_target_pairs={{0,16},{4,20},{8,24},{12,28},{16,0},{20,4},{24,8},{28,12},{1,17},{... | collective-permute-start | bytes 589832 | tf_op jit(solution)/shard_map/ppermute | solution.py:397
  18.0 7.3 %collective-permute-start.23 = (bf16[6,64,256]{2,1,0:T(8,128)(2,1)S(1)}, bf16[6,64,256]{2,1,0:T(8,128)(2,1)S(1)}, u32[]{:S(2)}, u32[]{:S(2)}) collective-permute-start(bf16[6,64,256]{2,1,0:T(8,128)(2,1)S(1)} %collective-permute-done.21.refs_5_), channel_id=1, source_target_pairs={{0,8},{4,12},{8,0},{12,4},{16,24},{20,28},{24,16},{28,20},{1,9},{5... | collective-permute-start | bytes 589832 | tf_op jit(solution)/shard_map/ppermute | solution.py:397
  19.3 3.9 %copy-start.1 = (s32[2,32]{1,0:T(2,128)S(1)}, s32[2,32]{1,0:T(2,128)}, u32[]{:S(2)}) copy-start(s32[2,32]{1,0:T(2,128)} %refs_0_.1) | copy-start | bytes 772
  34.1 1.5 %collective-permute-start.24 = (f32[4,40,256]{2,1,0:T(8,128)S(1)}, f32[4,40,256]{2,1,0:T(8,128)S(1)}, u32[]{:S(2)}, u32[]{:S(2)}) collective-permute-start(f32[4,40,256]{2,1,0:T(8,128)S(1)} %get-tuple-element.108), channel_id=1, source_target_pairs={{0,4},{4,0},{8,12},{12,8},{16,20},{20,16},{24,28},{28,24},{1,5},{5... | collective-permute-start | bytes 491528 | tf_op jit(solution)/shard_map/ppermute | solution.py:397
  35.6 4.1 %collective-permute-start.25 = (f32[40,256]{1,0:T(8,128)S(1)}, f32[40,256]{1,0:T(8,128)S(1)}, u32[]{:S(2)}, u32[]{:S(2)}) collective-permute-start(f32[40,256]{1,0:T(8,128)S(1)} %get-tuple-element.119), channel_id=1, source_target_pairs={{0,8},{4,12},{8,0},{12,4},{16,24},{20,28},{24,16},{28,20},{1,9},{5... | collective-permute-start | bytes 122888 | tf_op jit(solution)/shard_map/ppermute | solution.py:397
  36.3 4.0 %collective-permute-start.26 = (f32[40,256]{1,0:T(8,128)S(1)}, f32[40,256]{1,0:T(8,128)S(1)}, u32[]{:S(2)}, u32[]{:S(2)}) collective-permute-start(f32[40,256]{1,0:T(8,128)S(1)} %get-tuple-element.121), channel_id=1, source_target_pairs={{0,16},{4,20},{8,24},{12,28},{16,0},{20,4},{24,8},{28,12},{1,17},{... | collective-permute-start | bytes 122888 | tf_op jit(solution)/shard_map/ppermute | solution.py:397
  37.8 4.9 %collective-permute-start.27 = (f32[40,256]{1,0:T(8,128)S(1)}, f32[40,256]{1,0:T(8,128)S(1)}, u32[]{:S(2)}, u32[]{:S(2)}) collective-permute-start(f32[40,256]{1,0:T(8,128)S(1)} %get-tuple-element.120), channel_id=1, source_target_pairs={{0,24},{4,28},{8,16},{12,20},{16,8},{20,12},{24,0},{28,4},{1,25},{... | collective-permute-start | bytes 122888 | tf_op jit(solution)/shard_map/ppermute | solution.py:397
  42.7 5.9 %collective-permute-start.28 = (f32[32,256]{1,0:T(8,128)S(1)}, f32[32,256]{1,0:T(8,128)S(1)}, u32[]{:S(2)}, u32[]{:S(2)}) collective-permute-start(f32[32,256]{1,0:T(8,128)S(1)} %slice.55), channel_id=1, source_target_pairs={{0,3},{1,2},{2,1},{3,0},{4,7},{5,6},{6,5},{7,4},{8,11},{9,10},{10,... | collective-permute-start | bytes 98312 | tf_op jit(solution)/shard_map/ppermute | solution.py:462
  46.4 4.8 %collective-permute-start.29 = (f32[32,256]{1,0:T(8,128)S(1)}, f32[32,256]{1,0:T(8,128)S(1)}, u32[]{:S(2)}, u32[]{:S(2)}) collective-permute-start(f32[32,256]{1,0:T(8,128)S(1)} %slice.55), channel_id=1, source_target_pairs={{0,2},{1,3},{2,0},{3,1},{4,6},{5,7},{6,4},{7,5},{8,10},{9,11},{10,... | collective-permute-start | bytes 98312 | tf_op jit(solution)/shard_map/ppermute | solution.py:462
  46.4 4.8 %collective-permute-start.30 = (f32[32,256]{1,0:T(8,128)S(1)}, f32[32,256]{1,0:T(8,128)S(1)}, u32[]{:S(2)}, u32[]{:S(2)}) collective-permute-start(f32[32,256]{1,0:T(8,128)S(1)} %slice.55), channel_id=1, source_target_pairs={{0,1},{1,0},{2,3},{3,2},{4,5},{5,4},{6,7},{7,6},{8,9},{9,8},{10,11... | collective-permute-start | bytes 98312 | tf_op jit(solution)/shard_map/ppermute | solution.py:462
  51.4 0.6 %copy-start.2 = (f32[32,256]{1,0:T(8,128)}, f32[32,256]{1,0:T(8,128)S(1)}, u32[]{:S(2)}) copy-start(f32[32,256]{1,0:T(8,128)S(1)} %get-tuple-element.180) | copy-start | bytes 98308

commit v5 on v4

--- a/solution.py
+++ b/solution.py
@@ -18,7 +18,7 @@
 LANES = 128
 SLACK = 6 * 1024 * 1024
 PITCH = LANES + 9
-TURN = 16
+TURN = 32
 BIG = 8 * 1024 * 1024
 CAP = 25
 PACK = 2 * LANES
@@ -126,7 +126,12 @@
                 copy.wait()
             lefts.append(jnp.concatenate([buf[k, b * wg + i] for i in range(wg) for k in range(2)], axis=1))
         left = jnp.concatenate(lefts, axis=0)
-        got = jnp.dot(left, picker, preferred_element_type=F32).astype(BF)
+        got = []
+        for h in range(PACK // LANES):
+            first, last = h * LANES // cap * chans, min(-(-(h + 1) * LANES // cap), 2 * wg) * chans
+            part = picker[first:last, h * LANES : (h + 1) * LANES]
+            got.append(jnp.dot(left[:, first:last], part, preferred_element_type=F32))
+        got = jnp.concatenate(got, axis=1).astype(BF)
         for b in range(b0, b0 + turn):
             res[b] = got[(b - b0) * freqs : (b - b0 + 1) * freqs]
         for n, (start, ref) in enumerate(((other, send_ref), (mine, keep_ref))):
@@ -159,11 +164,8 @@
     )(src_ids, spectra)
 
 
-def place_sources(cap, names, src_ref, per_chip, xrefs, xs):
-    chips = len(names)
-    groups, part, _ = xrefs[0].shape
+def placement(cap, names, src_ref, per_chip):
     wg = PACK // (2 * cap)
-    wp = groups * wg // 2
     me = lax.axis_index("chan")
     row = source_row(src_ref)
     slots = row.shape[1]
@@ -174,7 +176,14 @@
     wide = 2 * wg * slots
     aligned = (lane_g == shift(iota((1, wide), 1), slots)) & (lane_r == rank_row)
     place = [jnp.where(aligned & (own_row == (shift(me, 2) ^ d)), 1.0, 0.0).astype(BF) for d in names]
-    place = jnp.concatenate(place, axis=0)
+    return jnp.concatenate(place, axis=0)
+
+
+def place_sources(place, xrefs, xs):
+    groups, part, _ = xrefs[0].shape
+    chips = place.shape[0] // PACK
+    wg = place.shape[1] // LANES
+    wp = groups * wg // 2
     for p in range(len(xrefs) // chips):
         got = jnp.concatenate([xrefs[p * chips + n][...] for n in range(chips)], axis=2)
         got = jnp.dot(got.reshape(groups * part, chips * PACK), place, preferred_element_type=F32)
@@ -271,33 +280,37 @@
     )(spectra, got, own_pairs, got_pairs, slot_of_bin[None, :])
 
 
-def early_kernel(cap, names, per_chip, src_ref, *refs):
-    place_sources(cap, names, src_ref, per_chip, refs[:-1], refs[-1])
-
-
-def place_early(arrays, names, src_ids, cap, per_chip):
+def early_kernel(cap, names, late, per_chip, src_ref, *refs):
+    *xrefs, xs_ref, late_ref = refs
+    place_sources(placement(cap, names, src_ref, per_chip), xrefs, xs_ref)
+    late_ref[...] = placement(cap, late, src_ref, per_chip)
+
+
+def place_early(arrays, names, late, src_ids, cap, per_chip):
     groups, part, _ = arrays[0].shape
     count = len(arrays) // len(names) * part
     shape = (count * XPITCH + 8, LANES)
     return pl.pallas_call(
-        functools.partial(early_kernel, cap, names, per_chip),
+        functools.partial(early_kernel, cap, names, late, per_chip),
         in_specs=[VMEM] * (1 + len(arrays)),
-        out_specs=VMEM,
-        out_shape=jax.ShapeDtypeStruct(shape, F32),
+        out_specs=[VMEM, VMEM],
+        out_shape=[
+            jax.ShapeDtypeStruct(shape, F32),
+            jax.ShapeDtypeStruct((len(late) * PACK, PACK // (2 * cap) * LANES), BF),
+        ],
         compiler_params=params(*staging(arrays, names)),
         name="place_early",
     )(src_ids, *arrays)
 
 
-def cross_kernel(cap, names, pieces, *refs):
-    src_ref, recv, hot, cos_ref, sin_ref, count_ref, xs_early = refs[:7]
-    xrefs = refs[7 : 7 + pieces * len(names)]
-    refs = refs[7 + pieces * len(names) :]
+def cross_kernel(inputs, *refs):
+    place_ref, recv, hot, cos_ref, sin_ref, count_ref, xs_early = refs[:7]
+    xrefs, refs = refs[7 : 7 + inputs], refs[7 + inputs :]
     outs, refs = refs[:2], refs[2:]
     xs, cross, sums, whole = refs
     count, _, chans2 = recv.shape
     slots, bins, _ = hot.shape
-    place_sources(cap, names, src_ref, chans2, xrefs, xs)
+    place_sources(place_ref[...], xrefs, xs)
     imag = iota((2 * WROWS, LANES), 1) >= slots
     quarter = shift(iota((1, 4 * 4 * WROWS), 1), 4 * WROWS)
     masks = [jnp.where(quarter == i, 1.0, 0.0).astype(BF) for i in range(4)]
@@ -308,12 +321,12 @@
             lefts = []
             for j in range(4 * q, 4 * q + 4):
                 at = pl.ds((g * 8 + j) * XPITCH, 2 * WROWS)
-                x = xs_early[at, :] + xs[at, :]
+                x = (xs_early[at, :] + xs[at, :]).astype(BF)
                 upper = jnp.where(imag, -x, x)
                 if j:
                     upper = pltpu.roll(upper, j, 1)
                 lefts += [upper, pltpu.roll(x, slots + j, 1)]
-            left = jnp.transpose(jnp.concatenate(lefts, axis=0)).astype(BF)
+            left = jnp.transpose(jnp.concatenate(lefts, axis=0))
             left = jnp.concatenate([left * mask for mask in masks], axis=0)
             right = recv[pl.ds(g * 8 + 4 * q, 4)].reshape(4 * 4 * WROWS, chans2)
             got = jnp.dot(left, right, preferred_element_type=F32)
@@ -369,7 +382,7 @@
     return [((groups * part, 4 * PACK), F32), ((groups * part, chips * PACK), BF), ((chips * PACK, 4 * PACK), F32)]
 
 
-def cross_and_bin(arrays, names, xs_early, src_ids, recv, hot, counts, cos, sin, cap, nchan):
+def cross_and_bin(arrays, names, xs_early, place, recv, hot, counts, cos, sin, nchan):
     _, bins, chans2 = hot.shape
     lags = cos.shape[1]
     count = recv.shape[0]
@@ -383,14 +396,14 @@
     ]
     buffers = scratch + staging(arrays, names)
     return pl.pallas_call(
-        functools.partial(cross_kernel, cap, names, len(arrays) // len(names)),
+        functools.partial(cross_kernel, len(arrays)),
         in_specs=[VMEM] * (7 + len(arrays)),
         out_specs=[VMEM, VMEM],
         out_shape=[out, out],
         scratch_shapes=[pltpu.VMEM(shape, kind) for shape, kind in scratch],
         compiler_params=params(*buffers, *([(hot.shape, BF)] if hot.size > BIG else [])),
         name="cross_and_bin",
-    )(src_ids, recv, hot, cos, sin, counts, xs_early, *arrays)
+    )(place, recv, hot, cos, sin, counts, xs_early, *arrays)
 
 
 def swap(x, size, bit):
@@ -435,11 +448,11 @@
     first = [held[d] for held in arrays for d in early]
     recv, hot, counts = tables(spectra, got_spec, pairs_own, got_pairs, slot_of_bin, nchan)
     counts, first = lax.optimization_barrier((counts, first))
-    xs_early = place_early(first, early, src_ids, cap, 2 * chans)
+    xs_early, place = place_early(first, early, late, src_ids, cap, 2 * chans)
     cos, sin = lag_basis(lax.axis_index("freq") * freqs + core * half, half, F, NLAG, windows)
     counts = counts[0].reshape(bins // NLAG, NLAG)
     last = [held[d] for held in arrays for d in late]
-    out = cross_and_bin(last, late, xs_early, src_ids, recv, hot, counts, cos, sin, cap, nchan)
+    out = cross_and_bin(last, late, xs_early, place, recv, hot, counts, cos, sin, nchan)
     mine, other = out
 
     per = bins // nchan
@@ -447,7 +460,7 @@
     at = me // 2
     if nchan // 2 <= 4:
         total = lax.dynamic_index_in_dim(mine, at, 0, keepdims=False)
-        for move in range(1, nchan // 2):
+        for move in range(nchan // 2 - 1, 0, -1):
             total = total + swap(lax.dynamic_index_in_dim(mine, at ^ move, 0, keepdims=False), nchan, 2 * move)
     else:
         for bit in rest[::-1]:

time: 52.2 us -> 50.1 us (0.960)
  Pallas kernels: 18.8 us -> 17.7 us
  waiting for transfers between devices: 11.3 us -> 10.4 us
    ppermute x13, waiting for transfers between devices: 8.72 us -> 7.75 us  [swap(): return lax.ppermute(x, 'chan', [(i, i ^ bit) for i in range(size)])]
    pallas_call x2, Pallas kernels: 10.1 us -> 9.4 us  [the longest x1 8.05 us: cross_and_bin(): pl.pallas_call(functools.partial(cross_kernel, len(arrays)), in_specs=[VM...]
where the time goes in v5:
time: 50.1 us; the launch traced here: 49.9 us
  starting transfers between devices  18.8 us (38%)
  Pallas kernels  17.7 us (35%)
  waiting for transfers between devices  10.4 us (21%)
  other arithmetic  1.6 us (3%)
  between operations  0.84 us (2%)
  local copies, waits for them, and re-layouts  0.66 us (1%)
    ppermute x13, starting transfers between devices, swap(): return lax.ppermute(x, 'chan', [(i, i ^ bit) for i in range(size)])  14.3 us
    pallas_call x1, Pallas kernels, cross_and_bin(): pl.pallas_call(functools.partial(cross_kernel, len(arrays)), in_specs=[VM...  8.05 us
    ppermute x13, waiting for transfers between devices, swap(): return lax.ppermute(x, 'chan', [(i, i ^ bit) for i in range(size)])  7.75 us
    ppermute x3, starting transfers between devices, finish(): lax.ppermute(owned, 'freq', [(i, i ^ k) for i in range(nfreq)])  4.45 us
    pallas_call x1, Pallas kernels, pick(): pl.pallas_call(functools.partial(pick_kernel, cap), in_specs=[VMEM, ANY],...  4.44 us
    pallas_call x1, Pallas kernels, tables(): pl.pallas_call(functools.partial(tables_kernel, nchan), in_specs=[ANY, AN...  3.82 us
    ppermute x3, waiting for transfers between devices, finish(): lax.ppermute(owned, 'freq', [(i, i ^ k) for i in range(nfreq)])  2.62 us
    pallas_call x1, Pallas kernels, place_early(): pl.pallas_call(functools.partial(early_kernel, cap, names, late, per_chip...  1.36 us
  transfers between devices with their start and end apart: 16, of which 9 were waited for; matrix products, arithmetic and copies ran while one was open for 3% of the time, Pallas kernels for 10%

profile of v5, /device:TPU:0, one launch (start us, length us, event | category | flops | bytes accessed | tf_op | source)
XLA Modules:
  0.0 49.9 jit_solution(14540492796339806118)
XLA Ops:
  0.0 0.0 copy-start
  0.0 0.0 copy-start.3
  0.0 4.4 %pick_sources.3 = (bf16[6,128,256]{2,1,0:T(8,128)(2,1)S(1)}, bf16[6,128,256]{2,1,0:T(8,128)(2,1)S(1)}) custom-call(s32[2,32]{1,0:T(2,128)} %src_ref.3, bf16[2,30,256,128]{3,2,1,0:T(8,128)(2,1)} %spec_ref.3), custom_call_target="tpu_custom_call" | custom-call | tf_op jit(solution)/shard_map/pick_sources/pallas_call | solution.py:151
  4.5 0.5 %collective-permute-start.16 = (bf16[6,128,256]{2,1,0:T(8,128)(2,1)S(1)}, bf16[6,128,256]{2,1,0:T(8,128)(2,1)S(1)}, u32[]{:S(2)}, u32[]{:S(2)}) collective-permute-start(bf16[6,128,256]{2,1,0:T(8,128)(2,1)S(1)} %get-tuple-element.97), channel_id=1, source_target_pairs={{0,4},{4,0},{8,12},{12,8},{16,20},{20,16},{24,28},{28,24},{1,5},{5... | collective-permute-start | bytes 1179656 | tf_op jit(solution)/shard_map/ppermute | solution.py:410
  5.0 1.3 %collective-permute-done.16 = bf16[6,128,256]{2,1,0:T(8,128)(2,1)S(1)} collective-permute-done((bf16[6,128,256]{2,1,0:T(8,128)(2,1)S(1)}, bf16[6,128,256]{2,1,0:T(8,128)(2,1)S(1)}, u32[]{:S(2)}, u32[]{:S(2)}) %collective-permute-start.16) | collective-permute-done | bytes 393248 | tf_op jit(solution)/shard_map/ppermute | solution.py:410
  6.4 0.4 collective-permute-start.17
  6.8 0.0 copy-done
  6.8 0.1 collective-permute-start.15
  6.9 2.9 %collective-permute-start.18 = (bf16[6,64,256]{2,1,0:T(8,128)(2,1)S(1)}, bf16[6,64,256]{2,1,0:T(8,128)(2,1)S(1)}, u32[]{:S(2)}, u32[]{:S(2)}) collective-permute-start(bf16[6,64,256]{2,1,0:T(8,128)(2,1)S(1)} %get-tuple-element.102.refs_0_), channel_id=1, source_target_pairs={{0,8},{4,12},{8,0},{12,4},{16,24},{20,28},{24,16},{28,20},{1,9},{5... | collective-permute-start | bytes 589832 | tf_op jit(solution)/shard_map/ppermute | solution.py:410
  9.8 1.5 %collective-permute-start.21 = (bf16[6,64,256]{2,1,0:T(8,128)(2,1)S(1)}, bf16[6,64,256]{2,1,0:T(8,128)(2,1)S(1)}, u32[]{:S(2)}, u32[]{:S(2)}) collective-permute-start(bf16[6,64,256]{2,1,0:T(8,128)(2,1)S(1)} %get-tuple-element.105.refs_3_), channel_id=1, source_target_pairs={{0,16},{4,20},{8,24},{12,28},{16,0},{20,4},{24,8},{28,12},{1,17},{... | collective-permute-start | bytes 589832 | tf_op jit(solution)/shard_map/ppermute | solution.py:410
  11.3 0.5 %collective-permute-start.19 = (bf16[6,64,256]{2,1,0:T(8,128)(2,1)S(1)}, bf16[6,64,256]{2,1,0:T(8,128)(2,1)S(1)}, u32[]{:S(2)}, u32[]{:S(2)}) collective-permute-start(bf16[6,64,256]{2,1,0:T(8,128)(2,1)S(1)} %get-tuple-element.102.refs_0_), channel_id=1, source_target_pairs={{0,16},{4,20},{8,24},{12,28},{16,0},{20,4},{24,8},{28,12},{1,17},{... | collective-permute-start | bytes 589832 | tf_op jit(solution)/shard_map/ppermute | solution.py:410
  11.8 0.0 collective-permute-done.15.got_pairs
  11.8 2.2 %collective-permute-start.20 = (bf16[6,64,256]{2,1,0:T(8,128)(2,1)S(1)}, bf16[6,64,256]{2,1,0:T(8,128)(2,1)S(1)}, u32[]{:S(2)}, u32[]{:S(2)}) collective-permute-start(bf16[6,64,256]{2,1,0:T(8,128)(2,1)S(1)} %get-tuple-element.105.refs_3_), channel_id=1, source_target_pairs={{0,8},{4,12},{8,0},{12,4},{16,24},{20,28},{24,16},{28,20},{1,9},{5... | collective-permute-start | bytes 589832 | tf_op jit(solution)/shard_map/ppermute | solution.py:410
  14.1 0.9 %collective-permute-done.18.refs_1_ = bf16[6,64,256]{2,1,0:T(8,128)(2,1)S(1)} collective-permute-done((bf16[6,64,256]{2,1,0:T(8,128)(2,1)S(1)}, bf16[6,64,256]{2,1,0:T(8,128)(2,1)S(1)}, u32[]{:S(2)}, u32[]{:S(2)}) %collective-permute-start.18) | collective-permute-done | bytes 196640 | tf_op jit(solution)/shard_map/ppermute | solution.py:410
  15.0 1.8 %collective-permute-start.22 = (bf16[6,64,256]{2,1,0:T(8,128)(2,1)S(1)}, bf16[6,64,256]{2,1,0:T(8,128)(2,1)S(1)}, u32[]{:S(2)}, u32[]{:S(2)}) collective-permute-start(bf16[6,64,256]{2,1,0:T(8,128)(2,1)S(1)} %collective-permute-done.18.refs_1_), channel_id=1, source_target_pairs={{0,16},{4,20},{8,24},{12,28},{16,0},{20,4},{24,8},{28,12},{1,17},{... | collective-permute-start | bytes 589832 | tf_op jit(solution)/shard_map/ppermute | solution.py:410
  16.8 0.8 %collective-permute-done.21.refs_5_ = bf16[6,64,256]{2,1,0:T(8,128)(2,1)S(1)} collective-permute-done((bf16[6,64,256]{2,1,0:T(8,128)(2,1)S(1)}, bf16[6,64,256]{2,1,0:T(8,128)(2,1)S(1)}, u32[]{:S(2)}, u32[]{:S(2)}) %collective-permute-start.21) | collective-permute-done | bytes 196640 | tf_op jit(solution)/shard_map/ppermute | solution.py:410
  17.6 0.7 %collective-permute-start.23 = (bf16[6,64,256]{2,1,0:T(8,128)(2,1)S(1)}, bf16[6,64,256]{2,1,0:T(8,128)(2,1)S(1)}, u32[]{:S(2)}, u32[]{:S(2)}) collective-permute-start(bf16[6,64,256]{2,1,0:T(8,128)(2,1)S(1)} %collective-permute-done.21.refs_5_), channel_id=1, source_target_pairs={{0,8},{4,12},{8,0},{12,4},{16,24},{20,28},{24,16},{28,20},{1,9},{5... | collective-permute-start | bytes 589832 | tf_op jit(solution)/shard_map/ppermute | solution.py:410
  18.3 0.6 %negate_multiply_fusion.1 = (f32[128,256]{1,0:T(8,128)S(1)}, f32[128,256]{1,0:T(8,128)S(1)}) fusion(s32[256]{0:T(256)S(1)} %iota_add_fusion.2, s32[128]{0:T(128)S(1)} %iota_add_fusion.3), kind=kLoop, calls=%fused_computation.37 | loop fusion | flops 557056 | bytes 263680 | tf_op jit(solution)/shard_map/mul | solution.py:38
  18.9 0.0 collective-permute-done.17.got_ref
  18.9 0.0 copy-done.3
  18.9 0.0 copy-start.2
  18.9 3.8 %tables.3 = (bf16[128,64,256]{2,1,0:T(8,128)(2,1)S(1)}, bf16[64,256,256]{2,1,0:T(8,128)(2,1)S(1)}, f32[8,256]{1,0:T(8,128)S(1)}) custom-call(bf16[2,30,256,128]{3,2,1,0:T(8,128)(2,1)} %spec_ref.3, bf16[2,30,256,128]{3,2,1,0:T(8,128)(2,1)} %collective-permute-done.17.got_ref, s32[64,128]{1,0:T(8,128)S(1)} %bitcast.32, ...), custom_call_target="tpu_custom_call" | custom-call | tf_op jit(solution)/shard_map/tables/pallas_call | solution.py:262
  22.7 0.0 collective-permute-done.19.refs_2_
  22.7 0.0 collective-permute-done.20.refs_4_
  22.8 0.0 copy-done.2
  22.8 1.4 %place_early.3 = (f32[4232,128]{1,0:T(8,128)S(1)}, bf16[256,640]{1,0:T(8,128)(2,1)S(1)}) custom-call(s32[2,32]{1,0:T(2,128)S(1)} %copy-done.2, bf16[6,64,256]{2,1,0:T(8,128)(2,1)S(1)} %get-tuple-element.102.refs_0_, bf16[6,64,256]{2,1,0:T(8,128)(2,1)S(1)} %collective-permute-done.18.refs_1_, bf16[6,64,256]{2,1,0:T(8,128)(2,1)S(1)} %collective-permute-done.19.refs_2_, ...), custom_call_target="tpu_custom_call" | custom-call | tf_op jit(solution)/shard_map/place_early/pallas_call | solution.py:293
  24.1 0.8 %collective-permute-done.22.refs_7_ = bf16[6,64,256]{2,1,0:T(8,128)(2,1)S(1)} collective-permute-done((bf16[6,64,256]{2,1,0:T(8,128)(2,1)S(1)}, bf16[6,64,256]{2,1,0:T(8,128)(2,1)S(1)}, u32[]{:S(2)}, u32[]{:S(2)}) %collective-permute-start.22) | collective-permute-done | bytes 196640 | tf_op jit(solution)/shard_map/ppermute | solution.py:410
  24.9 0.0 collective-permute-done.23.refs_8_
  24.9 8.0 %cross_and_bin.3 = (f32[4,40,256]{2,1,0:T(8,128)S(1)}, f32[4,40,256]{2,1,0:T(8,128)S(1)}) custom-call(bf16[256,640]{1,0:T(8,128)(2,1)S(1)} %get-tuple-element.108.refs_0_, bf16[128,64,256]{2,1,0:T(8,128)(2,1)S(1)} %get-tuple-element.109.refs_1_, bf16[64,256,256]{2,1,0:T(8,128)(2,1)S(1)} %get-tuple-element.110.refs_2_, ...), custom_call_target="tpu_custom_call" | custom-call | tf_op jit(solution)/shard_map/cross_and_bin/pallas_call | solution.py:398
  32.9 0.1 collective-permute-start.24
  33.1 1.4 %collective-permute-done.24 = f32[4,40,256]{2,1,0:T(8,128)S(1)} collective-permute-done((f32[4,40,256]{2,1,0:T(8,128)S(1)}, f32[4,40,256]{2,1,0:T(8,128)S(1)}, u32[]{:S(2)}, u32[]{:S(2)}) %collective-permute-start.24) | collective-permute-done | bytes 163872 | tf_op jit(solution)/shard_map/ppermute | solution.py:410
  34.5 1.6 %collective-permute-start.25 = (f32[40,256]{1,0:T(8,128)S(1)}, f32[40,256]{1,0:T(8,128)S(1)}, u32[]{:S(2)}, u32[]{:S(2)}) collective-permute-start(f32[40,256]{1,0:T(8,128)S(1)} %get-tuple-element.125), channel_id=1, source_target_pairs={{0,24},{4,28},{8,16},{12,20},{16,8},{20,12},{24,0},{28,4},{1,25},{... | collective-permute-start | bytes 122888 | tf_op jit(solution)/shard_map/ppermute | solution.py:410
  36.1 0.5 %collective-permute-start.26 = (f32[40,256]{1,0:T(8,128)S(1)}, f32[40,256]{1,0:T(8,128)S(1)}, u32[]{:S(2)}, u32[]{:S(2)}) collective-permute-start(f32[40,256]{1,0:T(8,128)S(1)} %get-tuple-element.127), channel_id=1, source_target_pairs={{0,16},{4,20},{8,24},{12,28},{16,0},{20,4},{24,8},{28,12},{1,17},{... | collective-permute-start | bytes 122888 | tf_op jit(solution)/shard_map/ppermute | solution.py:410
  36.6 1.4 %collective-permute-start.27 = (f32[40,256]{1,0:T(8,128)S(1)}, f32[40,256]{1,0:T(8,128)S(1)}, u32[]{:S(2)}, u32[]{:S(2)}) collective-permute-start(f32[40,256]{1,0:T(8,128)S(1)} %get-tuple-element.126), channel_id=1, source_target_pairs={{0,8},{4,12},{8,0},{12,4},{16,24},{20,28},{24,16},{28,20},{1,9},{5... | collective-permute-start | bytes 122888 | tf_op jit(solution)/shard_map/ppermute | solution.py:410
  38.0 1.4 %collective-permute-done.25 = f32[40,256]{1,0:T(8,128)S(1)} collective-permute-done((f32[40,256]{1,0:T(8,128)S(1)}, f32[40,256]{1,0:T(8,128)S(1)}, u32[]{:S(2)}, u32[]{:S(2)}) %collective-permute-start.25) | collective-permute-done | bytes 40992 | tf_op jit(solution)/shard_map/ppermute | solution.py:410
  39.5 0.6 %collective-permute-done.26 = f32[40,256]{1,0:T(8,128)S(1)} collective-permute-done((f32[40,256]{1,0:T(8,128)S(1)}, f32[40,256]{1,0:T(8,128)S(1)}, u32[]{:S(2)}, u32[]{:S(2)}) %collective-permute-start.26) | collective-permute-done | bytes 40992 | tf_op jit(solution)/shard_map/ppermute | solution.py:410
  40.1 0.5 %collective-permute-done.27 = f32[40,256]{1,0:T(8,128)S(1)} collective-permute-done((f32[40,256]{1,0:T(8,128)S(1)}, f32[40,256]{1,0:T(8,128)S(1)}, u32[]{:S(2)}, u32[]{:S(2)}) %collective-permute-start.27) | collective-permute-done | bytes 40992 | tf_op jit(solution)/shard_map/ppermute | solution.py:410
  40.6 3.7 %collective-permute-start.28 = (f32[32,256]{1,0:T(8,128)S(1)}, f32[32,256]{1,0:T(8,128)S(1)}, u32[]{:S(2)}, u32[]{:S(2)}) collective-permute-start(f32[32,256]{1,0:T(8,128)S(1)} %slice.55), channel_id=1, source_target_pairs={{0,3},{1,2},{2,1},{3,0},{4,7},{5,6},{6,5},{7,4},{8,11},{9,10},{10,... | collective-permute-start | bytes 98312 | tf_op jit(solution)/shard_map/ppermute | solution.py:475
  44.3 0.0 collective-permute-start.29
  44.3 0.8 %collective-permute-start.30 = (f32[32,256]{1,0:T(8,128)S(1)}, f32[32,256]{1,0:T(8,128)S(1)}, u32[]{:S(2)}, u32[]{:S(2)}) collective-permute-start(f32[32,256]{1,0:T(8,128)S(1)} %slice.55), channel_id=1, source_target_pairs={{0,1},{1,0},{2,3},{3,2},{4,5},{5,4},{6,7},{7,6},{8,9},{9,8},{10,11... | collective-permute-start | bytes 98312 | tf_op jit(solution)/shard_map/ppermute | solution.py:475
  45.1 0.1 convert_reduce_fusion
  45.2 0.6 %reduce_max.9 = s32[]{:T(128)} reduce(s32[4]{0:T(128)S(1)} %convert_reduce_fusion, s32[]{:T(128)} %constant.140.clone.1), dimensions={0}, to_apply=%region_1.2 | reduce | flops 3 | bytes 24 | tf_op jit(solution)/shard_map/reduce_max | solution.py:501
  46.5 0.0 collective-permute-done.28
  46.5 2.6 %collective-permute-done.29 = f32[32,256]{1,0:T(8,128)S(1)} collective-permute-done((f32[32,256]{1,0:T(8,128)S(1)}, f32[32,256]{1,0:T(8,128)S(1)}, u32[]{:S(2)}, u32[]{:S(2)}) %collective-permute-start.29) | collective-permute-done | bytes 32800 | tf_op jit(solution)/shard_map/ppermute | solution.py:475
  49.1 0.0 collective-permute-done.30
  49.1 0.2 conditional.1
  49.1 0.1 sqrt_bitcast_fusion
  49.2 0.1 add_divide_fusion.1
  49.2 0.0 copy-start.1
  49.3 0.6 %copy-done.1 = f32[32,256]{1,0:T(8,128)} copy-done((f32[32,256]{1,0:T(8,128)}, f32[32,256]{1,0:T(8,128)S(1)}, u32[]{:S(2)}) %copy-start.1) | copy-done | bytes 32792
  (10 shorter events, 0.1 us)
Async XLA Ops:
  0.0 6.8 %copy-start = (s32[2,32,128]{2,1,0:T(8,128)S(1)}, s32[2,32,128]{2,1,0:T(8,128)}, u32[]{:S(2)}) copy-start(s32[2,32,128]{2,1,0:T(8,128)} %param.8) | copy-start | bytes 98308
  0.0 18.9 %copy-start.3 = (s32[256]{0:T(256)S(1)}, s32[256]{0:T(256)}, u32[]{:S(2)}) copy-start(s32[256]{0:T(256)} %param.9) | copy-start | bytes 3076
  4.5 1.9 %collective-permute-start.16 = (bf16[6,128,256]{2,1,0:T(8,128)(2,1)S(1)}, bf16[6,128,256]{2,1,0:T(8,128)(2,1)S(1)}, u32[]{:S(2)}, u32[]{:S(2)}) collective-permute-start(bf16[6,128,256]{2,1,0:T(8,128)(2,1)S(1)} %get-tuple-element.97), channel_id=1, source_target_pairs={{0,4},{4,0},{8,12},{12,8},{16,20},{20,16},{24,28},{28,24},{1,5},{5... | collective-permute-start | bytes 1179656 | tf_op jit(solution)/shard_map/ppermute | solution.py:410
  6.4 12.5 %collective-permute-start.17 = (bf16[2,30,256,128]{3,2,1,0:T(8,128)(2,1)}, bf16[2,30,256,128]{3,2,1,0:T(8,128)(2,1)}, u32[]{:S(2)}, u32[]{:S(2)}) collective-permute-start(bf16[2,30,256,128]{3,2,1,0:T(8,128)(2,1)} %spec_ref.3), channel_id=1, source_target_pairs={{0,4},{4,0},{8,12},{12,8},{16,20},{20,16},{24,28},{28,24},{1,5},{5... | collective-permute-start | bytes 11796488 | tf_op jit(solution)/shard_map/ppermute | solution.py:410
  6.8 5.0 %collective-permute-start.15 = (s32[64,128]{1,0:T(8,128)S(1)}, s32[64,128]{1,0:T(8,128)S(1)}, u32[]{:S(2)}, u32[]{:S(2)}) collective-permute-start(s32[64,128]{1,0:T(8,128)S(1)} %bitcast.31), channel_id=1, source_target_pairs={{0,4},{4,0},{8,12},{12,8},{16,20},{20,16},{24,28},{28,24},{1,5},{5... | collective-permute-start | bytes 98312 | tf_op jit(solution)/shard_map/ppermute | solution.py:410
  6.9 8.1 %collective-permute-start.18 = (bf16[6,64,256]{2,1,0:T(8,128)(2,1)S(1)}, bf16[6,64,256]{2,1,0:T(8,128)(2,1)S(1)}, u32[]{:S(2)}, u32[]{:S(2)}) collective-permute-start(bf16[6,64,256]{2,1,0:T(8,128)(2,1)S(1)} %get-tuple-element.102.refs_0_), channel_id=1, source_target_pairs={{0,8},{4,12},{8,0},{12,4},{16,24},{20,28},{24,16},{28,20},{1,9},{5... | collective-permute-start | bytes 589832 | tf_op jit(solution)/shard_map/ppermute | solution.py:410
  9.8 7.8 %collective-permute-start.21 = (bf16[6,64,256]{2,1,0:T(8,128)(2,1)S(1)}, bf16[6,64,256]{2,1,0:T(8,128)(2,1)S(1)}, u32[]{:S(2)}, u32[]{:S(2)}) collective-permute-start(bf16[6,64,256]{2,1,0:T(8,128)(2,1)S(1)} %get-tuple-element.105.refs_3_), channel_id=1, source_target_pairs={{0,16},{4,20},{8,24},{12,28},{16,0},{20,4},{24,8},{28,12},{1,17},{... | collective-permute-start | bytes 589832 | tf_op jit(solution)/shard_map/ppermute | solution.py:410
  11.3 11.4 %collective-permute-start.19 = (bf16[6,64,256]{2,1,0:T(8,128)(2,1)S(1)}, bf16[6,64,256]{2,1,0:T(8,128)(2,1)S(1)}, u32[]{:S(2)}, u32[]{:S(2)}) collective-permute-start(bf16[6,64,256]{2,1,0:T(8,128)(2,1)S(1)} %get-tuple-element.102.refs_0_), channel_id=1, source_target_pairs={{0,16},{4,20},{8,24},{12,28},{16,0},{20,4},{24,8},{28,12},{1,17},{... | collective-permute-start | bytes 589832 | tf_op jit(solution)/shard_map/ppermute | solution.py:410
  11.8 10.9 %collective-permute-start.20 = (bf16[6,64,256]{2,1,0:T(8,128)(2,1)S(1)}, bf16[6,64,256]{2,1,0:T(8,128)(2,1)S(1)}, u32[]{:S(2)}, u32[]{:S(2)}) collective-permute-start(bf16[6,64,256]{2,1,0:T(8,128)(2,1)S(1)} %get-tuple-element.105.refs_3_), channel_id=1, source_target_pairs={{0,8},{4,12},{8,0},{12,4},{16,24},{20,28},{24,16},{28,20},{1,9},{5... | collective-permute-start | bytes 589832 | tf_op jit(solution)/shard_map/ppermute | solution.py:410
  15.0 9.9 %collective-permute-start.22 = (bf16[6,64,256]{2,1,0:T(8,128)(2,1)S(1)}, bf16[6,64,256]{2,1,0:T(8,128)(2,1)S(1)}, u32[]{:S(2)}, u32[]{:S(2)}) collective-permute-start(bf16[6,64,256]{2,1,0:T(8,128)(2,1)S(1)} %collective-permute-done.18.refs_1_), channel_id=1, source_target_pairs={{0,16},{4,20},{8,24},{12,28},{16,0},{20,4},{24,8},{28,12},{1,17},{... | collective-permute-start | bytes 589832 | tf_op jit(solution)/shard_map/ppermute | solution.py:410
  17.6 7.3 %collective-permute-start.23 = (bf16[6,64,256]{2,1,0:T(8,128)(2,1)S(1)}, bf16[6,64,256]{2,1,0:T(8,128)(2,1)S(1)}, u32[]{:S(2)}, u32[]{:S(2)}) collective-permute-start(bf16[6,64,256]{2,1,0:T(8,128)(2,1)S(1)} %collective-permute-done.21.refs_5_), channel_id=1, source_target_pairs={{0,8},{4,12},{8,0},{12,4},{16,24},{20,28},{24,16},{28,20},{1,9},{5... | collective-permute-start | bytes 589832 | tf_op jit(solution)/shard_map/ppermute | solution.py:410
  18.9 3.9 %copy-start.2 = (s32[2,32]{1,0:T(2,128)S(1)}, s32[2,32]{1,0:T(2,128)}, u32[]{:S(2)}) copy-start(s32[2,32]{1,0:T(2,128)} %src_ref.3) | copy-start | bytes 772
  32.9 1.5 %collective-permute-start.24 = (f32[4,40,256]{2,1,0:T(8,128)S(1)}, f32[4,40,256]{2,1,0:T(8,128)S(1)}, u32[]{:S(2)}, u32[]{:S(2)}) collective-permute-start(f32[4,40,256]{2,1,0:T(8,128)S(1)} %get-tuple-element.114), channel_id=1, source_target_pairs={{0,4},{4,0},{8,12},{12,8},{16,20},{20,16},{24,28},{28,24},{1,5},{5... | collective-permute-start | bytes 491528 | tf_op jit(solution)/shard_map/ppermute | solution.py:410
  34.5 5.0 %collective-permute-start.25 = (f32[40,256]{1,0:T(8,128)S(1)}, f32[40,256]{1,0:T(8,128)S(1)}, u32[]{:S(2)}, u32[]{:S(2)}) collective-permute-start(f32[40,256]{1,0:T(8,128)S(1)} %get-tuple-element.125), channel_id=1, source_target_pairs={{0,24},{4,28},{8,16},{12,20},{16,8},{20,12},{24,0},{28,4},{1,25},{... | collective-permute-start | bytes 122888 | tf_op jit(solution)/shard_map/ppermute | solution.py:410
  36.1 4.0 %collective-permute-start.26 = (f32[40,256]{1,0:T(8,128)S(1)}, f32[40,256]{1,0:T(8,128)S(1)}, u32[]{:S(2)}, u32[]{:S(2)}) collective-permute-start(f32[40,256]{1,0:T(8,128)S(1)} %get-tuple-element.127), channel_id=1, source_target_pairs={{0,16},{4,20},{8,24},{12,28},{16,0},{20,4},{24,8},{28,12},{1,17},{... | collective-permute-start | bytes 122888 | tf_op jit(solution)/shard_map/ppermute | solution.py:410
  36.6 4.0 %collective-permute-start.27 = (f32[40,256]{1,0:T(8,128)S(1)}, f32[40,256]{1,0:T(8,128)S(1)}, u32[]{:S(2)}, u32[]{:S(2)}) collective-permute-start(f32[40,256]{1,0:T(8,128)S(1)} %get-tuple-element.126), channel_id=1, source_target_pairs={{0,8},{4,12},{8,0},{12,4},{16,24},{20,28},{24,16},{28,20},{1,9},{5... | collective-permute-start | bytes 122888 | tf_op jit(solution)/shard_map/ppermute | solution.py:410
  40.6 5.9 %collective-permute-start.28 = (f32[32,256]{1,0:T(8,128)S(1)}, f32[32,256]{1,0:T(8,128)S(1)}, u32[]{:S(2)}, u32[]{:S(2)}) collective-permute-start(f32[32,256]{1,0:T(8,128)S(1)} %slice.55), channel_id=1, source_target_pairs={{0,3},{1,2},{2,1},{3,0},{4,7},{5,6},{6,5},{7,4},{8,11},{9,10},{10,... | collective-permute-start | bytes 98312 | tf_op jit(solution)/shard_map/ppermute | solution.py:475
  44.3 4.8 %collective-permute-start.29 = (f32[32,256]{1,0:T(8,128)S(1)}, f32[32,256]{1,0:T(8,128)S(1)}, u32[]{:S(2)}, u32[]{:S(2)}) collective-permute-start(f32[32,256]{1,0:T(8,128)S(1)} %slice.55), channel_id=1, source_target_pairs={{0,2},{1,3},{2,0},{3,1},{4,6},{5,7},{6,4},{7,5},{8,10},{9,11},{10,... | collective-permute-start | bytes 98312 | tf_op jit(solution)/shard_map/ppermute | solution.py:475
  44.3 4.8 %collective-permute-start.30 = (f32[32,256]{1,0:T(8,128)S(1)}, f32[32,256]{1,0:T(8,128)S(1)}, u32[]{:S(2)}, u32[]{:S(2)}) collective-permute-start(f32[32,256]{1,0:T(8,128)S(1)} %slice.55), channel_id=1, source_target_pairs={{0,1},{1,0},{2,3},{3,2},{4,5},{5,4},{6,7},{7,6},{8,9},{9,8},{10,11... | collective-permute-start | bytes 98312 | tf_op jit(solution)/shard_map/ppermute | solution.py:475
  49.2 0.6 %copy-start.1 = (f32[32,256]{1,0:T(8,128)}, f32[32,256]{1,0:T(8,128)S(1)}, u32[]{:S(2)}) copy-start(f32[32,256]{1,0:T(8,128)S(1)} %get-tuple-element.186) | copy-start | bytes 98308

commit v6 on v5

--- a/solution.py
+++ b/solution.py
@@ -289,7 +289,7 @@
 def place_early(arrays, names, late, src_ids, cap, per_chip):
     groups, part, _ = arrays[0].shape
     count = len(arrays) // len(names) * part
-    shape = (count * XPITCH + 8, LANES)
+    shape = ((count + 1) * XPITCH + 7, LANES)
     return pl.pallas_call(
         functools.partial(early_kernel, cap, names, late, per_chip),
         in_specs=[VMEM] * (1 + len(arrays)),
@@ -390,7 +390,7 @@
     out = jax.ShapeDtypeStruct((nchan // 2, per + 8, lags), F32)
     scratch = [
         (xs_early.shape, F32),
-        ((2, count * PITCH + 8, chans2 // 2), F32),
+        ((2, (count + 1) * PITCH, chans2 // 2), F32),
         ((4 * count, bins), F32),
         ((bins, lags), F32),
     ]
@@ -433,7 +433,7 @@
     return [keep[:, p * part : (p + 1) * part] + got[:, p * part : (p + 1) * part] for p in range(pieces)]
 
 
-def finish(nchan, nfreq, cap, chip, spectra, src_ids, pairs_own, got_pairs, slot_of_bin):
+def finish(nchan, nfreq, cap, chip, table, spectra, src_ids, pairs_own, got_pairs, slot_of_bin):
     _, windows, freqs, chans = spectra.shape
     half = freqs // 2
     bins = slot_of_bin.shape[0]
@@ -449,10 +449,9 @@
     recv, hot, counts = tables(spectra, got_spec, pairs_own, got_pairs, slot_of_bin, nchan)
     counts, first = lax.optimization_barrier((counts, first))
     xs_early, place = place_early(first, early, late, src_ids, cap, 2 * chans)
-    cos, sin = lag_basis(lax.axis_index("freq") * freqs + core * half, half, F, NLAG, windows)
     counts = counts[0].reshape(bins // NLAG, NLAG)
     last = [held[d] for held in arrays for d in late]
-    out = cross_and_bin(last, late, xs_early, place, recv, hot, counts, cos, sin, nchan)
+    out = cross_and_bin(last, late, xs_early, place, recv, hot, counts, *table, nchan)
     mine, other = out
 
     per = bins // nchan
@@ -495,7 +494,11 @@
     pieces = 2
     pairs_own = pair_bin.reshape(slots, chans)
     got_pairs = swap(pairs_own, nchan, 1)
-    chip = lax.optimization_barrier(chip_sources(nchan, CAP, pieces, spectra, src_ids))
+    windows, half = spectra.shape[1], spectra.shape[2] // 2
+    anchor = (lax.axis_index("freq") * 2 + (lax.axis_index("chan") & 1)) * half
+    table = lag_basis(anchor, half, F, NLAG, windows)
+    chip = chip_sources(nchan, CAP, pieces, spectra, src_ids)
+    chip, table, got_pairs = lax.optimization_barrier((chip, table, got_pairs))
     owner = src_ids // (2 * chans)
     loads = jnp.sum((owner[None] == lax.iota(I32, nchan // 2)[:, None, None]).astype(I32), axis=(1, 2))
     fits = jnp.max(loads) <= CAP
@@ -504,10 +507,10 @@
         return scaled(parts, count)
 
     def large(parts, count, *args):
-        chip = chip_sources(nchan, slots, pieces, *args[:2])
+        chip = chip_sources(nchan, slots, pieces, *args[1:3])
         return scaled(*finish(nchan, nfreq, slots, chip, *args))
 
-    args = (spectra, src_ids, pairs_own, got_pairs, slot_of_bin)
+    args = (table, spectra, src_ids, pairs_own, got_pairs, slot_of_bin)
     parts, count = finish(nchan, nfreq, CAP, chip, *args)
     return lax.cond(fits, small, large, parts, count, *args)
 

time: 50.1 us -> 49.8 us (level)
  starting transfers between devices: 18.8 us -> 17.4 us
  waiting for transfers between devices: 10.4 us -> 11.4 us
    ppermute x13, starting transfers between devices: 14.3 us -> 12.9 us  [swap(): return lax.ppermute(x, 'chan', [(i, i ^ bit) for i in range(size)])]
    ppermute x13, waiting for transfers between devices: 7.75 us -> 8.61 us  [swap(): return lax.ppermute(x, 'chan', [(i, i ^ bit) for i in range(size)])]
  transfers between devices with their start and end apart: 16 -> 16, of which waited for: 9 -> 8; matrix products, arithmetic and copies ran while one was open for 3% -> 3% of each run, Pallas kernels for 10% -> 11%
where the time goes in v6:
time: 49.8 us; the launch traced here: 49.7 us
  Pallas kernels  17.8 us (36%)
  starting transfers between devices  17.4 us (35%)
  waiting for transfers between devices  11.4 us (23%)
  other arithmetic  1.6 us (3%)
  between operations  0.82 us (2%)
  local copies, waits for them, and re-layouts  0.65 us (1%)
    ppermute x13, starting transfers between devices, swap(): return lax.ppermute(x, 'chan', [(i, i ^ bit) for i in range(size)])  12.9 us
    ppermute x13, waiting for transfers between devices, swap(): return lax.ppermute(x, 'chan', [(i, i ^ bit) for i in range(size)])  8.61 us
    pallas_call x1, Pallas kernels, cross_and_bin(): pl.pallas_call(functools.partial(cross_kernel, len(arrays)), in_specs=[VM...  8.04 us
    ppermute x3, starting transfers between devices, finish(): lax.ppermute(owned, 'freq', [(i, i ^ k) for i in range(nfreq)])  4.51 us
    pallas_call x1, Pallas kernels, pick(): pl.pallas_call(functools.partial(pick_kernel, cap), in_specs=[VMEM, ANY],...  4.44 us
    pallas_call x1, Pallas kernels, tables(): pl.pallas_call(functools.partial(tables_kernel, nchan), in_specs=[ANY, AN...  3.99 us
    ppermute x3, waiting for transfers between devices, finish(): lax.ppermute(owned, 'freq', [(i, i ^ k) for i in range(nfreq)])  2.76 us
    pallas_call x1, Pallas kernels, place_early(): pl.pallas_call(functools.partial(early_kernel, cap, names, late, per_chip...  1.35 us
  transfers between devices with their start and end apart: 16, of which 8 were waited for; matrix products, arithmetic and copies ran while one was open for 3% of the time, Pallas kernels for 11%

profile of v6, /device:TPU:0, one launch (start us, length us, event | category | flops | bytes accessed | tf_op | source)
XLA Modules:
  0.0 49.7 jit_solution(16329534855068775863)
XLA Ops:
  0.0 0.0 copy-start.1
  0.0 0.0 copy-start.4
  0.0 4.4 %pick_sources.3 = (bf16[6,128,256]{2,1,0:T(8,128)(2,1)S(1)}, bf16[6,128,256]{2,1,0:T(8,128)(2,1)S(1)}) custom-call(s32[2,32]{1,0:T(2,128)} %src_ref.3, bf16[2,30,256,128]{3,2,1,0:T(8,128)(2,1)} %spec_ref.3), custom_call_target="tpu_custom_call" | custom-call | tf_op jit(solution)/shard_map/pick_sources/pallas_call | solution.py:151
  4.5 0.5 %collective-permute-start.15 = (bf16[6,128,256]{2,1,0:T(8,128)(2,1)S(1)}, bf16[6,128,256]{2,1,0:T(8,128)(2,1)S(1)}, u32[]{:S(2)}, u32[]{:S(2)}) collective-permute-start(bf16[6,128,256]{2,1,0:T(8,128)(2,1)S(1)} %get-tuple-element.106), channel_id=1, source_target_pairs={{0,4},{4,0},{8,12},{12,8},{16,20},{20,16},{24,28},{28,24},{1,5},{5... | collective-permute-start | bytes 1179656 | tf_op jit(solution)/shard_map/ppermute | solution.py:410
  5.0 0.0 copy-done.1
  5.0 0.1 collective-permute-start.16
  5.1 0.6 %negate_multiply_fusion = (f32[128,256]{1,0:T(8,128)S(1)}, f32[128,256]{1,0:T(8,128)S(1)}) fusion(s32[256]{0:T(256)S(1)} %iota_add_fusion, s32[128]{0:T(128)S(1)} %iota_add_fusion.1), kind=kLoop, calls=%fused_computation.25 | loop fusion | flops 557056 | bytes 263680 | tf_op jit(solution)/shard_map/mul | solution.py:38
  5.7 0.6 %collective-permute-done.15 = bf16[6,128,256]{2,1,0:T(8,128)(2,1)S(1)} collective-permute-done((bf16[6,128,256]{2,1,0:T(8,128)(2,1)S(1)}, bf16[6,128,256]{2,1,0:T(8,128)(2,1)S(1)}, u32[]{:S(2)}, u32[]{:S(2)}) %collective-permute-start.15) | collective-permute-done | bytes 393248 | tf_op jit(solution)/shard_map/ppermute | solution.py:410
  6.4 0.0 collective-permute-done.16.got_pairs
  6.4 0.4 collective-permute-start.17
  6.8 2.6 %collective-permute-start.18 = (bf16[6,64,256]{2,1,0:T(8,128)(2,1)S(1)}, bf16[6,64,256]{2,1,0:T(8,128)(2,1)S(1)}, u32[]{:S(2)}, u32[]{:S(2)}) collective-permute-start(bf16[6,64,256]{2,1,0:T(8,128)(2,1)S(1)} %get-tuple-element.114.refs_0_), channel_id=1, source_target_pairs={{0,8},{4,12},{8,0},{12,4},{16,24},{20,28},{24,16},{28,20},{1,9},{5... | collective-permute-start | bytes 589832 | tf_op jit(solution)/shard_map/ppermute | solution.py:410
  9.5 1.5 %collective-permute-start.21 = (bf16[6,64,256]{2,1,0:T(8,128)(2,1)S(1)}, bf16[6,64,256]{2,1,0:T(8,128)(2,1)S(1)}, u32[]{:S(2)}, u32[]{:S(2)}) collective-permute-start(bf16[6,64,256]{2,1,0:T(8,128)(2,1)S(1)} %get-tuple-element.117.refs_3_), channel_id=1, source_target_pairs={{0,16},{4,20},{8,24},{12,28},{16,0},{20,4},{24,8},{28,12},{1,17},{... | collective-permute-start | bytes 589832 | tf_op jit(solution)/shard_map/ppermute | solution.py:410
  11.0 0.5 %collective-permute-start.19 = (bf16[6,64,256]{2,1,0:T(8,128)(2,1)S(1)}, bf16[6,64,256]{2,1,0:T(8,128)(2,1)S(1)}, u32[]{:S(2)}, u32[]{:S(2)}) collective-permute-start(bf16[6,64,256]{2,1,0:T(8,128)(2,1)S(1)} %get-tuple-element.114.refs_0_), channel_id=1, source_target_pairs={{0,16},{4,20},{8,24},{12,28},{16,0},{20,4},{24,8},{28,12},{1,17},{... | collective-permute-start | bytes 589832 | tf_op jit(solution)/shard_map/ppermute | solution.py:410
  11.5 0.1 collective-permute-start.20
  11.5 3.6 %collective-permute-done.18.refs_1_ = bf16[6,64,256]{2,1,0:T(8,128)(2,1)S(1)} collective-permute-done((bf16[6,64,256]{2,1,0:T(8,128)(2,1)S(1)}, bf16[6,64,256]{2,1,0:T(8,128)(2,1)S(1)}, u32[]{:S(2)}, u32[]{:S(2)}) %collective-permute-start.18) | collective-permute-done | bytes 196640 | tf_op jit(solution)/shard_map/ppermute | solution.py:410
  15.2 2.0 %collective-permute-start.22 = (bf16[6,64,256]{2,1,0:T(8,128)(2,1)S(1)}, bf16[6,64,256]{2,1,0:T(8,128)(2,1)S(1)}, u32[]{:S(2)}, u32[]{:S(2)}) collective-permute-start(bf16[6,64,256]{2,1,0:T(8,128)(2,1)S(1)} %collective-permute-done.18.refs_1_), channel_id=1, source_target_pairs={{0,16},{4,20},{8,24},{12,28},{16,0},{20,4},{24,8},{28,12},{1,17},{... | collective-permute-start | bytes 589832 | tf_op jit(solution)/shard_map/ppermute | solution.py:410
  17.2 0.0 collective-permute-done.21.refs_5_
  17.2 1.5 %collective-permute-start.23 = (bf16[6,64,256]{2,1,0:T(8,128)(2,1)S(1)}, bf16[6,64,256]{2,1,0:T(8,128)(2,1)S(1)}, u32[]{:S(2)}, u32[]{:S(2)}) collective-permute-start(bf16[6,64,256]{2,1,0:T(8,128)(2,1)S(1)} %collective-permute-done.21.refs_5_), channel_id=1, source_target_pairs={{0,8},{4,12},{8,0},{12,4},{16,24},{20,28},{24,16},{28,20},{1,9},{5... | collective-permute-start | bytes 589832 | tf_op jit(solution)/shard_map/ppermute | solution.py:410
  18.7 0.0 collective-permute-done.17.got_ref
  18.7 0.0 copy-done.4
  18.7 0.0 copy-start.3
  18.7 4.0 %tables.3 = (bf16[128,64,256]{2,1,0:T(8,128)(2,1)S(1)}, bf16[64,256,256]{2,1,0:T(8,128)(2,1)S(1)}, f32[8,256]{1,0:T(8,128)S(1)}) custom-call(bf16[2,30,256,128]{3,2,1,0:T(8,128)(2,1)} %spec_ref.3, bf16[2,30,256,128]{3,2,1,0:T(8,128)(2,1)S(1)} %collective-permute-done.17.got_ref, s32[64,128]{1,0:T(8,128)S(1)} %bitcast.32, ...), custom_call_target="tpu_custom_call" | custom-call | tf_op jit(solution)/shard_map/tables/pallas_call | solution.py:262
  22.7 0.0 collective-permute-done.19.refs_2_
  22.7 0.0 collective-permute-done.20.refs_4_
  22.7 0.0 copy-done.3
  22.7 1.4 %place_early.3 = (f32[4264,128]{1,0:T(8,128)S(1)}, bf16[256,640]{1,0:T(8,128)(2,1)S(1)}) custom-call(s32[2,32]{1,0:T(2,128)S(1)} %copy-done.3, bf16[6,64,256]{2,1,0:T(8,128)(2,1)S(1)} %get-tuple-element.114.refs_0_, bf16[6,64,256]{2,1,0:T(8,128)(2,1)S(1)} %collective-permute-done.18.refs_1_, bf16[6,64,256]{2,1,0:T(8,128)(2,1)S(1)} %collective-permute-done.19.refs_2_, ...), custom_call_target="tpu_custom_call" | custom-call | tf_op jit(solution)/shard_map/place_early/pallas_call | solution.py:293
  24.1 0.7 %collective-permute-done.22.refs_7_ = bf16[6,64,256]{2,1,0:T(8,128)(2,1)S(1)} collective-permute-done((bf16[6,64,256]{2,1,0:T(8,128)(2,1)S(1)}, bf16[6,64,256]{2,1,0:T(8,128)(2,1)S(1)}, u32[]{:S(2)}, u32[]{:S(2)}) %collective-permute-start.22) | collective-permute-done | bytes 196640 | tf_op jit(solution)/shard_map/ppermute | solution.py:410
  24.8 0.0 collective-permute-done.23.refs_8_
  24.8 8.0 %cross_and_bin.3 = (f32[4,40,256]{2,1,0:T(8,128)S(1)}, f32[4,40,256]{2,1,0:T(8,128)S(1)}) custom-call(bf16[256,640]{1,0:T(8,128)(2,1)S(1)} %get-tuple-element.120.refs_0_, bf16[128,64,256]{2,1,0:T(8,128)(2,1)S(1)} %get-tuple-element.121.refs_1_, bf16[64,256,256]{2,1,0:T(8,128)(2,1)S(1)} %get-tuple-element.122.refs_2_, ...), custom_call_target="tpu_custom_call" | custom-call | tf_op jit(solution)/shard_map/cross_and_bin/pallas_call | solution.py:398
  32.8 0.1 collective-permute-start.24
  32.9 1.4 %collective-permute-done.24 = f32[4,40,256]{2,1,0:T(8,128)S(1)} collective-permute-done((f32[4,40,256]{2,1,0:T(8,128)S(1)}, f32[4,40,256]{2,1,0:T(8,128)S(1)}, u32[]{:S(2)}, u32[]{:S(2)}) %collective-permute-start.24) | collective-permute-done | bytes 163872 | tf_op jit(solution)/shard_map/ppermute | solution.py:410
  34.3 1.5 %collective-permute-start.25 = (f32[40,256]{1,0:T(8,128)S(1)}, f32[40,256]{1,0:T(8,128)S(1)}, u32[]{:S(2)}, u32[]{:S(2)}) collective-permute-start(f32[40,256]{1,0:T(8,128)S(1)} %get-tuple-element.135), channel_id=1, source_target_pairs={{0,24},{4,28},{8,16},{12,20},{16,8},{20,12},{24,0},{28,4},{1,25},{... | collective-permute-start | bytes 122888 | tf_op jit(solution)/shard_map/ppermute | solution.py:410
  35.9 0.3 collective-permute-start.26
  36.2 1.7 %collective-permute-start.27 = (f32[40,256]{1,0:T(8,128)S(1)}, f32[40,256]{1,0:T(8,128)S(1)}, u32[]{:S(2)}, u32[]{:S(2)}) collective-permute-start(f32[40,256]{1,0:T(8,128)S(1)} %get-tuple-element.136), channel_id=1, source_target_pairs={{0,8},{4,12},{8,0},{12,4},{16,24},{20,28},{24,16},{28,20},{1,9},{5... | collective-permute-start | bytes 122888 | tf_op jit(solution)/shard_map/ppermute | solution.py:410
  37.9 1.4 %collective-permute-done.25 = f32[40,256]{1,0:T(8,128)S(1)} collective-permute-done((f32[40,256]{1,0:T(8,128)S(1)}, f32[40,256]{1,0:T(8,128)S(1)}, u32[]{:S(2)}, u32[]{:S(2)}) %collective-permute-start.25) | collective-permute-done | bytes 40992 | tf_op jit(solution)/shard_map/ppermute | solution.py:410
  39.3 0.5 %collective-permute-done.26 = f32[40,256]{1,0:T(8,128)S(1)} collective-permute-done((f32[40,256]{1,0:T(8,128)S(1)}, f32[40,256]{1,0:T(8,128)S(1)}, u32[]{:S(2)}, u32[]{:S(2)}) %collective-permute-start.26) | collective-permute-done | bytes 40992 | tf_op jit(solution)/shard_map/ppermute | solution.py:410
  39.9 0.3 collective-permute-done.27
  40.2 3.9 %collective-permute-start.28 = (f32[32,256]{1,0:T(8,128)S(1)}, f32[32,256]{1,0:T(8,128)S(1)}, u32[]{:S(2)}, u32[]{:S(2)}) collective-permute-start(f32[32,256]{1,0:T(8,128)S(1)} %slice.55), channel_id=1, source_target_pairs={{0,3},{1,2},{2,1},{3,0},{4,7},{5,6},{6,5},{7,4},{8,11},{9,10},{10,... | collective-permute-start | bytes 98312 | tf_op jit(solution)/shard_map/ppermute | solution.py:474
  44.1 0.0 collective-permute-start.29
  44.1 0.6 %collective-permute-start.30 = (f32[32,256]{1,0:T(8,128)S(1)}, f32[32,256]{1,0:T(8,128)S(1)}, u32[]{:S(2)}, u32[]{:S(2)}) collective-permute-start(f32[32,256]{1,0:T(8,128)S(1)} %slice.55), channel_id=1, source_target_pairs={{0,1},{1,0},{2,3},{3,2},{4,5},{5,4},{6,7},{7,6},{8,9},{9,8},{10,11... | collective-permute-start | bytes 98312 | tf_op jit(solution)/shard_map/ppermute | solution.py:474
  44.7 0.1 convert_reduce_fusion
  44.8 0.6 %reduce_max.9 = s32[]{:T(128)} reduce(s32[4]{0:T(128)S(1)} %convert_reduce_fusion, s32[]{:T(128)} %constant.118.clone.1), dimensions={0}, to_apply=%region_1.2 | reduce | flops 3 | bytes 24 | tf_op jit(solution)/shard_map/reduce_max | solution.py:504
  46.1 0.0 collective-permute-done.28
  46.1 2.8 %collective-permute-done.29 = f32[32,256]{1,0:T(8,128)S(1)} collective-permute-done((f32[32,256]{1,0:T(8,128)S(1)}, f32[32,256]{1,0:T(8,128)S(1)}, u32[]{:S(2)}, u32[]{:S(2)}) %collective-permute-start.29) | collective-permute-done | bytes 32800 | tf_op jit(solution)/shard_map/ppermute | solution.py:474
  48.9 0.0 collective-permute-done.30
  48.9 0.2 conditional.1
  48.9 0.1 sqrt_bitcast_fusion
  49.0 0.1 add_divide_fusion.1
  49.0 0.0 copy-start.2
  49.0 0.6 %copy-done.2 = f32[32,256]{1,0:T(8,128)} copy-done((f32[32,256]{1,0:T(8,128)}, f32[32,256]{1,0:T(8,128)S(1)}, u32[]{:S(2)}) %copy-start.2) | copy-done | bytes 32792
  (10 shorter events, 0.1 us)
Async XLA Ops:
  0.0 5.0 %copy-start.1 = (s32[2,32,128]{2,1,0:T(8,128)S(1)}, s32[2,32,128]{2,1,0:T(8,128)}, u32[]{:S(2)}) copy-start(s32[2,32,128]{2,1,0:T(8,128)} %param.8) | copy-start | bytes 98308
  0.0 18.7 %copy-start.4 = (s32[256]{0:T(256)S(1)}, s32[256]{0:T(256)}, u32[]{:S(2)}) copy-start(s32[256]{0:T(256)} %param.9) | copy-start | bytes 3076
  4.5 1.9 %collective-permute-start.15 = (bf16[6,128,256]{2,1,0:T(8,128)(2,1)S(1)}, bf16[6,128,256]{2,1,0:T(8,128)(2,1)S(1)}, u32[]{:S(2)}, u32[]{:S(2)}) collective-permute-start(bf16[6,128,256]{2,1,0:T(8,128)(2,1)S(1)} %get-tuple-element.106), channel_id=1, source_target_pairs={{0,4},{4,0},{8,12},{12,8},{16,20},{20,16},{24,28},{28,24},{1,5},{5... | collective-permute-start | bytes 1179656 | tf_op jit(solution)/shard_map/ppermute | solution.py:410
  5.0 1.4 %collective-permute-start.16 = (s32[64,128]{1,0:T(8,128)S(1)}, s32[64,128]{1,0:T(8,128)S(1)}, u32[]{:S(2)}, u32[]{:S(2)}) collective-permute-start(s32[64,128]{1,0:T(8,128)S(1)} %bitcast.31), channel_id=1, source_target_pairs={{0,4},{4,0},{8,12},{12,8},{16,20},{20,16},{24,28},{28,24},{1,5},{5... | collective-permute-start | bytes 98312 | tf_op jit(solution)/shard_map/ppermute | solution.py:410
  6.4 12.3 %collective-permute-start.17 = (bf16[2,30,256,128]{3,2,1,0:T(8,128)(2,1)}, bf16[2,30,256,128]{3,2,1,0:T(8,128)(2,1)S(1)}, u32[]{:S(2)}, u32[]{:S(2)}) collective-permute-start(bf16[2,30,256,128]{3,2,1,0:T(8,128)(2,1)} %spec_ref.3), channel_id=1, source_target_pairs={{0,4},{4,0},{8,12},{12,8},{16,20},{20,16},{24,28},{28,24},{1,5},{5... | collective-permute-start | bytes 11796488 | tf_op jit(solution)/shard_map/ppermute | solution.py:410
  6.8 8.4 %collective-permute-start.18 = (bf16[6,64,256]{2,1,0:T(8,128)(2,1)S(1)}, bf16[6,64,256]{2,1,0:T(8,128)(2,1)S(1)}, u32[]{:S(2)}, u32[]{:S(2)}) collective-permute-start(bf16[6,64,256]{2,1,0:T(8,128)(2,1)S(1)} %get-tuple-element.114.refs_0_), channel_id=1, source_target_pairs={{0,8},{4,12},{8,0},{12,4},{16,24},{20,28},{24,16},{28,20},{1,9},{5... | collective-permute-start | bytes 589832 | tf_op jit(solution)/shard_map/ppermute | solution.py:410
  9.5 7.8 %collective-permute-start.21 = (bf16[6,64,256]{2,1,0:T(8,128)(2,1)S(1)}, bf16[6,64,256]{2,1,0:T(8,128)(2,1)S(1)}, u32[]{:S(2)}, u32[]{:S(2)}) collective-permute-start(bf16[6,64,256]{2,1,0:T(8,128)(2,1)S(1)} %get-tuple-element.117.refs_3_), channel_id=1, source_target_pairs={{0,16},{4,20},{8,24},{12,28},{16,0},{20,4},{24,8},{28,12},{1,17},{... | collective-permute-start | bytes 589832 | tf_op jit(solution)/shard_map/ppermute | solution.py:410
  11.0 11.7 %collective-permute-start.19 = (bf16[6,64,256]{2,1,0:T(8,128)(2,1)S(1)}, bf16[6,64,256]{2,1,0:T(8,128)(2,1)S(1)}, u32[]{:S(2)}, u32[]{:S(2)}) collective-permute-start(bf16[6,64,256]{2,1,0:T(8,128)(2,1)S(1)} %get-tuple-element.114.refs_0_), channel_id=1, source_target_pairs={{0,16},{4,20},{8,24},{12,28},{16,0},{20,4},{24,8},{28,12},{1,17},{... | collective-permute-start | bytes 589832 | tf_op jit(solution)/shard_map/ppermute | solution.py:410
  11.5 11.2 %collective-permute-start.20 = (bf16[6,64,256]{2,1,0:T(8,128)(2,1)S(1)}, bf16[6,64,256]{2,1,0:T(8,128)(2,1)S(1)}, u32[]{:S(2)}, u32[]{:S(2)}) collective-permute-start(bf16[6,64,256]{2,1,0:T(8,128)(2,1)S(1)} %get-tuple-element.117.refs_3_), channel_id=1, source_target_pairs={{0,8},{4,12},{8,0},{12,4},{16,24},{20,28},{24,16},{28,20},{1,9},{5... | collective-permute-start | bytes 589832 | tf_op jit(solution)/shard_map/ppermute | solution.py:410
  15.2 9.6 %collective-permute-start.22 = (bf16[6,64,256]{2,1,0:T(8,128)(2,1)S(1)}, bf16[6,64,256]{2,1,0:T(8,128)(2,1)S(1)}, u32[]{:S(2)}, u32[]{:S(2)}) collective-permute-start(bf16[6,64,256]{2,1,0:T(8,128)(2,1)S(1)} %collective-permute-done.18.refs_1_), channel_id=1, source_target_pairs={{0,16},{4,20},{8,24},{12,28},{16,0},{20,4},{24,8},{28,12},{1,17},{... | collective-permute-start | bytes 589832 | tf_op jit(solution)/shard_map/ppermute | solution.py:410
  17.2 7.6 %collective-permute-start.23 = (bf16[6,64,256]{2,1,0:T(8,128)(2,1)S(1)}, bf16[6,64,256]{2,1,0:T(8,128)(2,1)S(1)}, u32[]{:S(2)}, u32[]{:S(2)}) collective-permute-start(bf16[6,64,256]{2,1,0:T(8,128)(2,1)S(1)} %collective-permute-done.21.refs_5_), channel_id=1, source_target_pairs={{0,8},{4,12},{8,0},{12,4},{16,24},{20,28},{24,16},{28,20},{1,9},{5... | collective-permute-start | bytes 589832 | tf_op jit(solution)/shard_map/ppermute | solution.py:410
  18.7 4.0 %copy-start.3 = (s32[2,32]{1,0:T(2,128)S(1)}, s32[2,32]{1,0:T(2,128)}, u32[]{:S(2)}) copy-start(s32[2,32]{1,0:T(2,128)} %src_ref.3) | copy-start | bytes 772
  32.8 1.5 %collective-permute-start.24 = (f32[4,40,256]{2,1,0:T(8,128)S(1)}, f32[4,40,256]{2,1,0:T(8,128)S(1)}, u32[]{:S(2)}, u32[]{:S(2)}) collective-permute-start(f32[4,40,256]{2,1,0:T(8,128)S(1)} %get-tuple-element.126), channel_id=1, source_target_pairs={{0,4},{4,0},{8,12},{12,8},{16,20},{20,16},{24,28},{28,24},{1,5},{5... | collective-permute-start | bytes 491528 | tf_op jit(solution)/shard_map/ppermute | solution.py:410
  34.3 5.0 %collective-permute-start.25 = (f32[40,256]{1,0:T(8,128)S(1)}, f32[40,256]{1,0:T(8,128)S(1)}, u32[]{:S(2)}, u32[]{:S(2)}) collective-permute-start(f32[40,256]{1,0:T(8,128)S(1)} %get-tuple-element.135), channel_id=1, source_target_pairs={{0,24},{4,28},{8,16},{12,20},{16,8},{20,12},{24,0},{28,4},{1,25},{... | collective-permute-start | bytes 122888 | tf_op jit(solution)/shard_map/ppermute | solution.py:410
  35.9 4.0 %collective-permute-start.26 = (f32[40,256]{1,0:T(8,128)S(1)}, f32[40,256]{1,0:T(8,128)S(1)}, u32[]{:S(2)}, u32[]{:S(2)}) collective-permute-start(f32[40,256]{1,0:T(8,128)S(1)} %get-tuple-element.137), channel_id=1, source_target_pairs={{0,16},{4,20},{8,24},{12,28},{16,0},{20,4},{24,8},{28,12},{1,17},{... | collective-permute-start | bytes 122888 | tf_op jit(solution)/shard_map/ppermute | solution.py:410
  36.2 4.0 %collective-permute-start.27 = (f32[40,256]{1,0:T(8,128)S(1)}, f32[40,256]{1,0:T(8,128)S(1)}, u32[]{:S(2)}, u32[]{:S(2)}) collective-permute-start(f32[40,256]{1,0:T(8,128)S(1)} %get-tuple-element.136), channel_id=1, source_target_pairs={{0,8},{4,12},{8,0},{12,4},{16,24},{20,28},{24,16},{28,20},{1,9},{5... | collective-permute-start | bytes 122888 | tf_op jit(solution)/shard_map/ppermute | solution.py:410
  40.2 5.9 %collective-permute-start.28 = (f32[32,256]{1,0:T(8,128)S(1)}, f32[32,256]{1,0:T(8,128)S(1)}, u32[]{:S(2)}, u32[]{:S(2)}) collective-permute-start(f32[32,256]{1,0:T(8,128)S(1)} %slice.55), channel_id=1, source_target_pairs={{0,3},{1,2},{2,1},{3,0},{4,7},{5,6},{6,5},{7,4},{8,11},{9,10},{10,... | collective-permute-start | bytes 98312 | tf_op jit(solution)/shard_map/ppermute | solution.py:474
  44.1 4.8 %collective-permute-start.29 = (f32[32,256]{1,0:T(8,128)S(1)}, f32[32,256]{1,0:T(8,128)S(1)}, u32[]{:S(2)}, u32[]{:S(2)}) collective-permute-start(f32[32,256]{1,0:T(8,128)S(1)} %slice.55), channel_id=1, source_target_pairs={{0,2},{1,3},{2,0},{3,1},{4,6},{5,7},{6,4},{7,5},{8,10},{9,11},{10,... | collective-permute-start | bytes 98312 | tf_op jit(solution)/shard_map/ppermute | solution.py:474
  44.1 4.8 %collective-permute-start.30 = (f32[32,256]{1,0:T(8,128)S(1)}, f32[32,256]{1,0:T(8,128)S(1)}, u32[]{:S(2)}, u32[]{:S(2)}) collective-permute-start(f32[32,256]{1,0:T(8,128)S(1)} %slice.55), channel_id=1, source_target_pairs={{0,1},{1,0},{2,3},{3,2},{4,5},{5,4},{6,7},{7,6},{8,9},{9,8},{10,11... | collective-permute-start | bytes 98312 | tf_op jit(solution)/shard_map/ppermute | solution.py:474
  49.0 0.6 %copy-start.2 = (f32[32,256]{1,0:T(8,128)}, f32[32,256]{1,0:T(8,128)S(1)}, u32[]{:S(2)}) copy-start(f32[32,256]{1,0:T(8,128)S(1)} %get-tuple-element.201) | copy-start | bytes 98308

commit v7 on v6

--- a/solution.py
+++ b/solution.py
@@ -11,6 +11,8 @@
 F = 1024
 NLAG = 256
 BF = jnp.bfloat16
+F8 = jnp.float8_e4m3fn
+F8_TOP = 224.0
 F32 = jnp.float32
 I32 = jnp.int32
 FB = 16
@@ -164,6 +166,11 @@
     )(src_ids, spectra)
 
 
+def largest(values, rows=16):
+    lanes = values.shape[-1]
+    return jnp.max(jnp.abs(values).reshape(-1, rows, lanes), axis=0)
+
+
 def placement(cap, names, src_ref, per_chip):
     wg = PACK // (2 * cap)
     me = lax.axis_index("chan")
@@ -198,8 +205,9 @@
 
 
 def tables_kernel(
-    nchan, spec_ref, got_ref, own_pairs, got_pairs, slot_ref, recv_ref, hot_ref, count_ref, own, got, named, tally, in_sem
+    nchan, spec_ref, got_ref, own_pairs, got_pairs, slot_ref, *refs
 ):
+    recv_ref, hot_ref, *narrow, count_ref, top_ref, own, got, named, tally, in_sem = refs
     _, windows, half, chans = got.shape
     slots = own_pairs.shape[0]
     bins = slot_ref.shape[1]
@@ -229,7 +237,11 @@
             bin_of = named[...]
             mine_hit = jnp.where(own_pairs[pl.ds(s, 1), :] == bin_of, 1.0, 0.0)
             hot_ref[s, :, pl.ds(0, chans)] = mine_hit.astype(BF)
-            hot_ref[s, :, pl.ds(chans, chans)] = jnp.where(got_pairs[pl.ds(s, 1), :] == bin_of, 1.0, 0.0).astype(BF)
+            got_hit = jnp.where(got_pairs[pl.ds(s, 1), :] == bin_of, 1.0, 0.0)
+            hot_ref[s, :, pl.ds(chans, chans)] = got_hit.astype(BF)
+            for hot8_ref in narrow:
+                hot8_ref[s, :, pl.ds(0, chans)] = mine_hit.astype(F8)
+                hot8_ref[s, :, pl.ds(chans, chans)] = got_hit.astype(F8)
             total = total + mine_hit
         tally[...] = total
         return carry
@@ -242,6 +254,7 @@
     turn = frequency_first(wp)
     for copy in ins:
         copy.wait()
+    top = jnp.zeros(top_ref.shape, BF)
     for b in range(half // FB):
         at = pl.ds(b * FB, FB)
         for k in range(2):
@@ -250,6 +263,8 @@
                 both = jnp.concatenate([own[k, ws, at, :], got[k, ws, at, :]], axis=2).reshape(wp * FB, 2 * chans)
                 moved = jnp.dot(turn, both, preferred_element_type=F32).astype(BF)
                 recv_ref[at, pl.ds((2 * k + w2) * WROWS, WROWS), :] = moved.reshape(FB, WROWS, 2 * chans)
+                top = jnp.maximum(top, largest(moved))
+    top_ref[...] = top
 
 
 def tables(spectra, got, own_pairs, got_pairs, slot_of_bin, nchan):
@@ -259,14 +274,18 @@
     bins = slot_of_bin.shape[0]
     side = ((2, windows, half, chans), BF)
     square = ((bins, chans), I32)
+    narrow = [jax.ShapeDtypeStruct((slots, bins, 2 * chans), F8)]
+    narrow = narrow if narrow[0].size <= BIG else []
     return pl.pallas_call(
         functools.partial(tables_kernel, nchan),
         in_specs=[ANY, ANY, VMEM, VMEM, VMEM],
-        out_specs=[VMEM, VMEM, VMEM],
+        out_specs=[VMEM] * (4 + len(narrow)),
         out_shape=[
             jax.ShapeDtypeStruct((half, 4 * WROWS, 2 * chans), BF),
             jax.ShapeDtypeStruct((slots, bins, 2 * chans), BF),
+            *narrow,
             jax.ShapeDtypeStruct((8, bins), F32),
+            jax.ShapeDtypeStruct((16, 2 * chans), BF),
         ],
         scratch_shapes=[
             pltpu.VMEM(*side),
@@ -281,7 +300,8 @@
 
 
 def early_kernel(cap, names, late, per_chip, src_ref, *refs):
-    *xrefs, xs_ref, late_ref = refs
+    *xrefs, xs_ref, late_ref, top_ref = refs
+    top_ref[...] = functools.reduce(jnp.maximum, [largest(x[...]) for x in xrefs])
     place_sources(placement(cap, names, src_ref, per_chip), xrefs, xs_ref)
     late_ref[...] = placement(cap, late, src_ref, per_chip)
 
@@ -293,24 +313,31 @@
     return pl.pallas_call(
         functools.partial(early_kernel, cap, names, late, per_chip),
         in_specs=[VMEM] * (1 + len(arrays)),
-        out_specs=[VMEM, VMEM],
+        out_specs=[VMEM] * 3,
         out_shape=[
             jax.ShapeDtypeStruct(shape, F32),
             jax.ShapeDtypeStruct((len(late) * PACK, PACK // (2 * cap) * LANES), BF),
+            jax.ShapeDtypeStruct((16, PACK), BF),
         ],
         compiler_params=params(*staging(arrays, names)),
         name="place_early",
     )(src_ids, *arrays)
 
 
-def cross_kernel(inputs, *refs):
-    place_ref, recv, hot, cos_ref, sin_ref, count_ref, xs_early = refs[:7]
-    xrefs, refs = refs[7 : 7 + inputs], refs[7 + inputs :]
+def cross_kernel(inputs, hots, *refs):
+    place_ref, recv, cos_ref, sin_ref, count_ref, xs_early, top_recv, top_early = refs[:8]
+    xrefs, refs = refs[8 : 8 + inputs], refs[8 + inputs :]
+    (hot, *narrow), refs = refs[:hots], refs[hots:]
     outs, refs = refs[:2], refs[2:]
     xs, cross, sums, whole = refs
     count, _, chans2 = recv.shape
     slots, bins, _ = hot.shape
     place_sources(place_ref[...], xrefs, xs)
+    top_src = functools.reduce(jnp.maximum, [top_early[...]] + [largest(x[...]) for x in xrefs]).astype(F32)
+    products = 2 * xrefs[0].shape[0] * place_ref.shape[1] // LANES
+    bound = jnp.max(top_src, axis=(0, 1), keepdims=True) * jnp.max(top_recv[...].astype(F32), axis=(0, 1), keepdims=True)
+    bound = jnp.maximum(bound * products, 1e-30) * (1.0 / 256)
+    scale, unscale = F8_TOP / bound, bound * (1.0 / F8_TOP)
     imag = iota((2 * WROWS, LANES), 1) >= slots
     quarter = shift(iota((1, 4 * 4 * WROWS), 1), 4 * WROWS)
     masks = [jnp.where(quarter == i, 1.0, 0.0).astype(BF) for i in range(4)]
@@ -345,7 +372,7 @@
     sums[...] = jnp.zeros_like(sums)
 
     def one_turn(step, carry):
-        lefts = []
+        lefts, lows = [], []
         for u in range(TURN):
             s = step * TURN + u
             parts = []
@@ -354,15 +381,26 @@
                 parts.append(jnp.concatenate([cross[0, at, :], cross[1, at, :]], axis=1))
             x = jnp.concatenate(parts, axis=0)
             high = x.astype(BF)
-            low = (x - high.astype(F32)).astype(BF)
-            lefts.append(jnp.concatenate([high, low], axis=0))
+            low = x - high.astype(F32)
+            if narrow:
+                lefts.append(high)
+                lows.append((low * scale).astype(F8))
+            else:
+                lefts.append(jnp.concatenate([high, low.astype(BF)], axis=0))
         left = jnp.concatenate(lefts, axis=1)
         right = jnp.concatenate([hot[step * TURN + u] for u in range(TURN)], axis=1)
-        sums[...] += lax.dot_general(left, right, (((1,), (1,)), ((), ())), preferred_element_type=F32)
+        at = pl.ds(0, left.shape[0])
+        sums[at, :] += lax.dot_general(left, right, (((1,), (1,)), ((), ())), preferred_element_type=F32)
+        for hot8 in narrow:
+            left = jnp.concatenate(lows, axis=1)
+            right = jnp.concatenate([hot8[step * TURN + u] for u in range(TURN)], axis=1)
+            at = pl.ds(2 * count, 2 * count)
+            sums[at, :] += lax.dot_general(left, right, (((1,), (1,)), ((), ())), preferred_element_type=F32)
         return carry
 
     lax.fori_loop(0, slots // TURN, one_turn, 0)
-    total = sums[pl.ds(0, 2 * count), :] + sums[pl.ds(2 * count, 2 * count), :]
+    low = sums[pl.ds(2 * count, 2 * count), :]
+    total = sums[pl.ds(0, 2 * count), :] + (low * unscale if narrow else low)
     table = jnp.concatenate([cos_ref[...], sin_ref[...]], axis=0)
     whole[...] = lax.dot_general(total, table, (((0,), (0,)), ((), ())), precision=lax.Precision.HIGHEST, preferred_element_type=F32)
     core = lax.axis_index("chan") & 1
@@ -382,7 +420,8 @@
     return [((groups * part, 4 * PACK), F32), ((groups * part, chips * PACK), BF), ((chips * PACK, 4 * PACK), F32)]
 
 
-def cross_and_bin(arrays, names, xs_early, place, recv, hot, counts, cos, sin, nchan):
+def cross_and_bin(arrays, names, xs_early, place, recv, hots, counts, tops, cos, sin, nchan):
+    hot = hots[0]
     _, bins, chans2 = hot.shape
     lags = cos.shape[1]
     count = recv.shape[0]
@@ -396,14 +435,14 @@
     ]
     buffers = scratch + staging(arrays, names)
     return pl.pallas_call(
-        functools.partial(cross_kernel, len(arrays)),
-        in_specs=[VMEM] * (7 + len(arrays)),
+        functools.partial(cross_kernel, len(arrays), len(hots)),
+        in_specs=[VMEM] * (8 + len(arrays) + len(hots)),
         out_specs=[VMEM, VMEM],
         out_shape=[out, out],
         scratch_shapes=[pltpu.VMEM(shape, kind) for shape, kind in scratch],
         compiler_params=params(*buffers, *([(hot.shape, BF)] if hot.size > BIG else [])),
         name="cross_and_bin",
-    )(place, recv, hot, cos, sin, counts, xs_early, *arrays)
+    )(place, recv, cos, sin, counts, xs_early, *tops, *arrays, *hots)
 
 
 def swap(x, size, bit):
@@ -446,12 +485,12 @@
     chips = len(arrays[0])
     early, late = list(range(chips - chips // 4)), list(range(chips - chips // 4, chips))
     first = [held[d] for held in arrays for d in early]
-    recv, hot, counts = tables(spectra, got_spec, pairs_own, got_pairs, slot_of_bin, nchan)
+    recv, *hots, counts, top_recv = tables(spectra, got_spec, pairs_own, got_pairs, slot_of_bin, nchan)
     counts, first = lax.optimization_barrier((counts, first))
-    xs_early, place = place_early(first, early, late, src_ids, cap, 2 * chans)
+    xs_early, place, top_early = place_early(first, early, late, src_ids, cap, 2 * chans)
     counts = counts[0].reshape(bins // NLAG, NLAG)
     last = [held[d] for held in arrays for d in late]
-    out = cross_and_bin(last, late, xs_early, place, recv, hot, counts, *table, nchan)
+    out = cross_and_bin(last, late, xs_early, place, recv, hots, counts, (top_recv, top_early), *table, nchan)
     mine, other = out
 
     per = bins // nchan

time: 49.8 us -> 49.5 us (level)
    pallas_call x1, Pallas kernels: 3.99 us -> 4.57 us  [tables(): pl.pallas_call(functools.partial(tables_kernel, nchan), in_specs=[ANY, AN...]
  transfers between devices with their start and end apart: 16 -> 16, of which waited for: 8 -> 9; matrix products, arithmetic and copies ran while one was open for 3% -> 3% of each run, Pallas kernels for 11% -> 12%
where the time goes in v7:
time: 49.5 us; the launch traced here: 49.3 us
  Pallas kernels  17.9 us (36%)
  starting transfers between devices  17.3 us (35%)
  waiting for transfers between devices  11 us (22%)
  other arithmetic  1.6 us (3%)
  between operations  0.83 us (2%)
  local copies, waits for them, and re-layouts  0.66 us (1%)
    ppermute x13, starting transfers between devices, swap(): return lax.ppermute(x, 'chan', [(i, i ^ bit) for i in range(size)])  12.8 us
    ppermute x13, waiting for transfers between devices, swap(): return lax.ppermute(x, 'chan', [(i, i ^ bit) for i in range(size)])  8.41 us
    pallas_call x1, Pallas kernels, cross_and_bin(): pl.pallas_call(functools.partial(cross_kernel, len(arrays), len(hots)), i...  7.57 us
    pallas_call x1, Pallas kernels, tables(): pl.pallas_call(functools.partial(tables_kernel, nchan), in_specs=[ANY, AN...  4.57 us
    ppermute x3, starting transfers between devices, finish(): lax.ppermute(owned, 'freq', [(i, i ^ k) for i in range(nfreq)])  4.45 us
    pallas_call x1, Pallas kernels, pick(): pl.pallas_call(functools.partial(pick_kernel, cap), in_specs=[VMEM, ANY],...  4.44 us
    ppermute x3, waiting for transfers between devices, finish(): lax.ppermute(owned, 'freq', [(i, i ^ k) for i in range(nfreq)])  2.64 us
    pallas_call x1, Pallas kernels, place_early(): pl.pallas_call(functools.partial(early_kernel, cap, names, late, per_chip...  1.35 us
  transfers between devices with their start and end apart: 16, of which 9 were waited for; matrix products, arithmetic and copies ran while one was open for 3% of the time, Pallas kernels for 12%

profile of v7, /device:TPU:0, one launch (start us, length us, event | category | flops | bytes accessed | tf_op | source)
XLA Modules:
  0.0 49.3 jit_solution(8006857007200288550)
XLA Ops:
  0.0 0.0 copy-start.1
  0.0 0.0 copy-start.4
  0.0 4.4 %pick_sources.3 = (bf16[6,128,256]{2,1,0:T(8,128)(2,1)S(1)}, bf16[6,128,256]{2,1,0:T(8,128)(2,1)S(1)}) custom-call(s32[2,32]{1,0:T(2,128)} %src_ref.3, bf16[2,30,256,128]{3,2,1,0:T(8,128)(2,1)} %spec_ref.3), custom_call_target="tpu_custom_call" | custom-call | tf_op jit(solution)/shard_map/pick_sources/pallas_call | solution.py:153
  4.5 0.5 %collective-permute-start.15 = (bf16[6,128,256]{2,1,0:T(8,128)(2,1)S(1)}, bf16[6,128,256]{2,1,0:T(8,128)(2,1)S(1)}, u32[]{:S(2)}, u32[]{:S(2)}) collective-permute-start(bf16[6,128,256]{2,1,0:T(8,128)(2,1)S(1)} %get-tuple-element.112), channel_id=1, source_target_pairs={{0,4},{4,0},{8,12},{12,8},{16,20},{20,16},{24,28},{28,24},{1,5},{5... | collective-permute-start | bytes 1179656 | tf_op jit(solution)/shard_map/ppermute | solution.py:449
  5.0 0.1 collective-permute-start.16
  5.1 0.6 %negate_multiply_fusion = (f32[128,256]{1,0:T(8,128)S(1)}, f32[128,256]{1,0:T(8,128)S(1)}) fusion(s32[256]{0:T(256)S(1)} %iota_add_fusion, s32[128]{0:T(128)S(1)} %iota_add_fusion.1), kind=kLoop, calls=%fused_computation.25 | loop fusion | flops 557056 | bytes 263680 | tf_op jit(solution)/shard_map/mul | solution.py:40
  5.7 0.7 %collective-permute-done.15 = bf16[6,128,256]{2,1,0:T(8,128)(2,1)S(1)} collective-permute-done((bf16[6,128,256]{2,1,0:T(8,128)(2,1)S(1)}, bf16[6,128,256]{2,1,0:T(8,128)(2,1)S(1)}, u32[]{:S(2)}, u32[]{:S(2)}) %collective-permute-start.15) | collective-permute-done | bytes 393248 | tf_op jit(solution)/shard_map/ppermute | solution.py:449
  6.4 0.0 copy-start.3
  6.4 0.2 collective-permute-done.16.got_pairs
  6.6 0.4 collective-permute-start.17
  7.0 2.6 %collective-permute-start.18 = (bf16[6,64,256]{2,1,0:T(8,128)(2,1)S(1)}, bf16[6,64,256]{2,1,0:T(8,128)(2,1)S(1)}, u32[]{:S(2)}, u32[]{:S(2)}) collective-permute-start(bf16[6,64,256]{2,1,0:T(8,128)(2,1)S(1)} %get-tuple-element.120.refs_0_), channel_id=1, source_target_pairs={{0,8},{4,12},{8,0},{12,4},{16,24},{20,28},{24,16},{28,20},{1,9},{5... | collective-permute-start | bytes 589832 | tf_op jit(solution)/shard_map/ppermute | solution.py:449
  9.6 1.5 %collective-permute-start.21 = (bf16[6,64,256]{2,1,0:T(8,128)(2,1)S(1)}, bf16[6,64,256]{2,1,0:T(8,128)(2,1)S(1)}, u32[]{:S(2)}, u32[]{:S(2)}) collective-permute-start(bf16[6,64,256]{2,1,0:T(8,128)(2,1)S(1)} %get-tuple-element.123.refs_3_), channel_id=1, source_target_pairs={{0,16},{4,20},{8,24},{12,28},{16,0},{20,4},{24,8},{28,12},{1,17},{... | collective-permute-start | bytes 589832 | tf_op jit(solution)/shard_map/ppermute | solution.py:449
  11.1 0.5 %collective-permute-start.19 = (bf16[6,64,256]{2,1,0:T(8,128)(2,1)S(1)}, bf16[6,64,256]{2,1,0:T(8,128)(2,1)S(1)}, u32[]{:S(2)}, u32[]{:S(2)}) collective-permute-start(bf16[6,64,256]{2,1,0:T(8,128)(2,1)S(1)} %get-tuple-element.120.refs_0_), channel_id=1, source_target_pairs={{0,16},{4,20},{8,24},{12,28},{16,0},{20,4},{24,8},{28,12},{1,17},{... | collective-permute-start | bytes 589832 | tf_op jit(solution)/shard_map/ppermute | solution.py:449
  11.6 0.1 collective-permute-start.20
  11.7 3.6 %collective-permute-done.18.refs_1_ = bf16[6,64,256]{2,1,0:T(8,128)(2,1)S(1)} collective-permute-done((bf16[6,64,256]{2,1,0:T(8,128)(2,1)S(1)}, bf16[6,64,256]{2,1,0:T(8,128)(2,1)S(1)}, u32[]{:S(2)}, u32[]{:S(2)}) %collective-permute-start.18) | collective-permute-done | bytes 196640 | tf_op jit(solution)/shard_map/ppermute | solution.py:449
  15.3 2.0 %collective-permute-start.22 = (bf16[6,64,256]{2,1,0:T(8,128)(2,1)S(1)}, bf16[6,64,256]{2,1,0:T(8,128)(2,1)S(1)}, u32[]{:S(2)}, u32[]{:S(2)}) collective-permute-start(bf16[6,64,256]{2,1,0:T(8,128)(2,1)S(1)} %collective-permute-done.18.refs_1_), channel_id=1, source_target_pairs={{0,16},{4,20},{8,24},{12,28},{16,0},{20,4},{24,8},{28,12},{1,17},{... | collective-permute-start | bytes 589832 | tf_op jit(solution)/shard_map/ppermute | solution.py:449
  17.3 0.0 collective-permute-done.21.refs_5_
  17.3 1.5 %collective-permute-start.23 = (bf16[6,64,256]{2,1,0:T(8,128)(2,1)S(1)}, bf16[6,64,256]{2,1,0:T(8,128)(2,1)S(1)}, u32[]{:S(2)}, u32[]{:S(2)}) collective-permute-start(bf16[6,64,256]{2,1,0:T(8,128)(2,1)S(1)} %collective-permute-done.21.refs_5_), channel_id=1, source_target_pairs={{0,8},{4,12},{8,0},{12,4},{16,24},{20,28},{24,16},{28,20},{1,9},{5... | collective-permute-start | bytes 589832 | tf_op jit(solution)/shard_map/ppermute | solution.py:449
  18.8 0.0 collective-permute-done.17.got_ref
  18.8 0.0 copy-done.1
  18.8 0.0 copy-done.4
  18.8 4.6 %tables.3 = (bf16[128,64,256]{2,1,0:T(8,128)(2,1)S(1)}, bf16[64,256,256]{2,1,0:T(8,128)(2,1)S(1)}, f8e4m3fn[64,256,256]{2,1,0:T(32,128)(4,1)S(1)}, f32[8,256]{1,0:T(8,128)S(1)}, bf16[16,256]{1,0:T(8,128)(2,1)S(1)}) custom-call(bf16[2,30,256,128]{3,2,1,0:T(8,128)(2,1)} %spec_ref.3, bf16[2,30,256,128]{3,2,1,0:T(8,128)(2,1)S(1)} %collective-permute-done.17.got_ref, ...), custom_call_target="tpu_custom_call" | custom-call | tf_op jit(solution)/shard_map/tables/pallas_call | solution.py:279
  23.4 0.0 collective-permute-done.19.refs_2_
  23.4 0.0 collective-permute-done.20.refs_4_
  23.5 0.0 copy-done.3
  23.5 1.3 %place_early.3 = (f32[4264,128]{1,0:T(8,128)S(1)}, bf16[256,640]{1,0:T(8,128)(2,1)S(1)}, bf16[16,256]{1,0:T(8,128)(2,1)S(1)}) custom-call(s32[2,32]{1,0:T(2,128)S(1)} %copy-done.3, bf16[6,64,256]{2,1,0:T(8,128)(2,1)S(1)} %get-tuple-element.120.refs_0_, bf16[6,64,256]{2,1,0:T(8,128)(2,1)S(1)} %collective-permute-done.18.refs_1_, ...), custom_call_target="tpu_custom_call" | custom-call | tf_op jit(solution)/shard_map/place_early/pallas_call | solution.py:313
  24.8 0.1 collective-permute-done.22.refs_8_
  24.9 0.0 collective-permute-done.23.refs_9_
  24.9 7.6 %cross_and_bin.3 = (f32[4,40,256]{2,1,0:T(8,128)S(1)}, f32[4,40,256]{2,1,0:T(8,128)S(1)}) custom-call(bf16[256,640]{1,0:T(8,128)(2,1)S(1)} %get-tuple-element.126.refs_0_, bf16[128,64,256]{2,1,0:T(8,128)(2,1)S(1)} %get-tuple-element.127.refs_1_, f32[128,256]{1,0:T(8,128)S(1)} %get-tuple-element.114.refs_2_, f32[128,256]{1,0:T(8,128)S(1)} %get-tuple-element.115.refs_3_, ...), custom_call_target="tpu_custom_call" | custom-call | tf_op jit(solution)/shard_map/cross_and_bin/pallas_call | solution.py:437
  32.5 0.1 collective-permute-start.24
  32.6 1.4 %collective-permute-done.24 = f32[4,40,256]{2,1,0:T(8,128)S(1)} collective-permute-done((f32[4,40,256]{2,1,0:T(8,128)S(1)}, f32[4,40,256]{2,1,0:T(8,128)S(1)}, u32[]{:S(2)}, u32[]{:S(2)}) %collective-permute-start.24) | collective-permute-done | bytes 163872 | tf_op jit(solution)/shard_map/ppermute | solution.py:449
  34.0 1.6 %collective-permute-start.25 = (f32[40,256]{1,0:T(8,128)S(1)}, f32[40,256]{1,0:T(8,128)S(1)}, u32[]{:S(2)}, u32[]{:S(2)}) collective-permute-start(f32[40,256]{1,0:T(8,128)S(1)} %get-tuple-element.144), channel_id=1, source_target_pairs={{0,24},{4,28},{8,16},{12,20},{16,8},{20,12},{24,0},{28,4},{1,25},{... | collective-permute-start | bytes 122888 | tf_op jit(solution)/shard_map/ppermute | solution.py:449
  35.5 0.5 collective-permute-start.26
  36.0 1.5 %collective-permute-start.27 = (f32[40,256]{1,0:T(8,128)S(1)}, f32[40,256]{1,0:T(8,128)S(1)}, u32[]{:S(2)}, u32[]{:S(2)}) collective-permute-start(f32[40,256]{1,0:T(8,128)S(1)} %get-tuple-element.145), channel_id=1, source_target_pairs={{0,8},{4,12},{8,0},{12,4},{16,24},{20,28},{24,16},{28,20},{1,9},{5... | collective-permute-start | bytes 122888 | tf_op jit(solution)/shard_map/ppermute | solution.py:449
  37.6 1.4 %collective-permute-done.25 = f32[40,256]{1,0:T(8,128)S(1)} collective-permute-done((f32[40,256]{1,0:T(8,128)S(1)}, f32[40,256]{1,0:T(8,128)S(1)}, u32[]{:S(2)}, u32[]{:S(2)}) %collective-permute-start.25) | collective-permute-done | bytes 40992 | tf_op jit(solution)/shard_map/ppermute | solution.py:449
  39.0 0.5 %collective-permute-done.26 = f32[40,256]{1,0:T(8,128)S(1)} collective-permute-done((f32[40,256]{1,0:T(8,128)S(1)}, f32[40,256]{1,0:T(8,128)S(1)}, u32[]{:S(2)}, u32[]{:S(2)}) %collective-permute-start.26) | collective-permute-done | bytes 40992 | tf_op jit(solution)/shard_map/ppermute | solution.py:449
  39.6 0.5 collective-permute-done.27
  40.0 3.7 %collective-permute-start.28 = (f32[32,256]{1,0:T(8,128)S(1)}, f32[32,256]{1,0:T(8,128)S(1)}, u32[]{:S(2)}, u32[]{:S(2)}) collective-permute-start(f32[32,256]{1,0:T(8,128)S(1)} %slice.55), channel_id=1, source_target_pairs={{0,3},{1,2},{2,1},{3,0},{4,7},{5,6},{6,5},{7,4},{8,11},{9,10},{10,... | collective-permute-start | bytes 98312 | tf_op jit(solution)/shard_map/ppermute | solution.py:513
  43.7 0.0 collective-permute-start.29
  43.7 0.8 %collective-permute-start.30 = (f32[32,256]{1,0:T(8,128)S(1)}, f32[32,256]{1,0:T(8,128)S(1)}, u32[]{:S(2)}, u32[]{:S(2)}) collective-permute-start(f32[32,256]{1,0:T(8,128)S(1)} %slice.55), channel_id=1, source_target_pairs={{0,1},{1,0},{2,3},{3,2},{4,5},{5,4},{6,7},{7,6},{8,9},{9,8},{10,11... | collective-permute-start | bytes 98312 | tf_op jit(solution)/shard_map/ppermute | solution.py:513
  44.5 0.1 convert_reduce_fusion
  44.6 0.6 %reduce_max.9 = s32[]{:T(128)} reduce(s32[4]{0:T(128)S(1)} %convert_reduce_fusion, s32[]{:T(128)} %constant.118.clone.1), dimensions={0}, to_apply=%region_1.2 | reduce | flops 3 | bytes 24 | tf_op jit(solution)/shard_map/reduce_max | solution.py:543
  45.9 0.0 collective-permute-done.28
  45.9 2.6 %collective-permute-done.29 = f32[32,256]{1,0:T(8,128)S(1)} collective-permute-done((f32[32,256]{1,0:T(8,128)S(1)}, f32[32,256]{1,0:T(8,128)S(1)}, u32[]{:S(2)}, u32[]{:S(2)}) %collective-permute-start.29) | collective-permute-done | bytes 32800 | tf_op jit(solution)/shard_map/ppermute | solution.py:513
  48.5 0.0 collective-permute-done.30
  48.5 0.2 conditional.1
  48.6 0.1 sqrt_bitcast_fusion
  48.6 0.1 add_divide_fusion.1
  48.7 0.0 copy-start.2
  48.7 0.6 %copy-done.2 = f32[32,256]{1,0:T(8,128)} copy-done((f32[32,256]{1,0:T(8,128)}, f32[32,256]{1,0:T(8,128)S(1)}, u32[]{:S(2)}) %copy-start.2) | copy-done | bytes 32792
  (10 shorter events, 0.1 us)
Async XLA Ops:
  0.0 18.8 %copy-start.1 = (s32[2,32,128]{2,1,0:T(8,128)S(1)}, s32[2,32,128]{2,1,0:T(8,128)}, u32[]{:S(2)}) copy-start(s32[2,32,128]{2,1,0:T(8,128)} %param.8) | copy-start | bytes 98308
  0.0 18.8 %copy-start.4 = (s32[256]{0:T(256)S(1)}, s32[256]{0:T(256)}, u32[]{:S(2)}) copy-start(s32[256]{0:T(256)} %param.9) | copy-start | bytes 3076
  4.5 1.9 %collective-permute-start.15 = (bf16[6,128,256]{2,1,0:T(8,128)(2,1)S(1)}, bf16[6,128,256]{2,1,0:T(8,128)(2,1)S(1)}, u32[]{:S(2)}, u32[]{:S(2)}) collective-permute-start(bf16[6,128,256]{2,1,0:T(8,128)(2,1)S(1)} %get-tuple-element.112), channel_id=1, source_target_pairs={{0,4},{4,0},{8,12},{12,8},{16,20},{20,16},{24,28},{28,24},{1,5},{5... | collective-permute-start | bytes 1179656 | tf_op jit(solution)/shard_map/ppermute | solution.py:449
  5.0 1.6 %collective-permute-start.16 = (s32[64,128]{1,0:T(8,128)}, s32[64,128]{1,0:T(8,128)S(1)}, u32[]{:S(2)}, u32[]{:S(2)}) collective-permute-start(s32[64,128]{1,0:T(8,128)} %bitcast.31), channel_id=1, source_target_pairs={{0,4},{4,0},{8,12},{12,8},{16,20},{20,16},{24,28},{28,24},{1,5},{5... | collective-permute-start | bytes 98312 | tf_op jit(solution)/shard_map/ppermute | solution.py:449
  6.4 17.1 %copy-start.3 = (s32[2,32]{1,0:T(2,128)S(1)}, s32[2,32]{1,0:T(2,128)}, u32[]{:S(2)}) copy-start(s32[2,32]{1,0:T(2,128)} %src_ref.3) | copy-start | bytes 772
  6.6 12.3 %collective-permute-start.17 = (bf16[2,30,256,128]{3,2,1,0:T(8,128)(2,1)}, bf16[2,30,256,128]{3,2,1,0:T(8,128)(2,1)S(1)}, u32[]{:S(2)}, u32[]{:S(2)}) collective-permute-start(bf16[2,30,256,128]{3,2,1,0:T(8,128)(2,1)} %spec_ref.3), channel_id=1, source_target_pairs={{0,4},{4,0},{8,12},{12,8},{16,20},{20,16},{24,28},{28,24},{1,5},{5... | collective-permute-start | bytes 11796488 | tf_op jit(solution)/shard_map/ppermute | solution.py:449
  7.0 8.4 %collective-permute-start.18 = (bf16[6,64,256]{2,1,0:T(8,128)(2,1)S(1)}, bf16[6,64,256]{2,1,0:T(8,128)(2,1)S(1)}, u32[]{:S(2)}, u32[]{:S(2)}) collective-permute-start(bf16[6,64,256]{2,1,0:T(8,128)(2,1)S(1)} %get-tuple-element.120.refs_0_), channel_id=1, source_target_pairs={{0,8},{4,12},{8,0},{12,4},{16,24},{20,28},{24,16},{28,20},{1,9},{5... | collective-permute-start | bytes 589832 | tf_op jit(solution)/shard_map/ppermute | solution.py:449
  9.6 7.8 %collective-permute-start.21 = (bf16[6,64,256]{2,1,0:T(8,128)(2,1)S(1)}, bf16[6,64,256]{2,1,0:T(8,128)(2,1)S(1)}, u32[]{:S(2)}, u32[]{:S(2)}) collective-permute-start(bf16[6,64,256]{2,1,0:T(8,128)(2,1)S(1)} %get-tuple-element.123.refs_3_), channel_id=1, source_target_pairs={{0,16},{4,20},{8,24},{12,28},{16,0},{20,4},{24,8},{28,12},{1,17},{... | collective-permute-start | bytes 589832 | tf_op jit(solution)/shard_map/ppermute | solution.py:449
  11.1 12.3 %collective-permute-start.19 = (bf16[6,64,256]{2,1,0:T(8,128)(2,1)S(1)}, bf16[6,64,256]{2,1,0:T(8,128)(2,1)S(1)}, u32[]{:S(2)}, u32[]{:S(2)}) collective-permute-start(bf16[6,64,256]{2,1,0:T(8,128)(2,1)S(1)} %get-tuple-element.120.refs_0_), channel_id=1, source_target_pairs={{0,16},{4,20},{8,24},{12,28},{16,0},{20,4},{24,8},{28,12},{1,17},{... | collective-permute-start | bytes 589832 | tf_op jit(solution)/shard_map/ppermute | solution.py:449
  11.6 11.8 %collective-permute-start.20 = (bf16[6,64,256]{2,1,0:T(8,128)(2,1)S(1)}, bf16[6,64,256]{2,1,0:T(8,128)(2,1)S(1)}, u32[]{:S(2)}, u32[]{:S(2)}) collective-permute-start(bf16[6,64,256]{2,1,0:T(8,128)(2,1)S(1)} %get-tuple-element.123.refs_3_), channel_id=1, source_target_pairs={{0,8},{4,12},{8,0},{12,4},{16,24},{20,28},{24,16},{28,20},{1,9},{5... | collective-permute-start | bytes 589832 | tf_op jit(solution)/shard_map/ppermute | solution.py:449
  15.3 9.6 %collective-permute-start.22 = (bf16[6,64,256]{2,1,0:T(8,128)(2,1)S(1)}, bf16[6,64,256]{2,1,0:T(8,128)(2,1)S(1)}, u32[]{:S(2)}, u32[]{:S(2)}) collective-permute-start(bf16[6,64,256]{2,1,0:T(8,128)(2,1)S(1)} %collective-permute-done.18.refs_1_), channel_id=1, source_target_pairs={{0,16},{4,20},{8,24},{12,28},{16,0},{20,4},{24,8},{28,12},{1,17},{... | collective-permute-start | bytes 589832 | tf_op jit(solution)/shard_map/ppermute | solution.py:449
  17.3 7.6 %collective-permute-start.23 = (bf16[6,64,256]{2,1,0:T(8,128)(2,1)S(1)}, bf16[6,64,256]{2,1,0:T(8,128)(2,1)S(1)}, u32[]{:S(2)}, u32[]{:S(2)}) collective-permute-start(bf16[6,64,256]{2,1,0:T(8,128)(2,1)S(1)} %collective-permute-done.21.refs_5_), channel_id=1, source_target_pairs={{0,8},{4,12},{8,0},{12,4},{16,24},{20,28},{24,16},{28,20},{1,9},{5... | collective-permute-start | bytes 589832 | tf_op jit(solution)/shard_map/ppermute | solution.py:449
  32.5 1.5 %collective-permute-start.24 = (f32[4,40,256]{2,1,0:T(8,128)S(1)}, f32[4,40,256]{2,1,0:T(8,128)S(1)}, u32[]{:S(2)}, u32[]{:S(2)}) collective-permute-start(f32[4,40,256]{2,1,0:T(8,128)S(1)} %get-tuple-element.135), channel_id=1, source_target_pairs={{0,4},{4,0},{8,12},{12,8},{16,20},{20,16},{24,28},{28,24},{1,5},{5... | collective-permute-start | bytes 491528 | tf_op jit(solution)/shard_map/ppermute | solution.py:449
  34.0 5.0 %collective-permute-start.25 = (f32[40,256]{1,0:T(8,128)S(1)}, f32[40,256]{1,0:T(8,128)S(1)}, u32[]{:S(2)}, u32[]{:S(2)}) collective-permute-start(f32[40,256]{1,0:T(8,128)S(1)} %get-tuple-element.144), channel_id=1, source_target_pairs={{0,24},{4,28},{8,16},{12,20},{16,8},{20,12},{24,0},{28,4},{1,25},{... | collective-permute-start | bytes 122888 | tf_op jit(solution)/shard_map/ppermute | solution.py:449
  35.5 4.0 %collective-permute-start.26 = (f32[40,256]{1,0:T(8,128)S(1)}, f32[40,256]{1,0:T(8,128)S(1)}, u32[]{:S(2)}, u32[]{:S(2)}) collective-permute-start(f32[40,256]{1,0:T(8,128)S(1)} %get-tuple-element.146), channel_id=1, source_target_pairs={{0,16},{4,20},{8,24},{12,28},{16,0},{20,4},{24,8},{28,12},{1,17},{... | collective-permute-start | bytes 122888 | tf_op jit(solution)/shard_map/ppermute | solution.py:449
  36.0 4.0 %collective-permute-start.27 = (f32[40,256]{1,0:T(8,128)S(1)}, f32[40,256]{1,0:T(8,128)S(1)}, u32[]{:S(2)}, u32[]{:S(2)}) collective-permute-start(f32[40,256]{1,0:T(8,128)S(1)} %get-tuple-element.145), channel_id=1, source_target_pairs={{0,8},{4,12},{8,0},{12,4},{16,24},{20,28},{24,16},{28,20},{1,9},{5... | collective-permute-start | bytes 122888 | tf_op jit(solution)/shard_map/ppermute | solution.py:449
  40.0 5.9 %collective-permute-start.28 = (f32[32,256]{1,0:T(8,128)S(1)}, f32[32,256]{1,0:T(8,128)S(1)}, u32[]{:S(2)}, u32[]{:S(2)}) collective-permute-start(f32[32,256]{1,0:T(8,128)S(1)} %slice.55), channel_id=1, source_target_pairs={{0,3},{1,2},{2,1},{3,0},{4,7},{5,6},{6,5},{7,4},{8,11},{9,10},{10,... | collective-permute-start | bytes 98312 | tf_op jit(solution)/shard_map/ppermute | solution.py:513
  43.7 4.8 %collective-permute-start.29 = (f32[32,256]{1,0:T(8,128)S(1)}, f32[32,256]{1,0:T(8,128)S(1)}, u32[]{:S(2)}, u32[]{:S(2)}) collective-permute-start(f32[32,256]{1,0:T(8,128)S(1)} %slice.55), channel_id=1, source_target_pairs={{0,2},{1,3},{2,0},{3,1},{4,6},{5,7},{6,4},{7,5},{8,10},{9,11},{10,... | collective-permute-start | bytes 98312 | tf_op jit(solution)/shard_map/ppermute | solution.py:513
  43.7 4.8 %collective-permute-start.30 = (f32[32,256]{1,0:T(8,128)S(1)}, f32[32,256]{1,0:T(8,128)S(1)}, u32[]{:S(2)}, u32[]{:S(2)}) collective-permute-start(f32[32,256]{1,0:T(8,128)S(1)} %slice.55), channel_id=1, source_target_pairs={{0,1},{1,0},{2,3},{3,2},{4,5},{5,4},{6,7},{7,6},{8,9},{9,8},{10,11... | collective-permute-start | bytes 98312 | tf_op jit(solution)/shard_map/ppermute | solution.py:513
  48.7 0.6 %copy-start.2 = (f32[32,256]{1,0:T(8,128)}, f32[32,256]{1,0:T(8,128)S(1)}, u32[]{:S(2)}) copy-start(f32[32,256]{1,0:T(8,128)S(1)} %get-tuple-element.210) | copy-start | bytes 98308

commit v8 on v7

--- a/solution.py
+++ b/solution.py
@@ -120,7 +120,7 @@
     mine = pl.multiple_of(core * half, half)
     other = pl.multiple_of((1 - core) * half, half)
     outs = []
-    turn = 2 if groups % 2 == 0 else 1
+    turn = 3 if groups % 3 == 0 else 1
     for b0 in range(0, groups, turn):
         lefts = []
         for b in range(b0, b0 + turn):

time: 49.5 us -> 49.5 us (level)
  no operation moved by 1% of the time
where the time goes in v8:
time: 49.5 us; the launch traced here: 49.3 us
  Pallas kernels  17.9 us (36%)
  starting transfers between devices  17.3 us (35%)
  waiting for transfers between devices  11.1 us (22%)
  other arithmetic  1.6 us (3%)
  between operations  0.83 us (2%)
  local copies, waits for them, and re-layouts  0.66 us (1%)
    ppermute x13, starting transfers between devices, swap(): return lax.ppermute(x, 'chan', [(i, i ^ bit) for i in range(size)])  12.8 us
    ppermute x13, waiting for transfers between devices, swap(): return lax.ppermute(x, 'chan', [(i, i ^ bit) for i in range(size)])  8.4 us
    pallas_call x1, Pallas kernels, cross_and_bin(): pl.pallas_call(functools.partial(cross_kernel, len(arrays), len(hots)), i...  7.57 us
    pallas_call x1, Pallas kernels, tables(): pl.pallas_call(functools.partial(tables_kernel, nchan), in_specs=[ANY, AN...  4.57 us
    ppermute x3, starting transfers between devices, finish(): lax.ppermute(owned, 'freq', [(i, i ^ k) for i in range(nfreq)])  4.45 us
    pallas_call x1, Pallas kernels, pick(): pl.pallas_call(functools.partial(pick_kernel, cap), in_specs=[VMEM, ANY],...  4.36 us
    ppermute x3, waiting for transfers between devices, finish(): lax.ppermute(owned, 'freq', [(i, i ^ k) for i in range(nfreq)])  2.67 us
    pallas_call x1, Pallas kernels, place_early(): pl.pallas_call(functools.partial(early_kernel, cap, names, late, per_chip...  1.36 us
  transfers between devices with their start and end apart: 16, of which 9 were waited for; matrix products, arithmetic and copies ran while one was open for 3% of the time, Pallas kernels for 12%

profile of v8, /device:TPU:0, one launch (start us, length us, event | category | flops | bytes accessed | tf_op | source)
XLA Modules:
  0.0 49.3 jit_solution(10617807282496590921)
XLA Ops:
  0.0 0.0 copy-start.1
  0.0 0.0 copy-start.4
  0.0 4.4 %pick_sources.3 = (bf16[6,128,256]{2,1,0:T(8,128)(2,1)S(1)}, bf16[6,128,256]{2,1,0:T(8,128)(2,1)S(1)}) custom-call(s32[2,32]{1,0:T(2,128)} %src_ref.3, bf16[2,30,256,128]{3,2,1,0:T(8,128)(2,1)} %spec_ref.3), custom_call_target="tpu_custom_call" | custom-call | tf_op jit(solution)/shard_map/pick_sources/pallas_call | solution.py:153
  4.4 0.5 %collective-permute-start.15 = (bf16[6,128,256]{2,1,0:T(8,128)(2,1)S(1)}, bf16[6,128,256]{2,1,0:T(8,128)(2,1)S(1)}, u32[]{:S(2)}, u32[]{:S(2)}) collective-permute-start(bf16[6,128,256]{2,1,0:T(8,128)(2,1)S(1)} %get-tuple-element.112), channel_id=1, source_target_pairs={{0,4},{4,0},{8,12},{12,8},{16,20},{20,16},{24,28},{28,24},{1,5},{5... | collective-permute-start | bytes 1179656 | tf_op jit(solution)/shard_map/ppermute | solution.py:449
  4.9 0.1 collective-permute-start.16
  5.0 0.6 %negate_multiply_fusion = (f32[128,256]{1,0:T(8,128)S(1)}, f32[128,256]{1,0:T(8,128)S(1)}) fusion(s32[256]{0:T(256)S(1)} %iota_add_fusion, s32[128]{0:T(128)S(1)} %iota_add_fusion.1), kind=kLoop, calls=%fused_computation.25 | loop fusion | flops 557056 | bytes 263680 | tf_op jit(solution)/shard_map/mul | solution.py:40
  5.6 0.7 %collective-permute-done.15 = bf16[6,128,256]{2,1,0:T(8,128)(2,1)S(1)} collective-permute-done((bf16[6,128,256]{2,1,0:T(8,128)(2,1)S(1)}, bf16[6,128,256]{2,1,0:T(8,128)(2,1)S(1)}, u32[]{:S(2)}, u32[]{:S(2)}) %collective-permute-start.15) | collective-permute-done | bytes 393248 | tf_op jit(solution)/shard_map/ppermute | solution.py:449
  6.3 0.0 copy-start.3
  6.3 0.2 collective-permute-done.16.got_pairs
  6.5 0.4 collective-permute-start.17
  6.9 2.6 %collective-permute-start.18 = (bf16[6,64,256]{2,1,0:T(8,128)(2,1)S(1)}, bf16[6,64,256]{2,1,0:T(8,128)(2,1)S(1)}, u32[]{:S(2)}, u32[]{:S(2)}) collective-permute-start(bf16[6,64,256]{2,1,0:T(8,128)(2,1)S(1)} %get-tuple-element.120.refs_0_), channel_id=1, source_target_pairs={{0,8},{4,12},{8,0},{12,4},{16,24},{20,28},{24,16},{28,20},{1,9},{5... | collective-permute-start | bytes 589832 | tf_op jit(solution)/shard_map/ppermute | solution.py:449
  9.5 1.5 %collective-permute-start.21 = (bf16[6,64,256]{2,1,0:T(8,128)(2,1)S(1)}, bf16[6,64,256]{2,1,0:T(8,128)(2,1)S(1)}, u32[]{:S(2)}, u32[]{:S(2)}) collective-permute-start(bf16[6,64,256]{2,1,0:T(8,128)(2,1)S(1)} %get-tuple-element.123.refs_3_), channel_id=1, source_target_pairs={{0,16},{4,20},{8,24},{12,28},{16,0},{20,4},{24,8},{28,12},{1,17},{... | collective-permute-start | bytes 589832 | tf_op jit(solution)/shard_map/ppermute | solution.py:449
  11.0 0.5 %collective-permute-start.19 = (bf16[6,64,256]{2,1,0:T(8,128)(2,1)S(1)}, bf16[6,64,256]{2,1,0:T(8,128)(2,1)S(1)}, u32[]{:S(2)}, u32[]{:S(2)}) collective-permute-start(bf16[6,64,256]{2,1,0:T(8,128)(2,1)S(1)} %get-tuple-element.120.refs_0_), channel_id=1, source_target_pairs={{0,16},{4,20},{8,24},{12,28},{16,0},{20,4},{24,8},{28,12},{1,17},{... | collective-permute-start | bytes 589832 | tf_op jit(solution)/shard_map/ppermute | solution.py:449
  11.5 0.1 collective-permute-start.20
  11.6 3.6 %collective-permute-done.18.refs_1_ = bf16[6,64,256]{2,1,0:T(8,128)(2,1)S(1)} collective-permute-done((bf16[6,64,256]{2,1,0:T(8,128)(2,1)S(1)}, bf16[6,64,256]{2,1,0:T(8,128)(2,1)S(1)}, u32[]{:S(2)}, u32[]{:S(2)}) %collective-permute-start.18) | collective-permute-done | bytes 196640 | tf_op jit(solution)/shard_map/ppermute | solution.py:449
  15.2 2.0 %collective-permute-start.22 = (bf16[6,64,256]{2,1,0:T(8,128)(2,1)S(1)}, bf16[6,64,256]{2,1,0:T(8,128)(2,1)S(1)}, u32[]{:S(2)}, u32[]{:S(2)}) collective-permute-start(bf16[6,64,256]{2,1,0:T(8,128)(2,1)S(1)} %collective-permute-done.18.refs_1_), channel_id=1, source_target_pairs={{0,16},{4,20},{8,24},{12,28},{16,0},{20,4},{24,8},{28,12},{1,17},{... | collective-permute-start | bytes 589832 | tf_op jit(solution)/shard_map/ppermute | solution.py:449
  17.3 0.0 collective-permute-done.21.refs_5_
  17.3 1.5 %collective-permute-start.23 = (bf16[6,64,256]{2,1,0:T(8,128)(2,1)S(1)}, bf16[6,64,256]{2,1,0:T(8,128)(2,1)S(1)}, u32[]{:S(2)}, u32[]{:S(2)}) collective-permute-start(bf16[6,64,256]{2,1,0:T(8,128)(2,1)S(1)} %collective-permute-done.21.refs_5_), channel_id=1, source_target_pairs={{0,8},{4,12},{8,0},{12,4},{16,24},{20,28},{24,16},{28,20},{1,9},{5... | collective-permute-start | bytes 589832 | tf_op jit(solution)/shard_map/ppermute | solution.py:449
  18.8 0.0 collective-permute-done.17.got_ref
  18.8 0.0 copy-done.1
  18.8 0.0 copy-done.4
  18.8 4.6 %tables.3 = (bf16[128,64,256]{2,1,0:T(8,128)(2,1)S(1)}, bf16[64,256,256]{2,1,0:T(8,128)(2,1)S(1)}, f8e4m3fn[64,256,256]{2,1,0:T(32,128)(4,1)S(1)}, f32[8,256]{1,0:T(8,128)S(1)}, bf16[16,256]{1,0:T(8,128)(2,1)S(1)}) custom-call(bf16[2,30,256,128]{3,2,1,0:T(8,128)(2,1)} %spec_ref.3, bf16[2,30,256,128]{3,2,1,0:T(8,128)(2,1)S(1)} %collective-permute-done.17.got_ref, ...), custom_call_target="tpu_custom_call" | custom-call | tf_op jit(solution)/shard_map/tables/pallas_call | solution.py:279
  23.3 0.0 collective-permute-done.19.refs_2_
  23.4 0.0 collective-permute-done.20.refs_4_
  23.4 0.0 copy-done.3
  23.4 1.4 %place_early.3 = (f32[4264,128]{1,0:T(8,128)S(1)}, bf16[256,640]{1,0:T(8,128)(2,1)S(1)}, bf16[16,256]{1,0:T(8,128)(2,1)S(1)}) custom-call(s32[2,32]{1,0:T(2,128)S(1)} %copy-done.3, bf16[6,64,256]{2,1,0:T(8,128)(2,1)S(1)} %get-tuple-element.120.refs_0_, bf16[6,64,256]{2,1,0:T(8,128)(2,1)S(1)} %collective-permute-done.18.refs_1_, ...), custom_call_target="tpu_custom_call" | custom-call | tf_op jit(solution)/shard_map/place_early/pallas_call | solution.py:313
  24.8 0.1 collective-permute-done.22.refs_8_
  24.8 0.0 collective-permute-done.23.refs_9_
  24.8 7.6 %cross_and_bin.3 = (f32[4,40,256]{2,1,0:T(8,128)S(1)}, f32[4,40,256]{2,1,0:T(8,128)S(1)}) custom-call(bf16[256,640]{1,0:T(8,128)(2,1)S(1)} %get-tuple-element.126.refs_0_, bf16[128,64,256]{2,1,0:T(8,128)(2,1)S(1)} %get-tuple-element.127.refs_1_, f32[128,256]{1,0:T(8,128)S(1)} %get-tuple-element.114.refs_2_, f32[128,256]{1,0:T(8,128)S(1)} %get-tuple-element.115.refs_3_, ...), custom_call_target="tpu_custom_call" | custom-call | tf_op jit(solution)/shard_map/cross_and_bin/pallas_call | solution.py:437
  32.4 0.1 collective-permute-start.24
  32.5 1.4 %collective-permute-done.24 = f32[4,40,256]{2,1,0:T(8,128)S(1)} collective-permute-done((f32[4,40,256]{2,1,0:T(8,128)S(1)}, f32[4,40,256]{2,1,0:T(8,128)S(1)}, u32[]{:S(2)}, u32[]{:S(2)}) %collective-permute-start.24) | collective-permute-done | bytes 163872 | tf_op jit(solution)/shard_map/ppermute | solution.py:449
  33.9 1.6 %collective-permute-start.25 = (f32[40,256]{1,0:T(8,128)S(1)}, f32[40,256]{1,0:T(8,128)S(1)}, u32[]{:S(2)}, u32[]{:S(2)}) collective-permute-start(f32[40,256]{1,0:T(8,128)S(1)} %get-tuple-element.144), channel_id=1, source_target_pairs={{0,24},{4,28},{8,16},{12,20},{16,8},{20,12},{24,0},{28,4},{1,25},{... | collective-permute-start | bytes 122888 | tf_op jit(solution)/shard_map/ppermute | solution.py:449
  35.5 0.5 collective-permute-start.26
  35.9 1.5 %collective-permute-start.27 = (f32[40,256]{1,0:T(8,128)S(1)}, f32[40,256]{1,0:T(8,128)S(1)}, u32[]{:S(2)}, u32[]{:S(2)}) collective-permute-start(f32[40,256]{1,0:T(8,128)S(1)} %get-tuple-element.145), channel_id=1, source_target_pairs={{0,8},{4,12},{8,0},{12,4},{16,24},{20,28},{24,16},{28,20},{1,9},{5... | collective-permute-start | bytes 122888 | tf_op jit(solution)/shard_map/ppermute | solution.py:449
  37.5 1.4 %collective-permute-done.25 = f32[40,256]{1,0:T(8,128)S(1)} collective-permute-done((f32[40,256]{1,0:T(8,128)S(1)}, f32[40,256]{1,0:T(8,128)S(1)}, u32[]{:S(2)}, u32[]{:S(2)}) %collective-permute-start.25) | collective-permute-done | bytes 40992 | tf_op jit(solution)/shard_map/ppermute | solution.py:449
  38.9 0.5 %collective-permute-done.26 = f32[40,256]{1,0:T(8,128)S(1)} collective-permute-done((f32[40,256]{1,0:T(8,128)S(1)}, f32[40,256]{1,0:T(8,128)S(1)}, u32[]{:S(2)}, u32[]{:S(2)}) %collective-permute-start.26) | collective-permute-done | bytes 40992 | tf_op jit(solution)/shard_map/ppermute | solution.py:449
  39.5 0.5 collective-permute-done.27
  40.0 3.7 %collective-permute-start.28 = (f32[32,256]{1,0:T(8,128)S(1)}, f32[32,256]{1,0:T(8,128)S(1)}, u32[]{:S(2)}, u32[]{:S(2)}) collective-permute-start(f32[32,256]{1,0:T(8,128)S(1)} %slice.55), channel_id=1, source_target_pairs={{0,3},{1,2},{2,1},{3,0},{4,7},{5,6},{6,5},{7,4},{8,11},{9,10},{10,... | collective-permute-start | bytes 98312 | tf_op jit(solution)/shard_map/ppermute | solution.py:513
  43.7 0.0 collective-permute-start.29
  43.7 0.7 %collective-permute-start.30 = (f32[32,256]{1,0:T(8,128)S(1)}, f32[32,256]{1,0:T(8,128)S(1)}, u32[]{:S(2)}, u32[]{:S(2)}) collective-permute-start(f32[32,256]{1,0:T(8,128)S(1)} %slice.55), channel_id=1, source_target_pairs={{0,1},{1,0},{2,3},{3,2},{4,5},{5,4},{6,7},{7,6},{8,9},{9,8},{10,11... | collective-permute-start | bytes 98312 | tf_op jit(solution)/shard_map/ppermute | solution.py:513
  44.4 0.1 convert_reduce_fusion
  44.5 0.6 %reduce_max.9 = s32[]{:T(128)} reduce(s32[4]{0:T(128)S(1)} %convert_reduce_fusion, s32[]{:T(128)} %constant.118.clone.1), dimensions={0}, to_apply=%region_1.2 | reduce | flops 3 | bytes 24 | tf_op jit(solution)/shard_map/reduce_max | solution.py:543
  45.8 0.0 collective-permute-done.28
  45.8 2.7 %collective-permute-done.29 = f32[32,256]{1,0:T(8,128)S(1)} collective-permute-done((f32[32,256]{1,0:T(8,128)S(1)}, f32[32,256]{1,0:T(8,128)S(1)}, u32[]{:S(2)}, u32[]{:S(2)}) %collective-permute-start.29) | collective-permute-done | bytes 32800 | tf_op jit(solution)/shard_map/ppermute | solution.py:513
  48.5 0.0 collective-permute-done.30
  48.5 0.2 conditional.1
  48.5 0.1 sqrt_bitcast_fusion
  48.6 0.1 add_divide_fusion.1
  48.7 0.0 copy-start.2
  48.7 0.6 %copy-done.2 = f32[32,256]{1,0:T(8,128)} copy-done((f32[32,256]{1,0:T(8,128)}, f32[32,256]{1,0:T(8,128)S(1)}, u32[]{:S(2)}) %copy-start.2) | copy-done | bytes 32792
  (10 shorter events, 0.1 us)
Async XLA Ops:
  0.0 18.8 %copy-start.1 = (s32[2,32,128]{2,1,0:T(8,128)S(1)}, s32[2,32,128]{2,1,0:T(8,128)}, u32[]{:S(2)}) copy-start(s32[2,32,128]{2,1,0:T(8,128)} %param.8) | copy-start | bytes 98308
  0.0 18.8 %copy-start.4 = (s32[256]{0:T(256)S(1)}, s32[256]{0:T(256)}, u32[]{:S(2)}) copy-start(s32[256]{0:T(256)} %param.9) | copy-start | bytes 3076
  4.4 1.9 %collective-permute-start.15 = (bf16[6,128,256]{2,1,0:T(8,128)(2,1)S(1)}, bf16[6,128,256]{2,1,0:T(8,128)(2,1)S(1)}, u32[]{:S(2)}, u32[]{:S(2)}) collective-permute-start(bf16[6,128,256]{2,1,0:T(8,128)(2,1)S(1)} %get-tuple-element.112), channel_id=1, source_target_pairs={{0,4},{4,0},{8,12},{12,8},{16,20},{20,16},{24,28},{28,24},{1,5},{5... | collective-permute-start | bytes 1179656 | tf_op jit(solution)/shard_map/ppermute | solution.py:449
  4.9 1.6 %collective-permute-start.16 = (s32[64,128]{1,0:T(8,128)}, s32[64,128]{1,0:T(8,128)S(1)}, u32[]{:S(2)}, u32[]{:S(2)}) collective-permute-start(s32[64,128]{1,0:T(8,128)} %bitcast.31), channel_id=1, source_target_pairs={{0,4},{4,0},{8,12},{12,8},{16,20},{20,16},{24,28},{28,24},{1,5},{5... | collective-permute-start | bytes 98312 | tf_op jit(solution)/shard_map/ppermute | solution.py:449
  6.3 17.1 %copy-start.3 = (s32[2,32]{1,0:T(2,128)S(1)}, s32[2,32]{1,0:T(2,128)}, u32[]{:S(2)}) copy-start(s32[2,32]{1,0:T(2,128)} %src_ref.3) | copy-start | bytes 772
  6.5 12.3 %collective-permute-start.17 = (bf16[2,30,256,128]{3,2,1,0:T(8,128)(2,1)}, bf16[2,30,256,128]{3,2,1,0:T(8,128)(2,1)S(1)}, u32[]{:S(2)}, u32[]{:S(2)}) collective-permute-start(bf16[2,30,256,128]{3,2,1,0:T(8,128)(2,1)} %spec_ref.3), channel_id=1, source_target_pairs={{0,4},{4,0},{8,12},{12,8},{16,20},{20,16},{24,28},{28,24},{1,5},{5... | collective-permute-start | bytes 11796488 | tf_op jit(solution)/shard_map/ppermute | solution.py:449
  6.9 8.4 %collective-permute-start.18 = (bf16[6,64,256]{2,1,0:T(8,128)(2,1)S(1)}, bf16[6,64,256]{2,1,0:T(8,128)(2,1)S(1)}, u32[]{:S(2)}, u32[]{:S(2)}) collective-permute-start(bf16[6,64,256]{2,1,0:T(8,128)(2,1)S(1)} %get-tuple-element.120.refs_0_), channel_id=1, source_target_pairs={{0,8},{4,12},{8,0},{12,4},{16,24},{20,28},{24,16},{28,20},{1,9},{5... | collective-permute-start | bytes 589832 | tf_op jit(solution)/shard_map/ppermute | solution.py:449
  9.5 7.8 %collective-permute-start.21 = (bf16[6,64,256]{2,1,0:T(8,128)(2,1)S(1)}, bf16[6,64,256]{2,1,0:T(8,128)(2,1)S(1)}, u32[]{:S(2)}, u32[]{:S(2)}) collective-permute-start(bf16[6,64,256]{2,1,0:T(8,128)(2,1)S(1)} %get-tuple-element.123.refs_3_), channel_id=1, source_target_pairs={{0,16},{4,20},{8,24},{12,28},{16,0},{20,4},{24,8},{28,12},{1,17},{... | collective-permute-start | bytes 589832 | tf_op jit(solution)/shard_map/ppermute | solution.py:449
  11.0 12.3 %collective-permute-start.19 = (bf16[6,64,256]{2,1,0:T(8,128)(2,1)S(1)}, bf16[6,64,256]{2,1,0:T(8,128)(2,1)S(1)}, u32[]{:S(2)}, u32[]{:S(2)}) collective-permute-start(bf16[6,64,256]{2,1,0:T(8,128)(2,1)S(1)} %get-tuple-element.120.refs_0_), channel_id=1, source_target_pairs={{0,16},{4,20},{8,24},{12,28},{16,0},{20,4},{24,8},{28,12},{1,17},{... | collective-permute-start | bytes 589832 | tf_op jit(solution)/shard_map/ppermute | solution.py:449
  11.5 11.8 %collective-permute-start.20 = (bf16[6,64,256]{2,1,0:T(8,128)(2,1)S(1)}, bf16[6,64,256]{2,1,0:T(8,128)(2,1)S(1)}, u32[]{:S(2)}, u32[]{:S(2)}) collective-permute-start(bf16[6,64,256]{2,1,0:T(8,128)(2,1)S(1)} %get-tuple-element.123.refs_3_), channel_id=1, source_target_pairs={{0,8},{4,12},{8,0},{12,4},{16,24},{20,28},{24,16},{28,20},{1,9},{5... | collective-permute-start | bytes 589832 | tf_op jit(solution)/shard_map/ppermute | solution.py:449
  15.2 9.6 %collective-permute-start.22 = (bf16[6,64,256]{2,1,0:T(8,128)(2,1)S(1)}, bf16[6,64,256]{2,1,0:T(8,128)(2,1)S(1)}, u32[]{:S(2)}, u32[]{:S(2)}) collective-permute-start(bf16[6,64,256]{2,1,0:T(8,128)(2,1)S(1)} %collective-permute-done.18.refs_1_), channel_id=1, source_target_pairs={{0,16},{4,20},{8,24},{12,28},{16,0},{20,4},{24,8},{28,12},{1,17},{... | collective-permute-start | bytes 589832 | tf_op jit(solution)/shard_map/ppermute | solution.py:449
  17.3 7.6 %collective-permute-start.23 = (bf16[6,64,256]{2,1,0:T(8,128)(2,1)S(1)}, bf16[6,64,256]{2,1,0:T(8,128)(2,1)S(1)}, u32[]{:S(2)}, u32[]{:S(2)}) collective-permute-start(bf16[6,64,256]{2,1,0:T(8,128)(2,1)S(1)} %collective-permute-done.21.refs_5_), channel_id=1, source_target_pairs={{0,8},{4,12},{8,0},{12,4},{16,24},{20,28},{24,16},{28,20},{1,9},{5... | collective-permute-start | bytes 589832 | tf_op jit(solution)/shard_map/ppermute | solution.py:449
  32.4 1.5 %collective-permute-start.24 = (f32[4,40,256]{2,1,0:T(8,128)S(1)}, f32[4,40,256]{2,1,0:T(8,128)S(1)}, u32[]{:S(2)}, u32[]{:S(2)}) collective-permute-start(f32[4,40,256]{2,1,0:T(8,128)S(1)} %get-tuple-element.135), channel_id=1, source_target_pairs={{0,4},{4,0},{8,12},{12,8},{16,20},{20,16},{24,28},{28,24},{1,5},{5... | collective-permute-start | bytes 491528 | tf_op jit(solution)/shard_map/ppermute | solution.py:449
  33.9 5.0 %collective-permute-start.25 = (f32[40,256]{1,0:T(8,128)S(1)}, f32[40,256]{1,0:T(8,128)S(1)}, u32[]{:S(2)}, u32[]{:S(2)}) collective-permute-start(f32[40,256]{1,0:T(8,128)S(1)} %get-tuple-element.144), channel_id=1, source_target_pairs={{0,24},{4,28},{8,16},{12,20},{16,8},{20,12},{24,0},{28,4},{1,25},{... | collective-permute-start | bytes 122888 | tf_op jit(solution)/shard_map/ppermute | solution.py:449
  35.5 4.0 %collective-permute-start.26 = (f32[40,256]{1,0:T(8,128)S(1)}, f32[40,256]{1,0:T(8,128)S(1)}, u32[]{:S(2)}, u32[]{:S(2)}) collective-permute-start(f32[40,256]{1,0:T(8,128)S(1)} %get-tuple-element.146), channel_id=1, source_target_pairs={{0,16},{4,20},{8,24},{12,28},{16,0},{20,4},{24,8},{28,12},{1,17},{... | collective-permute-start | bytes 122888 | tf_op jit(solution)/shard_map/ppermute | solution.py:449
  35.9 4.0 %collective-permute-start.27 = (f32[40,256]{1,0:T(8,128)S(1)}, f32[40,256]{1,0:T(8,128)S(1)}, u32[]{:S(2)}, u32[]{:S(2)}) collective-permute-start(f32[40,256]{1,0:T(8,128)S(1)} %get-tuple-element.145), channel_id=1, source_target_pairs={{0,8},{4,12},{8,0},{12,4},{16,24},{20,28},{24,16},{28,20},{1,9},{5... | collective-permute-start | bytes 122888 | tf_op jit(solution)/shard_map/ppermute | solution.py:449
  40.0 5.9 %collective-permute-start.28 = (f32[32,256]{1,0:T(8,128)S(1)}, f32[32,256]{1,0:T(8,128)S(1)}, u32[]{:S(2)}, u32[]{:S(2)}) collective-permute-start(f32[32,256]{1,0:T(8,128)S(1)} %slice.55), channel_id=1, source_target_pairs={{0,3},{1,2},{2,1},{3,0},{4,7},{5,6},{6,5},{7,4},{8,11},{9,10},{10,... | collective-permute-start | bytes 98312 | tf_op jit(solution)/shard_map/ppermute | solution.py:513
  43.7 4.8 %collective-permute-start.29 = (f32[32,256]{1,0:T(8,128)S(1)}, f32[32,256]{1,0:T(8,128)S(1)}, u32[]{:S(2)}, u32[]{:S(2)}) collective-permute-start(f32[32,256]{1,0:T(8,128)S(1)} %slice.55), channel_id=1, source_target_pairs={{0,2},{1,3},{2,0},{3,1},{4,6},{5,7},{6,4},{7,5},{8,10},{9,11},{10,... | collective-permute-start | bytes 98312 | tf_op jit(solution)/shard_map/ppermute | solution.py:513
  43.7 4.8 %collective-permute-start.30 = (f32[32,256]{1,0:T(8,128)S(1)}, f32[32,256]{1,0:T(8,128)S(1)}, u32[]{:S(2)}, u32[]{:S(2)}) collective-permute-start(f32[32,256]{1,0:T(8,128)S(1)} %slice.55), channel_id=1, source_target_pairs={{0,1},{1,0},{2,3},{3,2},{4,5},{5,4},{6,7},{7,6},{8,9},{9,8},{10,11... | collective-permute-start | bytes 98312 | tf_op jit(solution)/shard_map/ppermute | solution.py:513
  48.7 0.6 %copy-start.2 = (f32[32,256]{1,0:T(8,128)}, f32[32,256]{1,0:T(8,128)S(1)}, u32[]{:S(2)}) copy-start(f32[32,256]{1,0:T(8,128)S(1)} %get-tuple-element.210) | copy-start | bytes 98308
